TPU v7x, 32 devices: a whole 2x2x4 slice. The times are simulated.
32 devices in a mesh: ctx: 8 (over y, x, core), fsdp: 4 (over z).
Axes of the slice: x: 2, y: 2, z: 4, core: 2. Of those that a mesh axis runs over, the one named last changes fastest.
Arguments:
- layer_in: bfloat16 [4, 2048, 2048], P('fsdp', 'ctx'), may hold values from -6 to 6
- cotangent: bfloat16 [4, 2048, 2048], P('fsdp', 'ctx'), may hold values from -6 to 6
- block_map: int32 [4, 8], P('fsdp'), may hold values from 0 to 7, as said below
- attn_in: float32 [2048, 6144], P(('ctx', 'fsdp')), may hold values from -0.125 to 0.125
- attn_out: float32 [2048, 2048], P(('ctx', 'fsdp')), may hold values from -1 to 1
- ffn_in: float32 [2048, 11264], P(('ctx', 'fsdp')), may hold values from -0.125 to 0.125
- ffn_out: float32 [5632, 2048], P(('ctx', 'fsdp')), may hold values from -0.15625 to 0.15625
- vectors: float32 [2048, 7], P(('ctx', 'fsdp')), may hold values from -2.5 to 3.5
- first_attn_in: float32 [2048, 6144], P(('ctx', 'fsdp')), may hold values from -9.1552734e-05 to 9.1552734e-05
- first_attn_out: float32 [2048, 2048], P(('ctx', 'fsdp')), may hold values from -9.1552734e-05 to 9.1552734e-05
- first_ffn_in: float32 [2048, 11264], P(('ctx', 'fsdp')), may hold values from -9.1552734e-05 to 9.1552734e-05
- first_ffn_out: float32 [5632, 2048], P(('ctx', 'fsdp')), may hold values from -9.1552734e-05 to 9.1552734e-05
- first_vectors: float32 [2048, 7], P(('ctx', 'fsdp')), may hold values from -9.1552734e-05 to 9.1552734e-05
- second_attn_in: float32 [2048, 6144], P(('ctx', 'fsdp')), may hold values from 9.728656e-10 to 3.8914623e-09
- second_attn_out: float32 [2048, 2048], P(('ctx', 'fsdp')), may hold values from 9.728656e-10 to 3.8914623e-09
- second_ffn_in: float32 [2048, 11264], P(('ctx', 'fsdp')), may hold values from 9.728656e-10 to 3.8914623e-09
- second_ffn_out: float32 [5632, 2048], P(('ctx', 'fsdp')), may hold values from 9.728656e-10 to 3.8914623e-09
- second_vectors: float32 [2048, 7], P(('ctx', 'fsdp')), may hold values from 9.728656e-10 to 3.8914623e-09
Outputs:
- layer_out: bfloat16 [4, 2048, 2048], P('fsdp', 'ctx')
- input_grad: float32 [4, 2048, 2048], P('fsdp', 'ctx')
- grad_norm: float32 [], replicated
- new_attn_in: float32 [2048, 6144], P(('ctx', 'fsdp'))
- new_first_attn_in: float32 [2048, 6144], P(('ctx', 'fsdp'))
- new_second_attn_in: float32 [2048, 6144], P(('ctx', 'fsdp'))
- new_attn_out: float32 [2048, 2048], P(('ctx', 'fsdp'))
- new_first_attn_out: float32 [2048, 2048], P(('ctx', 'fsdp'))
- new_second_attn_out: float32 [2048, 2048], P(('ctx', 'fsdp'))
- new_ffn_in: float32 [2048, 11264], P(('ctx', 'fsdp'))
- new_first_ffn_in: float32 [2048, 11264], P(('ctx', 'fsdp'))
- new_second_ffn_in: float32 [2048, 11264], P(('ctx', 'fsdp'))
- new_ffn_out: float32 [5632, 2048], P(('ctx', 'fsdp'))
- new_first_ffn_out: float32 [5632, 2048], P(('ctx', 'fsdp'))
- new_second_ffn_out: float32 [5632, 2048], P(('ctx', 'fsdp'))
- new_vectors: float32 [2048, 7], P(('ctx', 'fsdp'))
- new_first_vectors: float32 [2048, 7], P(('ctx', 'fsdp'))
- new_second_vectors: float32 [2048, 7], P(('ctx', 'fsdp'))
Inputs may be any that keep to these rules, and one draw needn't show every extreme that they name: `block_map`: each group's row is a permutation of 0 to 7; codes under 1024 / 256 are prompt blocks, and the first and last block of every group hold prompt blocks.
All inputs are finite; a program needn't handle non-finite values.
Results may differ from a plain program's by a relative error of at most 0.017.
The roundings to bfloat16 on the way count: a program that leaves them out, or rounds other values in their place, can miss the bound.
Values may be sent and summed in bfloat16 or wider, within the bound.
No kernel may reach another device: no remote copies, remote signals or barrier semaphores. Data moves between devices by JAX's collectives and lax.ppermute only.
A program may use at most 640 MiB of HBM per device.

v0:
```python
import math

import jax
import jax.numpy as jnp
from jax import lax
from jax.sharding import PartitionSpec as P

D = 2048
HEADS = 32
HEAD_DIM = 64
FF = 5632
ROTARY = 16
CONT = 1024
BLOCK = 256
STEP = 10


NORM_EPS = 1e-05
BETA_ONE = 0.9
BETA_TWO = 0.95
ADAM_EPS = 1e-08
DECAY = 0.1
CLIP_LIMIT = 1.0
ROPE_BASE = 10000.0
MASKED = -1e30


def layout(codes, prompt):
    tokens = codes.shape[0] * BLOCK
    spread = jnp.repeat(codes, BLOCK, total_repeat_length=tokens)
    inner = jnp.arange(tokens, dtype=jnp.int32) % BLOCK
    prompt_blocks = prompt // BLOCK
    later = CONT // BLOCK
    offset = spread - prompt_blocks
    is_prompt = spread < prompt_blocks
    segments = jnp.where(is_prompt, 0, offset // later + 1)
    positions = jnp.where(
        is_prompt, spread * BLOCK + inner, prompt + offset % later * BLOCK + inner
    )
    return (segments, positions)


def standardize(values):
    center = values - jnp.mean(values, axis=-1, keepdims=True)
    scaled = lax.rsqrt(jnp.mean(center * center, axis=-1, keepdims=True) + NORM_EPS)
    return (center * scaled, scaled)


def norm_back(grad_normed, normed, scaled):
    return scaled * (
        grad_normed
        - jnp.mean(grad_normed, axis=-1, keepdims=True)
        - normed * jnp.mean(grad_normed * normed, axis=-1, keepdims=True)
    )


def angles(positions):
    half = ROTARY // 2
    freq = jnp.power(ROPE_BASE, -2.0 * jnp.arange(half, dtype=jnp.float32) / ROTARY)
    turn = positions.astype(jnp.float32)[:, None] * freq[None, :]
    return (jnp.cos(turn), jnp.sin(turn))


def rotate(field, cosine, sine, sign):
    half = cosine.shape[1]
    cosine = cosine[:, None, :]
    sine = sign * sine[:, None, :]
    first = field[..., :half]
    second = field[..., half : 2 * half]
    return jnp.concatenate(
        [first * cosine - second * sine, second * cosine + first * sine, field[..., 2 * half :]],
        axis=-1,
    )


def adam(weight, grad, first, second, rate):
    first = BETA_ONE * first + (1.0 - BETA_ONE) * grad
    second = BETA_TWO * second + (1.0 - BETA_TWO) * grad * grad
    fixed_first = first / (1.0 - BETA_ONE**STEP)
    fixed_second = second / (1.0 - BETA_TWO**STEP)
    weight = weight - rate * (fixed_first / (jnp.sqrt(fixed_second) + ADAM_EPS) + DECAY * weight)
    return (weight, first, second)


def local(
    layer_in,
    cotangent,
    block_map,
    attn_in,
    attn_out,
    ffn_in,
    ffn_out,
    vectors,
    first_attn_in,
    first_attn_out,
    first_ffn_in,
    first_ffn_out,
    first_vectors,
    second_attn_in,
    second_attn_out,
    second_ffn_in,
    second_ffn_out,
    second_vectors,
):
    cycle = lax.axis_size("ctx")
    count = layer_in.shape[1]
    width = layer_in.shape[2]
    group_tokens = count * cycle
    prompt = group_tokens // 2
    scale = HEAD_DIM ** (-0.5)
    span = math.gcd(512, group_tokens)
    nblocks = group_tokens // span
    seg_all, pos_all = layout(block_map[0], prompt)
    offset = lax.axis_index("ctx") * count
    seg_mine = lax.dynamic_slice_in_dim(seg_all, offset, count)
    pos_mine = lax.dynamic_slice_in_dim(pos_all, offset, count)
    owned = (
        attn_in.astype(jnp.bfloat16),
        attn_out.astype(jnp.bfloat16),
        ffn_in.astype(jnp.bfloat16),
        ffn_out.astype(jnp.bfloat16),
        vectors.astype(jnp.bfloat16),
    )
    gathered = (
        lax.all_gather(owned[0], ("ctx", "fsdp"), axis=0, tiled=True),
        lax.all_gather(owned[1], ("ctx", "fsdp"), axis=0, tiled=True),
        lax.all_gather(owned[2], ("ctx", "fsdp"), axis=0, tiled=True),
        lax.all_gather(owned[3], ("ctx", "fsdp"), axis=0, tiled=True),
        lax.all_gather(owned[4], ("ctx", "fsdp"), axis=0, tiled=True),
    )
    w_qkv, w_attn, w_up, w_down = (gathered[0], gathered[1], gathered[2], gathered[3])
    vec = gathered[4].astype(jnp.float32)
    inputs = layer_in[0].astype(jnp.float32)
    normed_one, scaled_one = standardize(inputs)
    attn_act = (normed_one * vec[:, 0] + vec[:, 1]).astype(jnp.bfloat16)
    bias = jnp.concatenate([vec[:, 2], vec[:, 3], vec[:, 4]])
    project = jnp.dot(attn_act, w_qkv, preferred_element_type=jnp.float32) + bias
    cosine, sine = angles(pos_mine)
    query = rotate(project[:, :width].reshape(count, HEADS, HEAD_DIM), cosine, sine, 1.0).astype(
        jnp.bfloat16
    )
    key_own = (
        rotate(project[:, width : 2 * width].reshape(count, HEADS, HEAD_DIM), cosine, sine, 1.0)
        .astype(jnp.bfloat16)
        .reshape(count, width)
    )
    value_own = project[:, 2 * width :].astype(jnp.bfloat16)
    keys_all, values_all = (
        lax.all_gather(key_own, "ctx", axis=0, tiled=True),
        lax.all_gather(value_own, "ctx", axis=0, tiled=True),
    )
    key_heads = keys_all.reshape(group_tokens, HEADS, HEAD_DIM)
    value_heads = values_all.reshape(group_tokens, HEADS, HEAD_DIM)

    def allowed_for(first, length):
        key_seg = lax.dynamic_slice_in_dim(seg_all, first, length)
        key_pos = lax.dynamic_slice_in_dim(pos_all, first, length)
        return (key_pos[None, :] <= pos_mine[:, None]) & (
            (key_seg[None, :] == seg_mine[:, None]) | (key_seg[None, :] == 0)
        )

    def logits_for(first, length, allowed, source):
        block = lax.dynamic_slice_in_dim(source, first, length, 0)
        raw = jnp.einsum("qhd,khd->hqk", query, block, preferred_element_type=jnp.float32) * scale
        return jnp.where(allowed[None], raw, MASKED)

    def stats_step(index, carry):
        first = index * span
        allowed = allowed_for(first, span)

        def stats_live(state):
            top, total = state
            logits = logits_for(first, span, allowed, key_heads)
            fresh = jnp.maximum(top, jnp.max(logits, axis=-1))
            total = total * jnp.exp(top - fresh) + jnp.sum(
                jnp.exp(logits - fresh[..., None]), axis=-1
            )
            return (fresh, total)

        return lax.cond(jnp.any(allowed), stats_live, lambda state: state, carry)

    start_top = jnp.full((HEADS, count), MASKED, jnp.float32)
    start_total = jnp.zeros((HEADS, count), jnp.float32)
    top, total = lax.fori_loop(0, nblocks, stats_step, (start_top, start_total))
    log_total = top + jnp.log(total)

    def mix_step(index, accum):
        first = index * span
        allowed = allowed_for(first, span)

        def mix_live(acc):
            logits = logits_for(first, span, allowed, key_heads)
            probs_low = jnp.exp(logits - log_total[..., None]).astype(jnp.bfloat16)
            block = lax.dynamic_slice_in_dim(value_heads, first, span, 0)
            return acc + jnp.einsum(
                "hqk,khd->qhd", probs_low, block, preferred_element_type=jnp.float32
            )

        return lax.cond(jnp.any(allowed), mix_live, lambda acc: acc, accum)

    mixed = lax.fori_loop(0, nblocks, mix_step, jnp.zeros((count, HEADS, HEAD_DIM), jnp.float32))
    mixed_low = mixed.reshape(count, width).astype(jnp.bfloat16)
    resid = inputs + jnp.dot(mixed_low, w_attn, preferred_element_type=jnp.float32)
    normed_two, scaled_two = standardize(resid)
    ffn_act = (normed_two * vec[:, 5] + vec[:, 6]).astype(jnp.bfloat16)
    both = jnp.dot(ffn_act, w_up, preferred_element_type=jnp.float32)
    gate = both[:, :FF]
    upper = both[:, FF:]
    sigma = jax.nn.sigmoid(gate)
    active = gate * sigma
    hidden = (active * upper).astype(jnp.bfloat16)
    result = resid + jnp.dot(hidden, w_down, preferred_element_type=jnp.float32)
    layer_out = result.astype(jnp.bfloat16)[None]
    cot_low = cotangent[0]
    grad_hidden = jnp.einsum("td,fd->tf", cot_low, w_down, preferred_element_type=jnp.float32)
    grad_gate = grad_hidden * upper * sigma * (1.0 + gate * (1.0 - sigma))
    grad_upper = grad_hidden * active
    grad_both = jnp.concatenate([grad_gate, grad_upper], axis=1).astype(jnp.bfloat16)
    grad_ffn_act = jnp.einsum("tj,dj->td", grad_both, w_up, preferred_element_type=jnp.float32)
    grad_resid = cot_low.astype(jnp.float32) + norm_back(
        grad_ffn_act * vec[:, 5], normed_two, scaled_two
    )
    grad_branch = grad_resid.astype(jnp.bfloat16)
    grad_mixed = jnp.einsum(
        "td,ed->te", grad_branch, w_attn, preferred_element_type=jnp.float32
    ).astype(jnp.bfloat16)
    grad_heads = grad_mixed.reshape(count, HEADS, HEAD_DIM)
    back_keys, back_values = (key_heads, value_heads)

    def probs_and_grads(first, length, allowed):
        logits = logits_for(first, length, allowed, back_keys)
        probs = jnp.exp(logits - log_total[..., None])
        block = lax.dynamic_slice_in_dim(back_values, first, length, 0)
        grad_probs = jnp.einsum(
            "qhd,khd->hqk", grad_heads, block, preferred_element_type=jnp.float32
        )
        return (probs, grad_probs)

    def delta_step(index, accum):
        first = index * span
        allowed = allowed_for(first, span)

        def delta_live(acc):
            probs, grad_probs = probs_and_grads(first, span, allowed)
            return acc + jnp.sum(probs * grad_probs, axis=-1)

        return lax.cond(jnp.any(allowed), delta_live, lambda acc: acc, accum)

    delta = lax.fori_loop(0, nblocks, delta_step, jnp.zeros((HEADS, count), jnp.float32))

    def query_step(index, accum):
        first = index * span
        allowed = allowed_for(first, span)

        def query_live(acc):
            probs, grad_probs = probs_and_grads(first, span, allowed)
            grad_scores = (probs * (grad_probs - delta[..., None])).astype(jnp.bfloat16)
            block = lax.dynamic_slice_in_dim(back_keys, first, span, 0)
            return acc + jnp.einsum(
                "hqk,khd->qhd", grad_scores, block, preferred_element_type=jnp.float32
            )

        return lax.cond(jnp.any(allowed), query_live, lambda acc: acc, accum)

    grad_query = scale * lax.fori_loop(
        0, nblocks, query_step, jnp.zeros((count, HEADS, HEAD_DIM), jnp.float32)
    )
    piece = math.gcd(span, count * lax.axis_size("ctx"))
    steps = count * lax.axis_size("ctx") // piece

    def one(index):
        begin = index * piece
        allowed = allowed_for(begin, piece)

        def one_live(unused):
            probs, grad_probs = probs_and_grads(begin, piece, allowed)
            grad_scores = (probs * (grad_probs - delta[..., None])).astype(jnp.bfloat16)
            probs_low = probs.astype(jnp.bfloat16)
            grad_key = scale * jnp.einsum(
                "hqk,qhd->khd", grad_scores, query, preferred_element_type=jnp.float32
            )
            grad_value = jnp.einsum(
                "hqk,qhd->khd", probs_low, grad_heads, preferred_element_type=jnp.float32
            )
            return jnp.concatenate(
                [grad_key.reshape(piece, width), grad_value.reshape(piece, width)], axis=1
            )

        def skip(unused):
            return jnp.zeros((piece, 2 * width), jnp.float32)

        return lax.cond(jnp.any(allowed), one_live, skip, 0)

    key_grads = lax.psum_scatter(
        lax.map(one, jnp.arange(steps, dtype=jnp.int32))
        .reshape(count * lax.axis_size("ctx"), 2 * width)
        .astype(jnp.bfloat16),
        "ctx",
        scatter_dimension=0,
        tiled=True,
    ).astype(jnp.float32)
    grad_key_own = rotate(
        key_grads[:, :width].reshape(count, HEADS, HEAD_DIM), cosine, sine, -1.0
    ).reshape(count, width)
    grad_query_pre = rotate(grad_query, cosine, sine, -1.0).reshape(count, width)
    grad_project = jnp.concatenate(
        [grad_query_pre, grad_key_own, key_grads[:, width:]], axis=1
    ).astype(jnp.bfloat16)
    grad_attn_act = jnp.einsum("tj,dj->td", grad_project, w_qkv, preferred_element_type=jnp.float32)
    input_grad = (grad_resid + norm_back(grad_attn_act * vec[:, 0], normed_one, scaled_one))[None]
    bias_grads = jnp.sum(grad_project.astype(jnp.float32), axis=0).reshape(3, width)
    vector_grads = jnp.stack(
        [
            jnp.sum(grad_attn_act * normed_one, axis=0),
            jnp.sum(grad_attn_act, axis=0),
            bias_grads[0],
            bias_grads[1],
            bias_grads[2],
            jnp.sum(grad_ffn_act * normed_two, axis=0),
            jnp.sum(grad_ffn_act, axis=0),
        ],
        axis=1,
    )
    wide_share = lax.psum_scatter(
        jnp.concatenate(
            [
                jnp.einsum("tr,tj->rj", attn_act, grad_project, preferred_element_type=jnp.float32),
                jnp.einsum("tr,tj->rj", mixed_low, grad_branch, preferred_element_type=jnp.float32),
                jnp.einsum("tr,tj->rj", ffn_act, grad_both, preferred_element_type=jnp.float32),
                vector_grads,
            ],
            axis=1,
        ),
        ("ctx", "fsdp"),
        scatter_dimension=0,
        tiled=True,
    )
    down_share = lax.psum_scatter(
        jnp.einsum("tr,tj->rj", hidden, cot_low, preferred_element_type=jnp.float32),
        ("ctx", "fsdp"),
        scatter_dimension=0,
        tiled=True,
    )
    grad_attn_in = wide_share[:, : 3 * width]
    grad_attn_out = wide_share[:, 3 * width : 4 * width]
    grad_ffn_in = wide_share[:, 4 * width : 4 * width + 2 * FF]
    grad_vectors = wide_share[:, 4 * width + 2 * FF :]
    grad_list = (grad_attn_in, grad_attn_out, grad_ffn_in, down_share, grad_vectors)
    squares = jnp.float32(0.0)
    for grad in grad_list:
        squares = squares + jnp.sum(grad * grad)
    grad_norm = jnp.sqrt(lax.psum(squares, ("ctx", "fsdp")))
    clip = jnp.minimum(1.0, CLIP_LIMIT / (grad_norm + 1e-06))
    rates = (D ** (-0.5), 0.6 * max(D // 64, 32) ** (-0.5), D ** (-0.5), (FF // 4) ** (-0.5), 0.3)
    weights = (attn_in, attn_out, ffn_in, ffn_out, vectors)
    firsts = (first_attn_in, first_attn_out, first_ffn_in, first_ffn_out, first_vectors)
    seconds = (second_attn_in, second_attn_out, second_ffn_in, second_ffn_out, second_vectors)
    updated = []
    for index in range(5):
        updated.append(
            adam(
                weights[index], clip * grad_list[index], firsts[index], seconds[index], rates[index]
            )
        )
    return (
        layer_out,
        input_grad,
        grad_norm,
        updated[0][0],
        updated[0][1],
        updated[0][2],
        updated[1][0],
        updated[1][1],
        updated[1][2],
        updated[2][0],
        updated[2][1],
        updated[2][2],
        updated[3][0],
        updated[3][1],
        updated[3][2],
        updated[4][0],
        updated[4][1],
        updated[4][2],
    )


def solution(mesh):
    placed = (
        P("fsdp", "ctx", None),
        P("fsdp", "ctx", None),
        P("fsdp", None),
        P(("ctx", "fsdp"), None),
        P(("ctx", "fsdp"), None),
        P(("ctx", "fsdp"), None),
        P(("ctx", "fsdp"), None),
        P(("ctx", "fsdp"), None),
        P(("ctx", "fsdp"), None),
        P(("ctx", "fsdp"), None),
        P(("ctx", "fsdp"), None),
        P(("ctx", "fsdp"), None),
        P(("ctx", "fsdp"), None),
        P(("ctx", "fsdp"), None),
        P(("ctx", "fsdp"), None),
        P(("ctx", "fsdp"), None),
        P(("ctx", "fsdp"), None),
        P(("ctx", "fsdp"), None),
    )
    return jax.shard_map(
        local,
        mesh=mesh,
        in_specs=placed,
        out_specs=(
            P("fsdp", "ctx", None),
            P("fsdp", "ctx", None),
            P(),
            P(("ctx", "fsdp"), None),
            P(("ctx", "fsdp"), None),
            P(("ctx", "fsdp"), None),
            P(("ctx", "fsdp"), None),
            P(("ctx", "fsdp"), None),
            P(("ctx", "fsdp"), None),
            P(("ctx", "fsdp"), None),
            P(("ctx", "fsdp"), None),
            P(("ctx", "fsdp"), None),
            P(("ctx", "fsdp"), None),
            P(("ctx", "fsdp"), None),
            P(("ctx", "fsdp"), None),
            P(("ctx", "fsdp"), None),
            P(("ctx", "fsdp"), None),
            P(("ctx", "fsdp"), None),
        ),
        check_vma=False,
    )
```

profile of v0, /device:TPU:0, one launch (start us, length us, event | category | flops | bytes accessed | tf_op | source)
XLA Modules:
  0.0 3668.4 jit_solution(10475353720529771770)
XLA Ops:
  9.8 71.5 %all-gather = bf16[32,64,7]{1,2,0:T(8,128)(2,1)S(1)} all-gather(bf16[1,64,7]{1,2,0:T(8,128)(2,1)S(1)} %convert_bitcast_fusion.1), channel_id=1, replica_groups=mesh['ctx'=8,'fsdp'=4] {'ctx','fsdp'}, dimensions={0}, use_global_device_ids=true | all-gather | bytes 29568 | tf_op jit(solution)/shard_map/all_gather | solution.py:129
  82.2 87.2 %all-gather.8.cloned.1.call-done = bf16[2048,6144]{1,0:T(8,128)(2,1)} async-done(((bf16[64,6144]{1,0:T(8,128)(2,1)}), bf16[2048,6144]{1,0:T(8,128)(2,1)}) %all-gather.8.cloned.1.call-update) | async-done | bytes 25165840 | tf_op jit(solution)/shard_map/all_gather | solution.py:125
  169.5 11.8 convolution_add_fusion
  214.2 23.6 all-gather.10.cloned.1.call-done
  237.8 12.4 copy.171
  250.1 46.1 %all-gather.12.cloned.1.call-done = bf16[2048,2048]{0,1:T(8,128)(2,1)} async-done(((bf16[256,2048]{0,1:T(8,128)(2,1)}), bf16[2048,2048]{0,1:T(8,128)(2,1)}) %all-gather.12.cloned.1.call-update) | async-done | bytes 8388624 | tf_op jit(solution)/shard_map/all_gather | solution.py:149
  296.3 45.9 %while.74 = (s32[]{:T(128)}, f32[32,256]{1,0:T(8,128)S(1)}, f32[32,256]{1,0:T(8,128)S(1)}, s32[2048]{0:T(1024)S(1)}, s32[256]{0:T(256)S(1)}, /*index=5*/s32[2048...) while((s32[]{:T(128)}, f32[32,256]{1,0:T(8,128)S(1)}, ...), condition=%wide.region_8.9_spmd, body=%wide.region_2.8_spmd.sunk | while | flops 566903296 | bytes 37535040 | solution.py:184
  298.0 19.5 conditional.10
  298.0 10.1 fusion
  308.1 9.3 exponential_reduce_fusion
  322.7 19.5 conditional.10
  322.8 10.1 fusion
  332.9 9.3 exponential_reduce_fusion
  342.5 23.2 while.75
  344.7 7.8 conditional.11
  344.8 7.8 bitcast_add_fusion
  357.8 7.8 conditional.11
  357.8 7.8 bitcast_add_fusion
  366.8 10.3 all-gather.14.cloned.1.call-done
  377.0 6.3 fusion.144
  383.8 250.5 %all-gather.16.cloned.1.call-done = bf16[2048,11264]{1,0:T(8,128)(2,1)} async-done(((bf16[64,11264]{1,0:T(8,128)(2,1)}), bf16[2048,11264]{1,0:T(8,128)(2,1)}) %all-gather.16.cloned.1.call-update) | async-done | bytes 46137360 | tf_op jit(solution)/shard_map/all_gather | solution.py:127
  634.3 23.7 fusion.127
  658.0 122.3 %all-gather.18.cloned.1.call-done = bf16[5632,2048]{1,0:T(8,128)(2,1)} async-done(((bf16[176,2048]{1,0:T(8,128)(2,1)}), bf16[5632,2048]{1,0:T(8,128)(2,1)}) %all-gather.18.cloned.1.call-update) | async-done | bytes 23068688 | tf_op jit(solution)/shard_map/all_gather | solution.py:128
  780.3 18.7 multiply_convert_fusion.1
  799.0 22.0 multiply_reduce_fusion.2
  832.2 30.5 while.76
  833.9 11.7 conditional.12
  838.2 7.4 fusion.19
  850.9 11.7 conditional.12
  855.2 7.4 fusion.19
  862.7 137.7 %while.78 = (s32[]{:T(128)}, bf16[4,512,4096]{2,1,0:T(8,128)(2,1)}, s32[4]{0:T(128)S(1)}, s32[2048]{0:T(1024)S(1)}, s32[256]{0:T(256)S(1)}, /*index=5*/s32[2048]...) while((s32[]{:T(128)}, bf16[4,512,4096]{2,1,0:T(8,128)(2,1)}, ...), condition=%wide.region_33.34_spmd, body=%wide.region_29.33_spmd.sunk | while | flops 2200568320 | bytes 88587616 | solution.py:295
  866.1 38.2 %conditional.14 = (bf16[1,512,4096]{1,2,0:T(8,128)(2,1)}) conditional(s32[]{:T(128)} %convert_element_type.223, () %tuple.269, (pred[256,512]{0,1:T(8,128)(4,1)S(1)}, s32[]{:T(128)}, bf16[2048,32,64]{0,2,1:T(8,128)(2,1)}, bf16[256,32,64]{0,2,1:T(8,128)(2,1)S(1)}, f32[32,256]{1,0:T(8,128)S(1)}, /*index=5*/bf16[2048,32,64]{0,2,1:T(8,128)(2,1)}, ...), branch_computations={%region_31.31_spmd, %region_32.32_spmd} | conditional | flops 2199912448 | bytes 71663672 | solution.py:292
  866.1 10.9 fusion.58
  877.0 9.9 fusion.49
  886.8 13.6 broadcast_multiply_fusion
  904.3 6.4 copy.242
  920.7 6.4 copy.242
  937.0 6.4 copy.242
  951.1 38.0 %conditional.14 = (bf16[1,512,4096]{1,2,0:T(8,128)(2,1)}) conditional(s32[]{:T(128)} %convert_element_type.223, () %tuple.269, (pred[256,512]{0,1:T(8,128)(4,1)S(1)}, s32[]{:T(128)}, bf16[2048,32,64]{0,2,1:T(8,128)(2,1)}, bf16[256,32,64]{0,2,1:T(8,128)(2,1)S(1)}, f32[32,256]{1,0:T(8,128)S(1)}, /*index=5*/bf16[2048,32,64]{0,2,1:T(8,128)(2,1)}, ...), branch_computations={%region_31.31_spmd, %region_32.32_spmd} | conditional | flops 2199912448 | bytes 71663672 | solution.py:292
  951.1 10.7 fusion.58
  961.8 9.9 fusion.49
  971.7 13.5 broadcast_multiply_fusion
  989.1 6.4 copy.242
  1001.6 19.6 fusion.95
  1021.6 47.9 %while.77 = (s32[]{:T(128)}, f32[256,32,64]{0,2,1:T(8,128)S(1)}, s32[2048]{0:T(1024)S(1)}, s32[256]{0:T(256)S(1)}, s32[2048]{0:T(1024)S(1)}, /*index=5*/s32[256]...) while((s32[]{:T(128)}, f32[256,32,64]{0,2,1:T(8,128)S(1)}, ...), condition=%wide.region_28.29_spmd, body=%wide.region_24.28_spmd.sunk | while | flops 1636958720 | bytes 46481744 | solution.py:265
  1023.3 20.4 conditional.13
  1023.3 9.7 fusion.34
  1033.0 10.7 bitcast_add_fusion.1
  1049.0 20.4 conditional.13
  1049.0 9.7 fusion.34
  1058.7 10.7 bitcast_add_fusion.1
  1077.8 9.8 fusion.99
  1087.6 44.3 %fusion.71 = f32[2048,11264]{1,0:T(8,128)} fusion(bf16[256,5632]{1,0:T(8,128)(2,1)} %get-tuple-element.1291, bf16[256,5632]{1,0:T(8,128)(2,1)} %get-tuple-element.1290, f32[256,2048]{1,0:T(8,128)S(1)} %copy-done.1, f32[2048]{0:T(1024)S(1)} %bitcast.219, f32[2048]{0:T(1024)S(1)} %bitcast.217, f32[256]{0:T(256)S(1)} %copy-done.34, f32[256]{0:T(256)S(1)} %copy-done.32), kind=kOutput, calls=%fused_computation.91 | convolution fusion | flops 11825315840 | bytes 100157440 | tf_op jit(solution)/shard_map/tr,tj->rj/dot_general | solution.py:329
  1131.9 78.1 %reduce-scatter.6.cloned.1.call-done = bf16[256,4096]{1,0:T(8,128)(2,1)} async-done(((bf16[2048,4096]{1,0:T(8,128)(2,1)}), bf16[256,4096]{1,0:T(8,128)(2,1)}) %reduce-scatter.6.cloned.1.call-update) | async-done | bytes 2097168 | tf_op jit(solution)/shard_map/reduce_scatter | solution.py:294
  1219.8 13.8 fusion.91
  1242.0 20.8 fusion.123
  1262.8 190.1 %concatenate.44 = f32[2048,19463]{1,0:T(8,128)} concatenate(f32[2048,6144]{1,0:T(8,128)} %fusion.123, f32[2048,2048]{1,0:T(8,128)} %fusion.99, f32[2048,11264]{1,0:T(8,128)} %fusion.71, f32[2048,1]{1,0:T(8,128)} %copy.180, f32[2048,1]{1,0:T(8,128)} %copy.181, f32[2048,1]{1,0:T(8,128)} %copy.182, f32[2048,1]{1,0:T(8,128)} %copy.183, f32[2048,1]{1,0:T(8,128)} %copy.184, ...), dimensions={1} | concatenate | bytes 318881792 | tf_op jit(solution)/shard_map/concatenate | solution.py:325
  1481.9 12.5 fusion.83
  1494.4 690.3 %reduce-scatter.8.cloned.1.call-done = f32[176,2048]{1,0:T(8,128)} async-done(((f32[5632,2048]{1,0:T(8,128)}), f32[176,2048]{1,0:T(8,128)}) %reduce-scatter.8.cloned.1.call-update) | async-done | bytes 1441808 | tf_op jit(solution)/shard_map/reduce_scatter | solution.py:338
  2187.1 1338.7 %reduce-scatter.10.cloned.1.call-done = f32[64,19463]{1,0:T(8,128)} async-done(((f32[2048,19463]{1,0:T(8,128)}), f32[64,19463]{1,0:T(8,128)}) %reduce-scatter.10.cloned.1.call-update) | async-done | bytes 4982544
  3560.0 39.4 %psum.7 = f32[]{:T(128)} all-reduce(f32[]{:T(128)S(6)} %add.409), channel_id=1, replica_groups=mesh['ctx'=8,'fsdp'=4] {'ctx','fsdp'}, use_global_device_ids=true, to_apply=%region_49.50 | all-reduce | flops 1 | bytes 8 | tf_op jit(solution)/shard_map/psum | solution.py:352
  3600.2 6.9 multiply_subtract_fusion.1
  3622.0 15.7 multiply_subtract_fusion
  3649.3 6.0 copy.208
  (331 shorter events, 238.7 us)
Async XLA Ops:
  7.2 2.6 copy-start.45
  7.2 74.3 %copy-start.3 = (bf16[1,256,2048]{2,1,0:T(8,128)(2,1)S(1)}, bf16[1,256,2048]{2,1,0:T(8,128)(2,1)}, u32[]{:S(2)}) copy-start(bf16[1,256,2048]{2,1,0:T(8,128)(2,1)} %param.40) | copy-start | bytes 3145732
  7.2 162.2 %all-gather.8.cloned.1.call-start = ((), (), s32[]{:S(2)}) async-start(), calls=%async_computation.3 | async-start | bytes 25952256 | tf_op jit(solution)/shard_map/all_gather | solution.py:125
  9.7 228.0 %all-gather.10.cloned.1.call-start = ((), (), s32[]{:S(2)}) async-start(), calls=%async_computation.4 | async-start | bytes 9437184 | tf_op jit(solution)/shard_map/all_gather | solution.py:150
  81.5 99.7 %copy-start.26 = (f32[2048,1]{0,1:T(1,128)}, f32[2048,1]{0,1:T(1,128)S(1)}, u32[]{:S(2)}) copy-start(f32[2048,1]{0,1:T(1,128)S(1)} %get-tuple-element.1311) | copy-start | bytes 24580
  81.5 99.7 %copy-start.29 = (f32[2048,1]{0,1:T(1,128)}, f32[2048,1]{0,1:T(1,128)S(1)}, u32[]{:S(2)}) copy-start(f32[2048,1]{0,1:T(1,128)S(1)} %get-tuple-element.1310) | copy-start | bytes 24580
  81.5 552.7 %copy-start.21 = (f32[2048,1]{0,1:T(1,128)}, f32[2048,1]{0,1:T(1,128)S(1)}, u32[]{:S(2)}) copy-start(f32[2048,1]{0,1:T(1,128)S(1)} %get-tuple-element.1306) | copy-start | bytes 24580
  81.5 739.6 %copy-start.19 = (f32[2048,1]{0,1:T(1,128)}, f32[2048,1]{0,1:T(1,128)S(1)}, u32[]{:S(2)}) copy-start(f32[2048,1]{0,1:T(1,128)S(1)} %get-tuple-element.1305) | copy-start | bytes 24580
  81.8 99.5 %copy-start.35 = (f32[256]{0:T(256)}, f32[256]{0:T(256)S(1)}, u32[]{:S(2)}) copy-start(f32[256]{0:T(256)S(1)} %broadcast_multiply_fusion.8) | copy-start | bytes 3076
  82.2 99.0 %copy-start.40 = (f32[256]{0:T(256)}, f32[256]{0:T(256)S(1)}, u32[]{:S(2)}) copy-start(f32[256]{0:T(256)S(1)} %add_rsqrt_fusion.1) | copy-start | bytes 3076
  181.3 2.6 copy-start.14
  183.9 1.9 copy-start.51
  183.9 1.9 copy-start.52
  183.9 1.9 copy-start.53
  183.9 1.9 copy-start.54
  183.9 1.9 copy-start.55
  183.9 1.9 copy-start.56
  183.9 1.9 copy-start.57
  185.1 111.2 %all-gather.12.cloned.1.call-start = ((), (), s32[]{:S(2)}) async-start(), calls=%async_computation.5 | async-start | bytes 9437184 | tf_op jit(solution)/shard_map/all_gather | solution.py:149
  191.8 11.3 copy-start.38
  203.1 4.5 copy-start.17
  203.1 5.3 copy-start.8
  207.5 169.5 %all-gather.14.cloned.1.call-start = ((), (), s32[]{:S(2)}) async-start(), calls=%async_computation.6 | async-start | bytes 8650752 | tf_op jit(solution)/shard_map/all_gather | solution.py:126
  208.4 425.9 %all-gather.16.cloned.1.call-start = ((), (), s32[]{:S(2)}) async-start(), calls=%async_computation.7 | async-start | bytes 47579136 | tf_op jit(solution)/shard_map/all_gather | solution.py:127
  209.7 4.4 copy-start.24
  209.7 4.4 copy-start.25
  209.7 570.6 %all-gather.18.cloned.1.call-start = ((), (), s32[]{:S(2)}) async-start(), calls=%async_computation.8 | async-start | bytes 23789568 | tf_op jit(solution)/shard_map/all_gather | solution.py:128
  212.1 997.9 %reduce-scatter.6.cloned.1.call-start = ((), (), s32[]{:S(2)}) async-start(), calls=%async_computation.9 | async-start | bytes 18874368 | tf_op jit(solution)/shard_map/reduce_scatter | solution.py:294
  383.4 437.7 %copy-start = (f32[256,2048]{1,0:T(8,128)}, f32[256,2048]{1,0:T(8,128)S(1)}, u32[]{:S(2)}) copy-start(f32[256,2048]{1,0:T(8,128)S(1)} %get-tuple-element.1333) | copy-start | bytes 6291460
  383.4 437.7 %copy-start.31 = (f32[256]{0:T(256)}, f32[256]{0:T(256)S(1)}, u32[]{:S(2)}) copy-start(f32[256]{0:T(256)S(1)} %broadcast_multiply_fusion.7) | copy-start | bytes 3076
  383.8 437.3 %copy-start.33 = (f32[256]{0:T(256)}, f32[256]{0:T(256)S(1)}, u32[]{:S(2)}) copy-start(f32[256]{0:T(256)S(1)} %add_rsqrt_fusion) | copy-start | bytes 3076
  1000.4 1184.3 %reduce-scatter.8.cloned.1.call-start = ((), (), s32[]{:S(2)}) async-start(), calls=%async_computation.10 | async-start | bytes 47579136 | tf_op jit(solution)/shard_map/reduce_scatter | solution.py:338
  1021.3 2504.5 %reduce-scatter.10.cloned.1.call-start = ((), (), s32[]{:S(2)}) async-start(), calls=%async_computation.11 | async-start | bytes 165445632
  1070.8 4.2 copy-start.48
  1070.8 5.5 copy-start.47
  1070.8 6.9 copy-start.7
  1072.6 1.4 copy-start.13
  1077.7 9.9 copy-start.1
  1077.7 9.9 copy-start.20
  1077.7 9.9 copy-start.22
  1077.7 9.9 copy-start.32
  1077.8 9.9 copy-start.34
  1215.1 4.7 copy-start.4
  1215.1 4.7 copy-start.27
  1215.1 4.7 copy-start.36
  1215.2 4.7 copy-start.41
  1236.3 5.6 copy-start.30
  1452.9 3.5 copy-start.18
  1452.9 4.8 copy-start.9
  1464.9 3.4 copy-start.23
  1464.9 7.1 copy-start.16
  1476.3 5.6 copy-start.2
  1481.9 12.5 copy-start.59
  1481.9 12.5 copy-start.58
  3547.3 4.1 slice-start
  3547.3 8.0 copy-start.28
  3547.3 8.0 copy-start.37
  3547.3 8.0 copy-start.42
  3610.3 3.4 copy-start.6
  3649.3 6.0 copy-start.46
  3649.3 6.0 copy-start.49
  3649.3 6.0 copy-start.50
  3649.3 6.6 copy-start.11
  3649.3 6.6 copy-start.12
  (6 other events, 7.3 us)
Sparse Core Ops, SparseCore 0:
  11.5 157.9 all-gather.7
  185.2 52.5 all-gather.9
  240.2 55.9 all-gather.11
  299.6 77.3 all-gather.13
  380.3 253.9 all-gather.15
  637.5 142.7 all-gather.17
  1000.5 209.4 reduce-scatter.5
  1212.3 972.3 reduce-scatter.7
  2191.2 1334.5 reduce-scatter.9
where the time goes:
time: 3680 us; the launch traced here: 3670 us
  waiting for transfers between devices  2650 us (72%)
  matrix products  378 us (10%)
  local copies, waits for them, and re-layouts  373 us (10%)
  other arithmetic  122 us (3%)
  blocking collectives  111 us (3%)
    unnamed x10, waiting for transfers between devices  1340 us
    reduce_scatter x1, waiting for transfers between devices, local(): lax.psum_scatter(jnp.einsum('tr,tj->rj', hidden, cot_low, preferred_eleme...  690 us
    all_gather x1, waiting for transfers between devices, local(): lax.all_gather(owned[2], ('ctx', 'fsdp'), axis=0, tiled=True)  250 us
    concatenate x1, local copies, waits for them, and re-layouts, local(): jnp.concatenate([jnp.einsum('tr,tj->rj', attn_act, grad_project, preferre...  190 us
    all_gather x1, waiting for transfers between devices, local(): lax.all_gather(owned[3], ('ctx', 'fsdp'), axis=0, tiled=True)  122 us
    all_gather x1, waiting for transfers between devices, local(): lax.all_gather(owned[0], ('ctx', 'fsdp'), axis=0, tiled=True)  87.2 us
    reduce_scatter x1, waiting for transfers between devices, local(): lax.psum_scatter(lax.map(one, jnp.arange(steps, dtype=jnp.int32)).reshape...  78.1 us
    unnamed x142, local copies, waits for them, and re-layouts  76.4 us
  transfers between devices with their start and end apart: 9, of which 9 were waited for; matrix products, arithmetic and copies ran while one was open for 15% of the time, Pallas kernels for 0%

commit v1 on v0

v1 whole, which is shorter than its diff:
```python
import functools
import math

import jax
import jax.numpy as jnp
from jax import lax
from jax.experimental import pallas as pl
from jax.experimental.pallas import tpu as pltpu
from jax.sharding import PartitionSpec as P

D = 2048
HEADS = 32
HEAD_DIM = 64
FF = 5632
ROTARY = 16
CONT = 1024
BLOCK = 256
STEP = 10

NORM_EPS = 1e-05
BETA_ONE = 0.9
BETA_TWO = 0.95
ADAM_EPS = 1e-08
DECAY = 0.1
CLIP_LIMIT = 1.0
ROPE_BASE = 10000.0
MASKED = -1e30
LANES = 128
SCALE = HEAD_DIM**-0.5
SCALE_LOG2 = SCALE * math.log2(math.e)
VMEM_LIMIT = 52 * 1024 * 1024
BF16 = jnp.bfloat16
F32 = jnp.float32

ORDER = (0, 2, 4, 6, 1, 3, 5, 7)


def standardize(values):
    center = values - jnp.mean(values, axis=-1, keepdims=True)
    scaled = lax.rsqrt(jnp.mean(center * center, axis=-1, keepdims=True) + NORM_EPS)
    return (center * scaled, scaled)


def norm_back(grad_normed, normed, scaled):
    return scaled * (
        grad_normed
        - jnp.mean(grad_normed, axis=-1, keepdims=True)
        - normed * jnp.mean(grad_normed * normed, axis=-1, keepdims=True)
    )


def adam(weight, grad, first, second, rate):
    first = BETA_ONE * first + (1.0 - BETA_ONE) * grad
    second = BETA_TWO * second + (1.0 - BETA_TWO) * grad * grad
    fixed_first = first / (1.0 - BETA_ONE**STEP)
    fixed_second = second / (1.0 - BETA_TWO**STEP)
    weight = weight - rate * (fixed_first / (jnp.sqrt(fixed_second) + ADAM_EPS) + DECAY * weight)
    return (weight, first, second)


def dot(left, right, left_dim, right_dim):
    return lax.dot_general(
        left, right, (((left_dim,), (right_dim,)), ((), ())), preferred_element_type=F32
    )


def swap(value, bit, axis="ctx"):
    size = lax.axis_size(axis)
    return lax.ppermute(value, axis, [(i, i ^ bit) for i in range(size)])


def cube():
    return lax.axis_size("ctx") == 8


def places():
    size = lax.axis_size("ctx")
    if cube():
        return lax.axis_index("ctx") ^ jnp.array(ORDER, jnp.int32)
    return jnp.arange(size, dtype=jnp.int32)


def gather_tokens(own):
    if not cube():
        return lax.all_gather(own, "ctx", axis=0, tiled=True)
    half = own.shape[0] // 2
    top, low = own[:half], own[half:]
    x_top = swap(top, 2)
    y_low = swap(low, 4)
    x_low = swap(low, 2)
    y_top = swap(top, 4)
    d_top = swap(x_top, 4)
    d_low = swap(y_low, 2)
    first = jnp.concatenate([own, x_top, x_low, y_top, y_low, d_top, d_low], axis=0)
    pieces = [own, x_top, x_low, y_top, y_low, d_top, d_low]
    other = [swap(piece, 1) for piece in pieces]
    return jnp.concatenate([first] + other, axis=0)


def scatter_tokens(make):
    size = lax.axis_size("ctx")
    if not cube():
        return lax.psum_scatter(
            make(0, size * BLOCK).astype(BF16), "ctx", scatter_dimension=0, tiled=True
        ).astype(F32)
    half = BLOCK // 2
    away = make(4 * BLOCK, 8 * BLOCK).astype(BF16)
    near = make(0, 4 * BLOCK)
    total = near + swap(away, 1).astype(F32)
    own = total[:BLOCK]
    x_part = total[BLOCK : 2 * BLOCK]
    y_part = total[2 * BLOCK : 3 * BLOCK]
    diag = total[3 * BLOCK :].astype(BF16)
    d_top = swap(diag[:half], 2).astype(F32)
    d_low = swap(diag[half:], 4).astype(F32)
    x_top = swap(x_part[:half].astype(BF16), 2).astype(F32)
    y_low = swap(y_part[half:].astype(BF16), 4).astype(F32)
    x_low = swap((x_part[half:] + d_low).astype(BF16), 2).astype(F32)
    y_top = swap((y_part[:half] + d_top).astype(BF16), 4).astype(F32)
    return own + jnp.concatenate([x_top + y_top, x_low + y_low], axis=0)


def sum_everywhere(value):
    for axis in ("ctx", "fsdp"):
        bit = 1
        while bit < lax.axis_size(axis):
            value = value + swap(value, bit, axis)
            bit *= 2
    return value


def aligned(index, step=BLOCK):
    return pl.ds(pl.multiple_of(index * step, step), step)


def turn(field, cosine, sine):
    lane = lax.broadcasted_iota(jnp.int32, field.shape, 1) % HEAD_DIM
    half = ROTARY // 2
    partner = jnp.where(
        lane < half, pltpu.roll(field, LANES - half, 1), pltpu.roll(field, half, 1)
    )
    return field * cosine + partner * sine


def full_blocks(code, prompt_blocks):
    later = CONT // BLOCK
    inside = lax.rem(code - prompt_blocks, later)
    return jnp.where(code < prompt_blocks, code, prompt_blocks + inside)


def key_block(code, index, prompt_blocks):
    later = CONT // BLOCK
    start = code - lax.rem(code - prompt_blocks, later)
    shifted = start + index - prompt_blocks
    return jnp.where(index < prompt_blocks, index, shifted)


def transposed(value):
    return value.astype(F32).T.astype(BF16)


def split_rows(pair):
    zero = jnp.zeros((HEAD_DIM, pair.shape[1]), pair.dtype)
    return (
        jnp.concatenate([pair[:HEAD_DIM], zero], axis=0),
        jnp.concatenate([zero, pair[HEAD_DIM:]], axis=0),
    )


def causal():
    key = lax.broadcasted_iota(jnp.int32, (BLOCK, BLOCK), 0)
    query = lax.broadcasted_iota(jnp.int32, (BLOCK, BLOCK), 1)
    return key <= query


def attend_kernel(
    pairs, blocks, inv_ref, proj_ref, bias_ref, cos_ref, sin_ref, q_ref, k_ref, v_ref, mix_ref, lse_ref, vt_ref
):
    prompt_blocks = blocks // 2
    wide = pairs * LANES
    lanes = [slice(p * LANES, (p + 1) * LANES) for p in range(pairs)]

    def prepare(code, carry):
        rows = aligned(inv_ref[code])
        place = aligned(code)
        cosine = cos_ref[place, :]
        sine = sin_ref[place, :]
        for p in range(pairs):
            at = [slice(part * wide + p * LANES, part * wide + (p + 1) * LANES) for part in range(3)]
            field = [proj_ref[rows, a] + bias_ref[:, a] for a in at]
            q_ref[place, lanes[p]] = turn(field[0], cosine, sine).astype(BF16)
            k_ref[place, lanes[p]] = turn(field[1], cosine, sine).astype(BF16)
            v_ref[place, lanes[p]] = field[2].astype(BF16)
            vt_ref[lanes[p], place] = field[2].T.astype(BF16)
        return carry

    lax.fori_loop(0, blocks, prepare, 0)
    allowed = causal()

    def one_query(code, carry):
        place = aligned(code)
        rows = aligned(inv_ref[code])
        heads = []
        for p in range(pairs):
            heads.extend(split_rows(transposed(q_ref[place, lanes[p]])))

        def scores(h, at):
            return dot(k_ref[at, lanes[h // 2]], heads[h], 1, 0) * SCALE_LOG2

        def mixing(h, at, probs):
            return dot(
                vt_ref[h * HEAD_DIM : (h + 1) * HEAD_DIM, at], probs.astype(BF16), 1, 0
            )

        state = []
        for h in range(2 * pairs):
            logits = jnp.where(allowed, scores(h, place), MASKED)
            top = jnp.max(logits, axis=0, keepdims=True)
            probs = jnp.exp2(logits - top)
            state.append((top, jnp.sum(probs, axis=0, keepdims=True), mixing(h, place, probs)))

        def step(index, state):
            at = aligned(key_block(code, index, prompt_blocks))
            fresh = []
            for h in range(2 * pairs):
                top, total, mixed = state[h]
                logits = scores(h, at)
                higher = jnp.maximum(top, jnp.max(logits, axis=0, keepdims=True))
                probs = jnp.exp2(logits - higher)
                fade = jnp.exp2(top - higher)
                fresh.append(
                    (
                        higher,
                        total * fade + jnp.sum(probs, axis=0, keepdims=True),
                        mixed * fade + mixing(h, at, probs),
                    )
                )
            return tuple(fresh)

        state = lax.fori_loop(0, full_blocks(code, prompt_blocks), step, tuple(state))
        for p in range(pairs):
            both = []
            for h in (2 * p, 2 * p + 1):
                top, total, mixed = state[h]
                both.append(mixed / total)
                lse_ref[h : h + 1, place] = top + jnp.log2(total)
            mix_ref[rows, lanes[p]] = jnp.concatenate(both, axis=0).T.astype(BF16)
        return carry

    lax.fori_loop(0, blocks, one_query, 0)


def attend(inv, project, bias, cosine, sine, pairs, blocks):
    tokens = blocks * BLOCK
    wide = pairs * LANES
    vmem = pl.BlockSpec(memory_space=pltpu.VMEM)
    low = jax.ShapeDtypeStruct((tokens, wide), BF16)
    return pl.pallas_call(
        functools.partial(attend_kernel, pairs, blocks),
        out_shape=(low, low, low, low, jax.ShapeDtypeStruct((2 * pairs, tokens), F32)),
        in_specs=[pl.BlockSpec(memory_space=pltpu.SMEM)] + [vmem] * 4,
        out_specs=(vmem,) * 5,
        scratch_shapes=[pltpu.VMEM((wide, tokens), BF16)],
        compiler_params=pltpu.CompilerParams(vmem_limit_bytes=VMEM_LIMIT),
        cost_estimate=pl.CostEstimate(
            flops=20 * pairs * tokens * tokens * HEAD_DIM,
            bytes_accessed=tokens * wide * 20,
            transcendentals=pairs * tokens * tokens,
        ),
        name="attend",
    )(inv, project, bias, cosine, sine)


def attend_back_kernel(
    pairs, blocks, inv_ref, q_ref, k_ref, v_ref, do_ref, lse_ref, cos_ref, sin_ref, gp_ref, kt_ref, dk_ref, dv_ref, p_ref, dp_ref
):
    prompt_blocks = blocks // 2
    wide = pairs * LANES
    lanes = [slice(p * LANES, (p + 1) * LANES) for p in range(pairs)]
    count = 2 * pairs

    def prepare(code, carry):
        place = aligned(code)
        for p in range(pairs):
            kt_ref[lanes[p], place] = transposed(k_ref[place, lanes[p]])
            zero = jnp.zeros((BLOCK, LANES), F32)
            dk_ref[place, lanes[p]] = zero
            dv_ref[place, lanes[p]] = zero
        return carry

    lax.fori_loop(0, blocks, prepare, 0)
    allowed = causal()
    lane = lax.broadcasted_iota(jnp.int32, (BLOCK, LANES), 1)

    def one_query(code, carry):
        place = aligned(code)
        rows = aligned(inv_ref[code])
        q_heads, do_heads, q_rows, do_rows = [], [], [], []
        for p in range(pairs):
            query = q_ref[place, lanes[p]]
            grad = do_ref[rows, lanes[p]]
            q_heads.extend(split_rows(transposed(query)))
            do_heads.extend(split_rows(transposed(grad)))
            for h in range(2):
                mine = (lane >= h * HEAD_DIM) & (lane < (h + 1) * HEAD_DIM)
                q_rows.append(jnp.where(mine, query, jnp.zeros_like(query)))
                do_rows.append(jnp.where(mine, grad, jnp.zeros_like(grad)))

        def probs_and_grads(slot, at, mask, sums):
            fresh = []
            for h in range(count):
                logits = dot(k_ref[at, lanes[h // 2]], q_heads[h], 1, 0) * SCALE_LOG2
                probs = jnp.exp2(logits - lse_ref[h : h + 1, place])
                if mask is not None:
                    probs = jnp.where(mask, probs, 0.0)
                grads = dot(v_ref[at, lanes[h // 2]], do_heads[h], 1, 0)
                p_ref[h, aligned(slot), :] = probs
                dp_ref[h, aligned(slot), :] = grads
                fresh.append(sums[h] + jnp.sum(probs * grads, axis=0, keepdims=True))
            return tuple(fresh)

        full = full_blocks(code, prompt_blocks)
        sums = probs_and_grads(full, place, allowed, (jnp.zeros((1, BLOCK), F32),) * count)
        sums = lax.fori_loop(
            0,
            full,
            lambda index, sums: probs_and_grads(
                index, aligned(key_block(code, index, prompt_blocks)), None, sums
            ),
            sums,
        )

        def step(index, grads):
            at = aligned(jnp.where(index == full, code, key_block(code, index, prompt_blocks)))
            fresh = []
            for p in range(pairs):
                for_key = dk_ref[at, lanes[p]]
                for_value = dv_ref[at, lanes[p]]
                for h in (2 * p, 2 * p + 1):
                    probs = p_ref[h, aligned(index), :]
                    low = (probs * (dp_ref[h, aligned(index), :] - sums[h])).astype(BF16)
                    for_key += dot(low, q_rows[h], 1, 0)
                    for_value += dot(probs.astype(BF16), do_rows[h], 1, 0)
                    fresh.append(
                        grads[h]
                        + dot(kt_ref[h * HEAD_DIM : (h + 1) * HEAD_DIM, at], low, 1, 0)
                    )
                dk_ref[at, lanes[p]] = for_key
                dv_ref[at, lanes[p]] = for_value
            return tuple(fresh)

        grads = lax.fori_loop(
            0, full + 1, step, (jnp.zeros((HEAD_DIM, BLOCK), F32),) * count
        )
        for p in range(pairs):
            pair = jnp.concatenate([grads[2 * p], grads[2 * p + 1]], axis=0).T * SCALE
            gp_ref[rows, lanes[p]] = turn(pair, cos_ref[place, :], -sin_ref[place, :]).astype(BF16)
        return carry

    lax.fori_loop(0, blocks, one_query, 0)

    def finish(code, carry):
        place = aligned(code)
        rows = aligned(inv_ref[code])
        for p in range(pairs):
            pair = dk_ref[place, lanes[p]] * SCALE
            at = slice(wide + p * LANES, wide + (p + 1) * LANES)
            gp_ref[rows, at] = turn(pair, cos_ref[place, :], -sin_ref[place, :]).astype(BF16)
            at = slice(2 * wide + p * LANES, 2 * wide + (p + 1) * LANES)
            gp_ref[rows, at] = dv_ref[place, lanes[p]].astype(BF16)
        return carry

    lax.fori_loop(0, blocks, finish, 0)


def attend_back(inv, query, key, value, grad, lse, cosine, sine, pairs, blocks):
    tokens = blocks * BLOCK
    wide = pairs * LANES
    vmem = pl.BlockSpec(memory_space=pltpu.VMEM)
    return pl.pallas_call(
        functools.partial(attend_back_kernel, pairs, blocks),
        out_shape=jax.ShapeDtypeStruct((tokens, 3 * wide), BF16),
        in_specs=[pl.BlockSpec(memory_space=pltpu.SMEM)] + [vmem] * 7,
        out_specs=vmem,
        scratch_shapes=[
            pltpu.VMEM((wide, tokens), BF16),
            pltpu.VMEM((tokens, wide), F32),
            pltpu.VMEM((tokens, wide), F32),
            pltpu.VMEM((2 * pairs, tokens, BLOCK), F32),
            pltpu.VMEM((2 * pairs, tokens, BLOCK), F32),
        ],
        compiler_params=pltpu.CompilerParams(vmem_limit_bytes=VMEM_LIMIT),
        cost_estimate=pl.CostEstimate(
            flops=60 * pairs * tokens * tokens * HEAD_DIM,
            bytes_accessed=tokens * wide * 20,
            transcendentals=pairs * tokens * tokens,
        ),
        name="attend_back",
    )(inv, query, key, value, grad, lse, cosine, sine)


def turn_tables(blocks):
    prompt_blocks = blocks // 2
    later = CONT // BLOCK
    token = jnp.arange(blocks * BLOCK, dtype=jnp.int32)
    code = token // BLOCK
    inner = token % BLOCK
    place = jnp.where(
        code < prompt_blocks,
        token,
        prompt_blocks * BLOCK + (code - prompt_blocks) % later * BLOCK + inner,
    )
    half = ROTARY // 2
    freq = jnp.power(ROPE_BASE, -2.0 * jnp.arange(half, dtype=F32) / ROTARY)
    angle = place.astype(F32)[:, None] * freq[None, :]
    cosine, sine = jnp.cos(angle), jnp.sin(angle)
    rest = HEAD_DIM - ROTARY
    ones = jnp.ones((blocks * BLOCK, rest), F32)
    one_cos = jnp.concatenate([cosine, cosine, ones], axis=1)
    one_sin = jnp.concatenate([-sine, sine, 0.0 * ones], axis=1)
    return (jnp.tile(one_cos, (1, 2)), jnp.tile(one_sin, (1, 2)))


def local(
    layer_in,
    cotangent,
    block_map,
    attn_in,
    attn_out,
    ffn_in,
    ffn_out,
    vectors,
    first_attn_in,
    first_attn_out,
    first_ffn_in,
    first_ffn_out,
    first_vectors,
    second_attn_in,
    second_attn_out,
    second_ffn_in,
    second_ffn_out,
    second_vectors,
):
    cycle = lax.axis_size("ctx")
    groups = lax.axis_size("fsdp")
    here = lax.axis_index("ctx")
    owner = here * groups + lax.axis_index("fsdp")
    blocks = block_map.shape[1]
    rows = attn_in.shape[0]
    wide = D // cycle
    pairs = wide // LANES
    units = FF // cycle
    padded = (units + LANES - 1) // LANES * LANES
    gap = padded - units

    mine = vectors.astype(BF16).T
    vec = lax.dynamic_update_slice(jnp.zeros((7, D), BF16), mine, (0, owner * rows))
    vec = sum_everywhere(vec).astype(F32)

    def spread(weight, parts):
        width = weight.shape[1] // (parts * cycle)
        split = weight.astype(BF16).reshape(rows, parts, cycle, width)
        split = split.transpose(2, 0, 1, 3).reshape(cycle, rows, parts * width)
        return lax.all_to_all(split, "ctx", 0, 0)

    def rows_of(split):
        full = lax.all_gather(split, "fsdp", axis=0, tiled=False)
        return full.transpose(1, 0, 2, 3).reshape(D, split.shape[2])

    w_qkv = rows_of(spread(attn_in, 3))
    w_attn = lax.all_gather(attn_out.astype(BF16), "fsdp", axis=0, tiled=True)
    both_in = rows_of(spread(ffn_in, 2))
    w_up = jnp.pad(both_in.reshape(D, 2, units), ((0, 0), (0, 0), (0, gap))).reshape(D, 2 * padded)
    w_down = lax.all_gather(ffn_out.astype(BF16), "fsdp", axis=0, tiled=True)
    w_down = jnp.pad(w_down, ((0, gap), (0, 0)))

    inputs = layer_in[0].astype(F32)
    normed_one, scaled_one = standardize(inputs)
    attn_act = gather_tokens((normed_one * vec[0] + vec[1]).astype(BF16))
    cot_low = gather_tokens(cotangent[0])
    codes = block_map[0][places()]
    inv = jnp.argsort(codes).astype(jnp.int32)
    cosine, sine = turn_tables(blocks)
    bias = lax.dynamic_slice_in_dim(vec[2:5], here * wide, wide, 1).reshape(1, 3 * wide)
    project = dot(attn_act, w_qkv, 1, 0)
    query, key, value, mixed, lse = attend(inv, project, bias, cosine, sine, pairs, blocks)
    resid = inputs + scatter_tokens(lambda a, b: dot(mixed[a:b], w_attn, 1, 0))

    normed_two, scaled_two = standardize(resid)
    ffn_act = gather_tokens((normed_two * vec[5] + vec[6]).astype(BF16))
    grad_hidden = dot(cot_low, w_down, 1, 1)
    both = dot(ffn_act, w_up, 1, 0)
    gate = both[:, :padded]
    upper = both[:, padded:]
    sigma = jax.nn.sigmoid(gate)
    active = gate * sigma
    hidden = (active * upper).astype(BF16)
    grad_gate = grad_hidden * upper * sigma * (1.0 + gate * (1.0 - sigma))
    grad_upper = grad_hidden * active
    grad_both = jnp.concatenate([grad_gate, grad_upper], axis=1).astype(BF16)
    grad_ffn_act = scatter_tokens(lambda a, b: dot(grad_both[a:b], w_up, 1, 1))

    def owners(grad):
        return lax.psum_scatter(grad, "fsdp", scatter_dimension=0, tiled=True).astype(F32)

    def owners_of_rows(grad):
        wider = grad.shape[1]
        split = grad.reshape(cycle, groups, rows, wider).transpose(1, 0, 2, 3)
        share = lax.psum_scatter(
            split.reshape(groups * cycle * rows, wider), "fsdp", scatter_dimension=0, tiled=True
        )
        return share.reshape(cycle, rows, wider)

    def collect(share, parts):
        width = share.shape[2] // parts
        split = lax.all_to_all(share, "ctx", 0, 0).reshape(cycle, rows, parts, width)
        return split.transpose(1, 2, 0, 3).reshape(rows, parts * cycle * width).astype(F32)

    grad_in = dot(ffn_act, grad_both, 0, 0).astype(BF16)
    grad_in = grad_in.reshape(D, 2, padded)[:, :, :units].reshape(D, 2 * units)
    share_in = owners_of_rows(grad_in)
    grad_down = dot(hidden, cot_low, 0, 0)[:units].astype(BF16)
    share_down = owners(grad_down)
    result = resid + scatter_tokens(lambda a, b: dot(hidden[a:b], w_down, 1, 0))
    layer_out = result.astype(BF16)[None]

    grad_resid = cotangent[0].astype(F32) + norm_back(
        grad_ffn_act * vec[5], normed_two, scaled_two
    )
    grad_branch = gather_tokens(grad_resid.astype(BF16))
    grad_mixed = dot(grad_branch, w_attn, 1, 1).astype(BF16)
    grad_project = attend_back(
        inv, query, key, value, grad_mixed, lse, cosine, sine, pairs, blocks
    )
    grad_attn_act = scatter_tokens(lambda a, b: dot(grad_project[a:b], w_qkv, 1, 1))
    input_grad = (grad_resid + norm_back(grad_attn_act * vec[0], normed_one, scaled_one))[None]
    share_out = owners(dot(mixed, grad_branch, 0, 0).astype(BF16))
    share_qkv = owners_of_rows(dot(attn_act, grad_project, 0, 0).astype(BF16))

    bias_grads = jnp.sum(grad_project.astype(F32), axis=0).reshape(3, wide)
    bias_grads = lax.dynamic_update_slice(jnp.zeros((3, D), F32), bias_grads, (0, here * wide))
    vector_grads = jnp.concatenate(
        [
            jnp.sum(grad_attn_act * normed_one, axis=0)[None],
            jnp.sum(grad_attn_act, axis=0)[None],
            bias_grads,
            jnp.sum(grad_ffn_act * normed_two, axis=0)[None],
            jnp.sum(grad_ffn_act, axis=0)[None],
        ],
        axis=0,
    )
    vector_grads = lax.dynamic_slice_in_dim(
        sum_everywhere(vector_grads), owner * rows, rows, 1
    ).T

    squares = F32(0.0)
    for grad in (share_qkv, share_out, share_in, share_down, vector_grads):
        wide_grad = grad.astype(F32)
        squares = squares + jnp.sum(wide_grad * wide_grad)
    grad_norm = jnp.sqrt(sum_everywhere(squares.reshape(1, 1)))[0, 0]
    clip = jnp.minimum(1.0, CLIP_LIMIT / (grad_norm + 1e-06))
    grad_list = (collect(share_qkv, 3), share_out, collect(share_in, 2), share_down, vector_grads)
    rates = (D ** (-0.5), 0.6 * max(D // 64, 32) ** (-0.5), D ** (-0.5), (FF // 4) ** (-0.5), 0.3)
    weights = (attn_in, attn_out, ffn_in, ffn_out, vectors)
    firsts = (first_attn_in, first_attn_out, first_ffn_in, first_ffn_out, first_vectors)
    seconds = (second_attn_in, second_attn_out, second_ffn_in, second_ffn_out, second_vectors)
    updated = []
    for index in range(5):
        updated.extend(
            adam(
                weights[index], clip * grad_list[index], firsts[index], seconds[index], rates[index]
            )
        )
    return (layer_out, input_grad, grad_norm, *updated)


def solution(mesh):
    tokens = P("fsdp", "ctx", None)
    owned = P(("ctx", "fsdp"), None)
    return jax.shard_map(
        local,
        mesh=mesh,
        in_specs=(tokens, tokens, P("fsdp", None)) + (owned,) * 15,
        out_specs=(tokens, tokens, P()) + (owned,) * 15,
        check_vma=False,
    )
```

time: 3680 us -> 870 us (0.24)
  waiting for transfers between devices: 2650 us -> 239 us
  matrix products: 378 us -> 148 us
  local copies, waits for them, and re-layouts: 373 us -> 178 us
  Pallas kernels: 0 us -> 98.6 us
  blocking collectives: 111 us -> 17.8 us
  starting transfers between devices: 0.66 us -> 92.7 us
  other arithmetic: 122 us -> 62.1 us
    unnamed x10 -> x8, waiting for transfers between devices: 1340 us -> 0.13 us
    reduce_scatter x2 -> x4, waiting for transfers between devices: 768 us -> 0.03 us  [the longest x2 0.02 us: owners(): lax.psum_scatter(grad, 'fsdp', scatter_dimension=0, tiled=True).astype(F32)]
    all_gather x6 -> x4, waiting for transfers between devices: 540 us -> 0.01 us  [the longest x2 0.01 us: rows_of(): full = lax.all_gather(split, 'fsdp', axis=0, tiled=False)]
    ppermute x0 -> x95, waiting for transfers between devices: none -> 239 us  [swap(): return lax.ppermute(value, axis, [(i, i ^ bit) for i in range(size)])]
    dot_general x30 -> x16, matrix products: 378 us -> 148 us  [dot(): lax.dot_general(left, right, (((left_dim,), (right_dim,)), ((), ())), pre...]
    concatenate x1 -> x7, local copies, waits for them, and re-layouts: 190 us -> 2.73 us  [the longest x4 2.5 us: gather_tokens(): return jnp.concatenate([first] + other, axis=0)]
    pallas_call x0 -> x2, Pallas kernels: none -> 98.6 us  [the longest x1 53.6 us: attend(): pl.pallas_call(functools.partial(attend_kernel, pairs, blocks), out_shape...]
    ppermute x0 -> x95, starting transfers between devices: none -> 79.9 us  [swap(): return lax.ppermute(value, axis, [(i, i ^ bit) for i in range(size)])]
  transfers between devices with their start and end apart: 9 -> 106, of which waited for: 9 -> 46; matrix products, arithmetic and copies ran while one was open for 15% -> 39% of each run, Pallas kernels for 0% -> 11%
where the time goes in v1:
time: 870 us; the launch traced here: 860 us
  waiting for transfers between devices  239 us (27%)
  local copies, waits for them, and re-layouts  178 us (20%)
  matrix products  148 us (17%)
  Pallas kernels  98.6 us (11%)
  starting transfers between devices  92.7 us (11%)
  other arithmetic  62.1 us (7%)
  between operations  23.5 us (3%)
  blocking collectives  17.8 us (2%)
    ppermute x95, waiting for transfers between devices, swap(): return lax.ppermute(value, axis, [(i, i ^ bit) for i in range(size)])  239 us
    dot_general x16, matrix products, dot(): lax.dot_general(left, right, (((left_dim,), (right_dim,)), ((), ())), pre...  148 us
    unnamed x163, local copies, waits for them, and re-layouts  80 us
    ppermute x95, starting transfers between devices, swap(): return lax.ppermute(value, axis, [(i, i ^ bit) for i in range(size)])  79.9 us
    pallas_call x1, Pallas kernels, attend(): pl.pallas_call(functools.partial(attend_kernel, pairs, blocks), out_shape...  53.6 us
    pallas_call x1, Pallas kernels, attend_back(): pl.pallas_call(functools.partial(attend_back_kernel, pairs, blocks), out_...  45 us
    all_to_all x1, blocking collectives, spread(): return lax.all_to_all(split, 'ctx', 0, 0)  17.8 us
  transfers between devices with their start and end apart: 106, of which 46 were waited for; matrix products, arithmetic and copies ran while one was open for 39% of the time, Pallas kernels for 11%

profile of v1, /device:TPU:0, one launch (start us, length us, event | category | flops | bytes accessed | tf_op | source)
XLA Modules:
  0.0 860.1 jit_solution(9793498026484471723)
XLA Ops:
  10.3 3.4 reshape.193
  13.7 17.8 %all_to_all.20 = bf16[8,64,768]{2,1,0:T(8,128)(2,1)} all-to-all(bf16[8,64,768]{2,1,0:T(8,128)(2,1)} %reshape.193), channel_id=1, replica_groups=mesh['ctx'=8,'fsdp'=4] {'ctx'}, dimensions={0} | all-to-all | bytes 1572864 | tf_op jit(solution)/shard_map/all_to_all | solution.py:464
  33.1 3.3 reshape.196
  39.6 3.6 all-to-all-start.1
  47.8 14.7 %collective-permute-done.1 = bf16[7,2048]{1,0:T(8,128)(2,1)S(1)} collective-permute-done((bf16[7,2048]{1,0:T(8,128)(2,1)S(1)}, bf16[7,2048]{1,0:T(8,128)(2,1)S(1)}, u32[]{:S(2)}, u32[]{:S(2)}) %collective-permute-start.1) | collective-permute-done | bytes 28704 | tf_op jit(solution)/shard_map/ppermute | solution.py:69
  74.4 4.2 collective-permute-done.4
  92.7 4.5 collective-permute-done.8
  102.2 7.6 collective-permute-done.6
  116.6 5.4 collective-permute-done.9
  137.5 11.8 %fusion.111.proj_ref = f32[2048,768]{1,0:T(8,128)} fusion(bf16[2048,2048]{1,0:T(8,128)(2,1)} %constant_dynamic-update-slice_fusion, bf16[2048,768]{1,0:T(8,128)(2,1)S(1)} %bitcast.158), kind=kOutput, calls=%fused_computation.257 | convolution fusion | flops 6442450944 | bytes 17825792 | tf_op jit(solution)/shard_map/dot_general | solution.py:62
  149.3 53.6 %attend.1 = (bf16[2048,256]{1,0:T(8,128)(2,1)S(1)}, bf16[2048,256]{1,0:T(8,128)(2,1)}, bf16[2048,256]{1,0:T(8,128)(2,1)}, bf16[2048,256]{1,0:T(8,128)(2,1)}, f32[4,2048]{1,0:T(4,128)S(1)}) custom-call(s32[8]{0:T(128)S(1)} %get-tuple-element.24.inv_ref, f32[2048,768]{1,0:T(8,128)} %fusion.111.proj_ref, f32[1,768]{1,0:T(1,128)S(1)} %bitcast.136, ...), custom_call_target="tpu_custom_call" | custom-call | flops 10737418240 | bytes 10485760 | tf_op jit(solution)/shard_map/attend/pallas_call | solution.py:258
  202.9 4.8 convolution_convert_fusion.2
  215.1 8.9 %collective-permute-done.48 = bf16[128,2048]{1,0:T(8,128)(2,1)} collective-permute-done((bf16[128,2048]{1,0:T(8,128)(2,1)}, bf16[128,2048]{1,0:T(8,128)(2,1)}, u32[]{:S(2)}, u32[]{:S(2)}) %collective-permute-start.48) | collective-permute-done | bytes 524320 | tf_op jit(solution)/shard_map/ppermute | solution.py:69
  226.8 8.5 collective-permute-done.46
  244.0 3.5 fusion.107
  248.5 5.4 collective-permute-done.49
  257.6 5.6 collective-permute-done.22
  271.0 7.9 collective-permute-done.19
  280.2 10.3 %collective-permute-done.24 = bf16[128,2048]{1,0:T(8,128)(2,1)S(1)} collective-permute-done((bf16[128,2048]{1,0:T(8,128)(2,1)S(1)}, bf16[128,2048]{1,0:T(8,128)(2,1)S(1)}, u32[]{:S(2)}, u32[]{:S(2)}) %collective-permute-start.24) | collective-permute-done | bytes 524320 | tf_op jit(solution)/shard_map/ppermute | solution.py:69
  301.7 5.6 copy.94
  307.3 15.3 %reshape_reshape.6 = bf16[2048,2,704]{2,1,0:T(2,128)(2,1)} reshape(bf16[8,4,64,1408]{3,2,1,0:T(8,128)(2,1)} %bitcast.139) | data formatting | bytes 11534336 | tf_op jit(solution)/shard_map/reshape;reshape | solution.py:473
  322.6 8.6 %pad.8 = bf16[2048,2,768]{2,1,0:T(2,128)(2,1)S(1)} pad(bf16[2048,2,704]{2,1,0:T(2,128)(2,1)} %reshape_reshape.6, bf16[]{:T(256)} %constant.60.clone.1), padding=0_0x0_0x0_64 | pad | bytes 12058626 | tf_op jit(solution)/shard_map/jit(_pad)/pad | solution.py:473
  342.8 6.6 collective-permute-done.29
  358.3 17.5 %fusion.112 = f32[2048,1536]{0,1:T(8,128)} fusion(bf16[2048,2048]{1,0:T(8,128)(2,1)} %constant_dynamic-update-slice_fusion.14, bf16[2048,1536]{1,0:T(8,128)(2,1)S(1)} %bitcast.145), kind=kOutput, calls=%fused_computation.258 | convolution fusion | flops 12884901888 | bytes 27262976 | tf_op jit(solution)/shard_map/dot_general | solution.py:62
  375.8 17.5 %multiply_convert_fusion = (bf16[2048,768]{0,1:T(8,128)(2,1)S(1)}, bf16[2048,768]{0,1:T(8,128)(2,1)}, bf16[2048,768]{0,1:T(8,128)(2,1)S(1)}) fusion(f32[2048,1536]{0,1:T(8,128)} %fusion.112, bf16[2048,2048]{1,0:T(8,128)(2,1)} %constant_dynamic-update-slice_fusion.28, bf16[704,2048]{1,0:T(8,128)(2,1)} %all-gather.9.cloned.1.call-done), kind=kOutput, calls=%fused_computation.12 | convolution fusion | flops 6466043904 | bytes 33292288 | tf_op jit(solution)/shard_map/dot_general | solution.py:62
  393.3 5.3 convolution_convert_fusion.4
  400.7 8.4 convolution_convert_fusion.1
  409.1 9.1 %fusion.113 = bf16[768,2048]{1,0:T(8,128)(2,1)S(1)} fusion(bf16[2048,768]{0,1:T(8,128)(2,1)S(1)} %get-tuple-element.68, bf16[2048,2048]{1,0:T(8,128)(2,1)} %constant_dynamic-update-slice_fusion.28), kind=kOutput, calls=%fused_computation.259 | convolution fusion | flops 6442450944 | bytes 14680064 | tf_op jit(solution)/shard_map/dot_general | solution.py:62
  420.1 7.1 fusion.109
  432.5 12.7 %fusion.108 = (bf16[1024,2048]{1,0:T(8,128)(2,1)S(1)}, f32[1024,2048]{1,0:T(8,128)}) fusion(bf16[1024,2048]{1,0:T(8,128)(2,1)} %collective-permute-done.58, bf16[2048,1536]{1,0:T(8,128)(2,1)} %bitcast.146, bf16[2048,768]{0,1:T(8,128)(2,1)} %get-tuple-element.67, bf16[2048,768]{0,1:T(8,128)(2,1)} %copy-done.52), kind=kOutput, calls=%fused_computation.254 | convolution fusion | flops 6455033856 | bytes 29360128 | tf_op jit(solution)/shard_map/dot_general | solution.py:62
  447.1 8.4 collective-permute-done.42
  458.5 10.4 %collective-permute-done.62 = bf16[128,2048]{1,0:T(8,128)(2,1)S(1)} collective-permute-done((bf16[128,2048]{1,0:T(8,128)(2,1)S(1)}, bf16[128,2048]{1,0:T(8,128)(2,1)S(1)}, u32[]{:S(2)}, u32[]{:S(2)}) %collective-permute-start.62) | collective-permute-done | bytes 524320 | tf_op jit(solution)/shard_map/ppermute | solution.py:69
  470.1 6.4 collective-permute-done.60
  483.2 8.1 collective-permute-done.43
  491.4 13.2 %collective-permute-done.61 = bf16[128,2048]{1,0:T(8,128)(2,1)S(1)} collective-permute-done((bf16[128,2048]{1,0:T(8,128)(2,1)S(1)}, bf16[128,2048]{1,0:T(8,128)(2,1)S(1)}, u32[]{:S(2)}, u32[]{:S(2)}) %collective-permute-start.61) | collective-permute-done | bytes 524320 | tf_op jit(solution)/shard_map/ppermute | solution.py:69
  504.9 3.5 multiply_reduce_fusion.1
  514.7 10.8 %collective-permute-done.68 = bf16[128,2048]{1,0:T(8,128)(2,1)S(1)} collective-permute-done((bf16[128,2048]{1,0:T(8,128)(2,1)S(1)}, bf16[128,2048]{1,0:T(8,128)(2,1)S(1)}, u32[]{:S(2)}, u32[]{:S(2)}) %collective-permute-start.68) | collective-permute-done | bytes 524320 | tf_op jit(solution)/shard_map/ppermute | solution.py:69
  527.2 10.8 %collective-permute-done.66 = bf16[128,2048]{1,0:T(8,128)(2,1)S(1)} collective-permute-done((bf16[128,2048]{1,0:T(8,128)(2,1)S(1)}, bf16[128,2048]{1,0:T(8,128)(2,1)S(1)}, u32[]{:S(2)}, u32[]{:S(2)}) %collective-permute-start.66) | collective-permute-done | bytes 524320 | tf_op jit(solution)/shard_map/ppermute | solution.py:69
  539.0 8.2 collective-permute-done.69
  551.4 3.3 copy-done.5
  554.8 3.3 convolution_convert_fusion.6
  558.2 18.1 %convolution_convert_fusion = bf16[2048,1536]{0,1:T(8,128)(2,1)S(1)} fusion(bf16[2048,2048]{1,0:T(8,128)(2,1)} %constant_dynamic-update-slice_fusion.14, bf16[2048,768]{0,1:T(8,128)(2,1)} %copy-done.52, bf16[2048,768]{0,1:T(8,128)(2,1)} %get-tuple-element.67), kind=kOutput, calls=%fused_computation.10 | convolution fusion | flops 12900630528 | bytes 20971520 | tf_op jit(solution)/shard_map/dot_general | solution.py:62
  579.3 16.3 %copy.86 = bf16[2048,2,704]{2,1,0:T(2,128)(2,1)} copy(bf16[2048,2,704]{0,2,1:T(8,128)(2,1)} %slice.322) | data formatting | bytes 11534336
  595.5 13.9 %reshape_reshape.7 = bf16[8,4,64,1408]{3,2,1,0:T(8,128)(2,1)} reshape(bf16[2048,2,704]{2,1,0:T(2,128)(2,1)} %copy.86) | data formatting | bytes 11534336 | tf_op jit(solution)/shard_map/reshape;reshape | solution.py:508
  609.4 5.6 copy.83
  616.3 6.8 convolution_convert_fusion.7.do_ref
  623.0 45.0 %attend_back.1 = bf16[2048,768]{1,0:T(8,128)(2,1)} custom-call(s32[8]{0:T(128)S(1)} %get-tuple-element.24.inv_ref, bf16[2048,256]{1,0:T(8,128)(2,1)S(1)} %get-tuple-element.26.q_ref, bf16[2048,256]{1,0:T(8,128)(2,1)} %get-tuple-element.27.k_ref, bf16[2048,256]{1,0:T(8,128)(2,1)} %get-tuple-element.28.v_ref, ...), custom_call_target="tpu_custom_call" | custom-call | flops 32212254720 | bytes 10485760 | tf_op jit(solution)/shard_map/attend_back/pallas_call | solution.py:380
  668.0 6.7 convolution_convert_fusion.3
  674.9 9.4 %convolution_convert_fusion.5 = bf16[2048,768]{1,0:T(8,128)(2,1)S(1)} fusion(bf16[2048,2048]{1,0:T(8,128)(2,1)} %constant_dynamic-update-slice_fusion, bf16[2048,768]{1,0:T(8,128)(2,1)S(1)} %copy-done.28), kind=kOutput, calls=%fused_computation.24 | convolution fusion | flops 6444023808 | bytes 14680064 | tf_op jit(solution)/shard_map/dot_general | solution.py:62
  688.3 5.7 fusion.110
  697.2 11.2 %collective-permute-done.82 = bf16[128,2048]{1,0:T(8,128)(2,1)S(1)} collective-permute-done((bf16[128,2048]{1,0:T(8,128)(2,1)S(1)}, bf16[128,2048]{1,0:T(8,128)(2,1)S(1)}, u32[]{:S(2)}, u32[]{:S(2)}) %collective-permute-start.82) | collective-permute-done | bytes 524320 | tf_op jit(solution)/shard_map/ppermute | solution.py:69
  721.2 5.1 collective-permute-done.81
  726.5 8.4 collective-permute-done.84
  735.1 3.9 fusion.31
  741.0 4.3 all-to-all-start.3
  750.0 15.3 %collective-permute-done.86 = f32[7,2048]{1,0:T(8,128)S(1)} collective-permute-done((f32[7,2048]{1,0:T(8,128)S(1)}, f32[7,2048]{1,0:T(8,128)S(1)}, u32[]{:S(2)}, u32[]{:S(2)}) %collective-permute-start.86) | collective-permute-done | bytes 57376 | tf_op jit(solution)/shard_map/ppermute | solution.py:69
  770.8 6.8 collective-permute-done.88
  799.7 3.2 collective-permute-start.93
  804.0 3.7 collective-permute-start.94
  809.2 4.4 all-to-all-start.2
  816.9 4.2 mul.487
  821.1 3.5 copy.85
  824.6 4.8 mul.489
  829.5 6.9 multiply_subtract_fusion
  (452 shorter events, 238.4 us)
Async XLA Ops:
  7.2 127.8 %all-gather.11.cloned.1.call-start = ((), (), s32[]{:S(2)}) async-start(), calls=%async_computation.14 | async-start | bytes 3932160 | tf_op jit(solution)/shard_map/all_gather | solution.py:467
  39.6 73.8 %all-to-all-start.1 = ((bf16[8,64,1408]{2,1,0:T(8,128)(2,1)}), bf16[8,64,1408]{2,1,0:T(8,128)(2,1)S(1)}, u32[]{:S(2)}, u32[]{:S(2)}) async-start(bf16[8,64,1408]{2,1,0:T(8,128)(2,1)} %reshape.197), calls=%async_computation.1 | async-start | bytes 2883584 | tf_op jit(solution)/shard_map/all_to_all | solution.py:464
  43.2 159.8 %all-gather.7.cloned.1.call-start = ((), (), s32[]{:S(2)}) async-start(), calls=%async_computation.8 | async-start | bytes 1310720 | tf_op jit(solution)/shard_map/all_gather | solution.py:471
  45.0 256.7 %all-gather.13.cloned.1.call-start = ((), (), s32[]{:S(2)}) async-start(), calls=%async_computation.15 | async-start | bytes 7208960 | tf_op jit(solution)/shard_map/all_gather | solution.py:467
  45.6 16.9 %collective-permute-start.1 = (bf16[7,2048]{1,0:T(8,128)(2,1)S(1)}, bf16[7,2048]{1,0:T(8,128)(2,1)S(1)}, u32[]{:S(2)}, u32[]{:S(2)}) collective-permute-start(bf16[7,2048]{1,0:T(8,128)(2,1)S(1)} %add.361), channel_id=1, source_target_pairs={{0,8},{4,12},{8,0},{12,4},{16,24},{20,28},{24,16},{28,20},{1,9},{5... | collective-permute-start | bytes 86024 | tf_op jit(solution)/shard_map/ppermute | solution.py:69
  82.1 15.1 %collective-permute-start.8 = (bf16[128,2048]{1,0:T(8,128)(2,1)}, bf16[128,2048]{1,0:T(8,128)(2,1)}, u32[]{:S(2)}, u32[]{:S(2)}) collective-permute-start(bf16[128,2048]{1,0:T(8,128)(2,1)} %get-tuple-element.100), channel_id=1, source_target_pairs={{0,16},{4,20},{8,24},{12,28},{16,0},{20,4},{24,8},{28,12},{1,17},{... | collective-permute-start | bytes 1572872 | tf_op jit(solution)/shard_map/ppermute | solution.py:69
  83.4 15.1 %collective-permute-start.5 = (bf16[128,2048]{1,0:T(8,128)(2,1)}, bf16[128,2048]{1,0:T(8,128)(2,1)}, u32[]{:S(2)}, u32[]{:S(2)}) collective-permute-start(bf16[128,2048]{1,0:T(8,128)(2,1)} %get-tuple-element.101), channel_id=1, source_target_pairs={{0,8},{4,12},{8,0},{12,4},{16,24},{20,28},{24,16},{28,20},{1,9},{5... | collective-permute-start | bytes 1572872 | tf_op jit(solution)/shard_map/ppermute | solution.py:69
  86.1 23.7 %collective-permute-start.6 = (bf16[128,2048]{1,0:T(8,128)(2,1)}, bf16[128,2048]{1,0:T(8,128)(2,1)}, u32[]{:S(2)}, u32[]{:S(2)}) collective-permute-start(bf16[128,2048]{1,0:T(8,128)(2,1)} %get-tuple-element.100), channel_id=1, source_target_pairs={{0,8},{4,12},{8,0},{12,4},{16,24},{20,28},{24,16},{28,20},{1,9},{5... | collective-permute-start | bytes 1572872 | tf_op jit(solution)/shard_map/ppermute | solution.py:69
  91.9 20.6 %collective-permute-start.7 = (bf16[128,2048]{1,0:T(8,128)(2,1)}, bf16[128,2048]{1,0:T(8,128)(2,1)S(1)}, u32[]{:S(2)}, u32[]{:S(2)}) collective-permute-start(bf16[128,2048]{1,0:T(8,128)(2,1)} %get-tuple-element.101), channel_id=1, source_target_pairs={{0,16},{4,20},{8,24},{12,28},{16,0},{20,4},{24,8},{28,12},{1,17},{... | collective-permute-start | bytes 1572872 | tf_op jit(solution)/shard_map/ppermute | solution.py:69
  92.7 33.6 %collective-permute-start.11 = (bf16[256,2048]{1,0:T(8,128)(2,1)}, bf16[256,2048]{1,0:T(8,128)(2,1)S(1)}, u32[]{:S(2)}, u32[]{:S(2)}) collective-permute-start(bf16[256,2048]{1,0:T(8,128)(2,1)} %copy-done.20), channel_id=1, source_target_pairs={{0,4},{4,0},{8,12},{12,8},{16,20},{20,16},{24,28},{28,24},{1,5},{5... | collective-permute-start | bytes 3145736 | tf_op jit(solution)/shard_map/ppermute | solution.py:69
  97.2 34.2 %collective-permute-start.15 = (bf16[128,2048]{1,0:T(8,128)(2,1)}, bf16[128,2048]{1,0:T(8,128)(2,1)}, u32[]{:S(2)}, u32[]{:S(2)}) collective-permute-start(bf16[128,2048]{1,0:T(8,128)(2,1)} %collective-permute-done.8), channel_id=1, source_target_pairs={{0,4},{4,0},{8,12},{12,8},{16,20},{20,16},{24,28},{28,24},{1,5},{5... | collective-permute-start | bytes 1572872 | tf_op jit(solution)/shard_map/ppermute | solution.py:69
  98.5 25.4 %collective-permute-start.10 = (bf16[128,2048]{1,0:T(8,128)(2,1)}, bf16[128,2048]{1,0:T(8,128)(2,1)}, u32[]{:S(2)}, u32[]{:S(2)}) collective-permute-start(bf16[128,2048]{1,0:T(8,128)(2,1)} %collective-permute-done.8), channel_id=1, source_target_pairs={{0,8},{4,12},{8,0},{12,4},{16,24},{20,28},{24,16},{28,20},{1,9},{5... | collective-permute-start | bytes 1572872 | tf_op jit(solution)/shard_map/ppermute | solution.py:69
  112.5 16.2 %collective-permute-start.13 = (bf16[128,2048]{1,0:T(8,128)(2,1)}, bf16[128,2048]{1,0:T(8,128)(2,1)}, u32[]{:S(2)}, u32[]{:S(2)}) collective-permute-start(bf16[128,2048]{1,0:T(8,128)(2,1)} %collective-permute-done.6), channel_id=1, source_target_pairs={{0,4},{4,0},{8,12},{12,8},{16,20},{20,16},{24,28},{28,24},{1,5},{5... | collective-permute-start | bytes 1572872 | tf_op jit(solution)/shard_map/ppermute | solution.py:69
  114.5 261.4 %all-gather.9.cloned.1.call-start = ((), (), s32[]{:S(2)}) async-start(), calls=%async_computation.9 | async-start | bytes 3604480 | tf_op jit(solution)/shard_map/all_gather | solution.py:474
  207.8 36.2 %collective-permute-start.18 = (bf16[1024,2048]{1,0:T(8,128)(2,1)}, bf16[1024,2048]{1,0:T(8,128)(2,1)}, u32[]{:S(2)}, u32[]{:S(2)}) collective-permute-start(bf16[1024,2048]{1,0:T(8,128)(2,1)} %convolution_convert_fusion.2), channel_id=1, source_target_pairs={{0,4},{4,0},{8,12},{12,8},{16,20},{20,16},{24,28},{28,24},{1,5},{5... | collective-permute-start | bytes 12582920 | tf_op jit(solution)/shard_map/ppermute | solution.py:69
  208.9 15.0 %collective-permute-start.48 = (bf16[128,2048]{1,0:T(8,128)(2,1)}, bf16[128,2048]{1,0:T(8,128)(2,1)}, u32[]{:S(2)}, u32[]{:S(2)}) collective-permute-start(bf16[128,2048]{1,0:T(8,128)(2,1)} %get-tuple-element.96), channel_id=1, source_target_pairs={{0,16},{4,20},{8,24},{12,28},{16,0},{20,4},{24,8},{28,12},{1,17},{... | collective-permute-start | bytes 1572872 | tf_op jit(solution)/shard_map/ppermute | solution.py:69
  209.8 15.1 %collective-permute-start.45 = (bf16[128,2048]{1,0:T(8,128)(2,1)}, bf16[128,2048]{1,0:T(8,128)(2,1)}, u32[]{:S(2)}, u32[]{:S(2)}) collective-permute-start(bf16[128,2048]{1,0:T(8,128)(2,1)} %get-tuple-element.97), channel_id=1, source_target_pairs={{0,8},{4,12},{8,0},{12,4},{16,24},{20,28},{24,16},{28,20},{1,9},{5... | collective-permute-start | bytes 1572872 | tf_op jit(solution)/shard_map/ppermute | solution.py:69
  211.4 24.0 %collective-permute-start.46 = (bf16[128,2048]{1,0:T(8,128)(2,1)}, bf16[128,2048]{1,0:T(8,128)(2,1)}, u32[]{:S(2)}, u32[]{:S(2)}) collective-permute-start(bf16[128,2048]{1,0:T(8,128)(2,1)} %get-tuple-element.96), channel_id=1, source_target_pairs={{0,8},{4,12},{8,0},{12,4},{16,24},{20,28},{24,16},{28,20},{1,9},{5... | collective-permute-start | bytes 1572872 | tf_op jit(solution)/shard_map/ppermute | solution.py:69
  211.8 27.0 %collective-permute-start.47 = (bf16[128,2048]{1,0:T(8,128)(2,1)}, bf16[128,2048]{1,0:T(8,128)(2,1)}, u32[]{:S(2)}, u32[]{:S(2)}) collective-permute-start(bf16[128,2048]{1,0:T(8,128)(2,1)} %get-tuple-element.97), channel_id=1, source_target_pairs={{0,16},{4,20},{8,24},{12,28},{16,0},{20,4},{24,8},{28,12},{1,17},{... | collective-permute-start | bytes 1572872 | tf_op jit(solution)/shard_map/ppermute | solution.py:69
  214.0 498.4 %reduce-scatter.11.cloned.1.call-start = ((), (), s32[]{:S(2)}) async-start(), calls=%async_computation.13 | async-start | bytes 3604480 | tf_op jit(solution)/shard_map/reduce_scatter | solution.py:504
  224.0 32.1 %collective-permute-start.51 = (bf16[256,2048]{1,0:T(8,128)(2,1)S(1)}, bf16[256,2048]{1,0:T(8,128)(2,1)S(1)}, u32[]{:S(2)}, u32[]{:S(2)}) collective-permute-start(bf16[256,2048]{1,0:T(8,128)(2,1)S(1)} %bitcast.143), channel_id=1, source_target_pairs={{0,4},{4,0},{8,12},{12,8},{16,20},{20,16},{24,28},{28,24},{1,5},{5... | collective-permute-start | bytes 3145736 | tf_op jit(solution)/shard_map/ppermute | solution.py:69
  224.9 71.9 %collective-permute-start.55 = (bf16[128,2048]{1,0:T(8,128)(2,1)}, bf16[128,2048]{1,0:T(8,128)(2,1)S(1)}, u32[]{:S(2)}, u32[]{:S(2)}) collective-permute-start(bf16[128,2048]{1,0:T(8,128)(2,1)} %collective-permute-done.48), channel_id=1, source_target_pairs={{0,4},{4,0},{8,12},{12,8},{16,20},{20,16},{24,28},{28,24},{1,5},{5... | collective-permute-start | bytes 1572872 | tf_op jit(solution)/shard_map/ppermute | solution.py:69
  235.3 19.9 %collective-permute-start.50 = (bf16[128,2048]{1,0:T(8,128)(2,1)}, bf16[128,2048]{1,0:T(8,128)(2,1)S(1)}, u32[]{:S(2)}, u32[]{:S(2)}) collective-permute-start(bf16[128,2048]{1,0:T(8,128)(2,1)} %collective-permute-done.48), channel_id=1, source_target_pairs={{0,8},{4,12},{8,0},{12,4},{16,24},{20,28},{24,16},{28,20},{1,9},{5... | collective-permute-start | bytes 1572872 | tf_op jit(solution)/shard_map/ppermute | solution.py:69
  238.8 15.1 %collective-permute-start.49 = (bf16[128,2048]{1,0:T(8,128)(2,1)}, bf16[128,2048]{1,0:T(8,128)(2,1)S(1)}, u32[]{:S(2)}, u32[]{:S(2)}) collective-permute-start(bf16[128,2048]{1,0:T(8,128)(2,1)} %collective-permute-done.45), channel_id=1, source_target_pairs={{0,16},{4,20},{8,24},{12,28},{16,0},{20,4},{24,8},{28,12},{1,17},{... | collective-permute-start | bytes 1572872 | tf_op jit(solution)/shard_map/ppermute | solution.py:69
  247.7 15.4 %collective-permute-start.22 = (bf16[128,2048]{1,0:T(8,128)(2,1)S(1)}, bf16[128,2048]{1,0:T(8,128)(2,1)S(1)}, u32[]{:S(2)}, u32[]{:S(2)}) collective-permute-start(bf16[128,2048]{1,0:T(8,128)(2,1)S(1)} %get-tuple-element.91), channel_id=1, source_target_pairs={{0,16},{4,20},{8,24},{12,28},{16,0},{20,4},{24,8},{28,12},{1,17},{... | collective-permute-start | bytes 1572872 | tf_op jit(solution)/shard_map/ppermute | solution.py:69
  268.2 22.3 %collective-permute-start.24 = (bf16[128,2048]{1,0:T(8,128)(2,1)S(1)}, bf16[128,2048]{1,0:T(8,128)(2,1)S(1)}, u32[]{:S(2)}, u32[]{:S(2)}) collective-permute-start(bf16[128,2048]{1,0:T(8,128)(2,1)S(1)} %get-tuple-element.90), channel_id=1, source_target_pairs={{0,16},{4,20},{8,24},{12,28},{16,0},{20,4},{24,8},{28,12},{1,17},{... | collective-permute-start | bytes 1572872 | tf_op jit(solution)/shard_map/ppermute | solution.py:69
  269.0 21.5 %collective-permute-start.23 = (bf16[128,2048]{1,0:T(8,128)(2,1)S(1)}, bf16[128,2048]{1,0:T(8,128)(2,1)S(1)}, u32[]{:S(2)}, u32[]{:S(2)}) collective-permute-start(bf16[128,2048]{1,0:T(8,128)(2,1)S(1)} %get-tuple-element.76), channel_id=1, source_target_pairs={{0,8},{4,12},{8,0},{12,4},{16,24},{20,28},{24,16},{28,20},{1,9},{5... | collective-permute-start | bytes 1572872 | tf_op jit(solution)/shard_map/ppermute | solution.py:69
  278.9 22.0 %collective-permute-start.57 = (bf16[128,2048]{1,0:T(8,128)(2,1)S(1)}, bf16[128,2048]{1,0:T(8,128)(2,1)S(1)}, u32[]{:S(2)}, u32[]{:S(2)}) collective-permute-start(bf16[128,2048]{1,0:T(8,128)(2,1)S(1)} %collective-permute-done.50), channel_id=1, source_target_pairs={{0,4},{4,0},{8,12},{12,8},{16,20},{20,16},{24,28},{28,24},{1,5},{5... | collective-permute-start | bytes 1572872 | tf_op jit(solution)/shard_map/ppermute | solution.py:69
  280.1 19.2 %collective-permute-start.56 = (bf16[128,2048]{1,0:T(8,128)(2,1)S(1)}, bf16[128,2048]{1,0:T(8,128)(2,1)S(1)}, u32[]{:S(2)}, u32[]{:S(2)}) collective-permute-start(bf16[128,2048]{1,0:T(8,128)(2,1)S(1)} %collective-permute-done.49), channel_id=1, source_target_pairs={{0,4},{4,0},{8,12},{12,8},{16,20},{20,16},{24,28},{28,24},{1,5},{5... | collective-permute-start | bytes 1572872 | tf_op jit(solution)/shard_map/ppermute | solution.py:69
  295.1 37.6 %collective-permute-start.28 = (bf16[128,2048]{1,0:T(8,128)(2,1)}, bf16[128,2048]{1,0:T(8,128)(2,1)}, u32[]{:S(2)}, u32[]{:S(2)}) collective-permute-start(bf16[128,2048]{1,0:T(8,128)(2,1)} %get-tuple-element.98), channel_id=1, source_target_pairs={{0,16},{4,20},{8,24},{12,28},{16,0},{20,4},{24,8},{28,12},{1,17},{... | collective-permute-start | bytes 1572872 | tf_op jit(solution)/shard_map/ppermute | solution.py:69
  296.4 36.9 %collective-permute-start.25 = (bf16[128,2048]{1,0:T(8,128)(2,1)}, bf16[128,2048]{1,0:T(8,128)(2,1)}, u32[]{:S(2)}, u32[]{:S(2)}) collective-permute-start(bf16[128,2048]{1,0:T(8,128)(2,1)} %get-tuple-element.99), channel_id=1, source_target_pairs={{0,8},{4,12},{8,0},{12,4},{16,24},{20,28},{24,16},{28,20},{1,9},{5... | collective-permute-start | bytes 1572872 | tf_op jit(solution)/shard_map/ppermute | solution.py:69
  297.6 38.4 %collective-permute-start.26 = (bf16[128,2048]{1,0:T(8,128)(2,1)}, bf16[128,2048]{1,0:T(8,128)(2,1)}, u32[]{:S(2)}, u32[]{:S(2)}) collective-permute-start(bf16[128,2048]{1,0:T(8,128)(2,1)} %get-tuple-element.98), channel_id=1, source_target_pairs={{0,8},{4,12},{8,0},{12,4},{16,24},{20,28},{24,16},{28,20},{1,9},{5... | collective-permute-start | bytes 1572872 | tf_op jit(solution)/shard_map/ppermute | solution.py:69
  300.1 39.0 %collective-permute-start.27 = (bf16[128,2048]{1,0:T(8,128)(2,1)}, bf16[128,2048]{1,0:T(8,128)(2,1)}, u32[]{:S(2)}, u32[]{:S(2)}) collective-permute-start(bf16[128,2048]{1,0:T(8,128)(2,1)} %get-tuple-element.99), channel_id=1, source_target_pairs={{0,16},{4,20},{8,24},{12,28},{16,0},{20,4},{24,8},{28,12},{1,17},{... | collective-permute-start | bytes 1572872 | tf_op jit(solution)/shard_map/ppermute | solution.py:69
  332.7 19.0 %collective-permute-start.31 = (bf16[256,2048]{1,0:T(8,128)(2,1)S(1)}, bf16[256,2048]{1,0:T(8,128)(2,1)S(1)}, u32[]{:S(2)}, u32[]{:S(2)}) collective-permute-start(bf16[256,2048]{1,0:T(8,128)(2,1)S(1)} %copy-done.22), channel_id=1, source_target_pairs={{0,4},{4,0},{8,12},{12,8},{16,20},{20,16},{24,28},{28,24},{1,5},{5... | collective-permute-start | bytes 3145736 | tf_op jit(solution)/shard_map/ppermute | solution.py:69
  332.8 23.0 %collective-permute-start.35 = (bf16[128,2048]{1,0:T(8,128)(2,1)}, bf16[128,2048]{1,0:T(8,128)(2,1)S(1)}, u32[]{:S(2)}, u32[]{:S(2)}) collective-permute-start(bf16[128,2048]{1,0:T(8,128)(2,1)} %collective-permute-done.28), channel_id=1, source_target_pairs={{0,4},{4,0},{8,12},{12,8},{16,20},{20,16},{24,28},{28,24},{1,5},{5... | collective-permute-start | bytes 1572872 | tf_op jit(solution)/shard_map/ppermute | solution.py:69
  333.3 17.1 %collective-permute-start.30 = (bf16[128,2048]{1,0:T(8,128)(2,1)}, bf16[128,2048]{1,0:T(8,128)(2,1)S(1)}, u32[]{:S(2)}, u32[]{:S(2)}) collective-permute-start(bf16[128,2048]{1,0:T(8,128)(2,1)} %collective-permute-done.28), channel_id=1, source_target_pairs={{0,8},{4,12},{8,0},{12,4},{16,24},{20,28},{24,16},{28,20},{1,9},{5... | collective-permute-start | bytes 1572872 | tf_op jit(solution)/shard_map/ppermute | solution.py:69
  339.1 15.0 %collective-permute-start.33 = (bf16[128,2048]{1,0:T(8,128)(2,1)}, bf16[128,2048]{1,0:T(8,128)(2,1)S(1)}, u32[]{:S(2)}, u32[]{:S(2)}) collective-permute-start(bf16[128,2048]{1,0:T(8,128)(2,1)} %collective-permute-done.26), channel_id=1, source_target_pairs={{0,4},{4,0},{8,12},{12,8},{16,20},{20,16},{24,28},{28,24},{1,5},{5... | collective-permute-start | bytes 1572872 | tf_op jit(solution)/shard_map/ppermute | solution.py:69
  398.6 21.5 %collective-permute-start.38 = (bf16[1024,2048]{1,0:T(8,128)(2,1)}, bf16[1024,2048]{1,0:T(8,128)(2,1)}, u32[]{:S(2)}, u32[]{:S(2)}) collective-permute-start(bf16[1024,2048]{1,0:T(8,128)(2,1)} %convolution_convert_fusion.4), channel_id=1, source_target_pairs={{0,4},{4,0},{8,12},{12,8},{16,20},{20,16},{24,28},{28,24},{1,5},{5... | collective-permute-start | bytes 12582920 | tf_op jit(solution)/shard_map/ppermute | solution.py:69
  409.1 23.3 %collective-permute-start.58 = (bf16[1024,2048]{1,0:T(8,128)(2,1)}, bf16[1024,2048]{1,0:T(8,128)(2,1)}, u32[]{:S(2)}, u32[]{:S(2)}) collective-permute-start(bf16[1024,2048]{1,0:T(8,128)(2,1)} %convolution_convert_fusion.1), channel_id=1, source_target_pairs={{0,4},{4,0},{8,12},{12,8},{16,20},{20,16},{24,28},{28,24},{1,5},{5... | collective-permute-start | bytes 12582920 | tf_op jit(solution)/shard_map/ppermute | solution.py:69
  420.1 319.1 %reduce-scatter.7.cloned.1.call-start = ((), (), s32[]{:S(2)}) async-start(), calls=%async_computation.11 | async-start | bytes 1310720 | tf_op jit(solution)/shard_map/reduce_scatter | solution.py:504
  428.4 51.5 %collective-permute-start.39 = (bf16[128,2048]{1,0:T(8,128)(2,1)S(1)}, bf16[128,2048]{1,0:T(8,128)(2,1)S(1)}, u32[]{:S(2)}, u32[]{:S(2)}) collective-permute-start(bf16[128,2048]{1,0:T(8,128)(2,1)S(1)} %get-tuple-element.85), channel_id=1, source_target_pairs={{0,8},{4,12},{8,0},{12,4},{16,24},{20,28},{24,16},{28,20},{1,9},{5... | collective-permute-start | bytes 1572872 | tf_op jit(solution)/shard_map/ppermute | solution.py:69
  430.0 52.7 %collective-permute-start.44 = (bf16[128,2048]{1,0:T(8,128)(2,1)}, bf16[128,2048]{1,0:T(8,128)(2,1)S(1)}, u32[]{:S(2)}, u32[]{:S(2)}) collective-permute-start(bf16[128,2048]{1,0:T(8,128)(2,1)} %get-tuple-element.86), channel_id=1, source_target_pairs={{0,16},{4,20},{8,24},{12,28},{16,0},{20,4},{24,8},{28,12},{1,17},{... | collective-permute-start | bytes 1572872 | tf_op jit(solution)/shard_map/ppermute | solution.py:69
  431.2 24.3 %collective-permute-start.42 = (bf16[128,2048]{1,0:T(8,128)(2,1)}, bf16[128,2048]{1,0:T(8,128)(2,1)S(1)}, u32[]{:S(2)}, u32[]{:S(2)}) collective-permute-start(bf16[128,2048]{1,0:T(8,128)(2,1)} %get-tuple-element.87), channel_id=1, source_target_pairs={{0,16},{4,20},{8,24},{12,28},{16,0},{20,4},{24,8},{28,12},{1,17},{... | collective-permute-start | bytes 1572872 | tf_op jit(solution)/shard_map/ppermute | solution.py:69
  432.0 24.7 %collective-permute-start.40 = (bf16[128,2048]{1,0:T(8,128)(2,1)S(1)}, bf16[128,2048]{1,0:T(8,128)(2,1)}, u32[]{:S(2)}, u32[]{:S(2)}) collective-permute-start(bf16[128,2048]{1,0:T(8,128)(2,1)S(1)} %get-tuple-element.88), channel_id=1, source_target_pairs={{0,8},{4,12},{8,0},{12,4},{16,24},{20,28},{24,16},{28,20},{1,9},{5... | collective-permute-start | bytes 1572872 | tf_op jit(solution)/shard_map/ppermute | solution.py:69
  445.5 45.9 %collective-permute-start.59 = (bf16[128,2048]{1,0:T(8,128)(2,1)S(1)}, bf16[128,2048]{1,0:T(8,128)(2,1)S(1)}, u32[]{:S(2)}, u32[]{:S(2)}) collective-permute-start(bf16[128,2048]{1,0:T(8,128)(2,1)S(1)} %get-tuple-element.81), channel_id=1, source_target_pairs={{0,8},{4,12},{8,0},{12,4},{16,24},{20,28},{24,16},{28,20},{1,9},{5... | collective-permute-start | bytes 1572872 | tf_op jit(solution)/shard_map/ppermute | solution.py:69
  456.7 19.7 %collective-permute-start.60 = (bf16[128,2048]{1,0:T(8,128)(2,1)S(1)}, bf16[128,2048]{1,0:T(8,128)(2,1)S(1)}, u32[]{:S(2)}, u32[]{:S(2)}) collective-permute-start(bf16[128,2048]{1,0:T(8,128)(2,1)S(1)} %get-tuple-element.84), channel_id=1, source_target_pairs={{0,8},{4,12},{8,0},{12,4},{16,24},{20,28},{24,16},{28,20},{1,9},{5... | collective-permute-start | bytes 1572872 | tf_op jit(solution)/shard_map/ppermute | solution.py:69
  479.9 24.8 %collective-permute-start.64 = (bf16[128,2048]{1,0:T(8,128)(2,1)S(1)}, bf16[128,2048]{1,0:T(8,128)(2,1)S(1)}, u32[]{:S(2)}, u32[]{:S(2)}) collective-permute-start(bf16[128,2048]{1,0:T(8,128)(2,1)S(1)} %get-tuple-element.82), channel_id=1, source_target_pairs={{0,16},{4,20},{8,24},{12,28},{16,0},{20,4},{24,8},{28,12},{1,17},{... | collective-permute-start | bytes 1572872 | tf_op jit(solution)/shard_map/ppermute | solution.py:69
  481.4 23.2 %collective-permute-start.61 = (bf16[128,2048]{1,0:T(8,128)(2,1)S(1)}, bf16[128,2048]{1,0:T(8,128)(2,1)S(1)}, u32[]{:S(2)}, u32[]{:S(2)}) collective-permute-start(bf16[128,2048]{1,0:T(8,128)(2,1)S(1)} %get-tuple-element.71), channel_id=1, source_target_pairs={{0,16},{4,20},{8,24},{12,28},{16,0},{20,4},{24,8},{28,12},{1,17},{... | collective-permute-start | bytes 1572872 | tf_op jit(solution)/shard_map/ppermute | solution.py:69
  482.8 22.0 %collective-permute-start.63 = (bf16[128,2048]{1,0:T(8,128)(2,1)S(1)}, bf16[128,2048]{1,0:T(8,128)(2,1)S(1)}, u32[]{:S(2)}, u32[]{:S(2)}) collective-permute-start(bf16[128,2048]{1,0:T(8,128)(2,1)S(1)} %get-tuple-element.72), channel_id=1, source_target_pairs={{0,8},{4,12},{8,0},{12,4},{16,24},{20,28},{24,16},{28,20},{1,9},{5... | collective-permute-start | bytes 1572872 | tf_op jit(solution)/shard_map/ppermute | solution.py:69
  510.6 14.9 %collective-permute-start.68 = (bf16[128,2048]{1,0:T(8,128)(2,1)S(1)}, bf16[128,2048]{1,0:T(8,128)(2,1)S(1)}, u32[]{:S(2)}, u32[]{:S(2)}) collective-permute-start(bf16[128,2048]{1,0:T(8,128)(2,1)S(1)} %get-tuple-element.94), channel_id=1, source_target_pairs={{0,16},{4,20},{8,24},{12,28},{16,0},{20,4},{24,8},{28,12},{1,17},{... | collective-permute-start | bytes 1572872 | tf_op jit(solution)/shard_map/ppermute | solution.py:69
  512.3 25.7 %collective-permute-start.66 = (bf16[128,2048]{1,0:T(8,128)(2,1)S(1)}, bf16[128,2048]{1,0:T(8,128)(2,1)S(1)}, u32[]{:S(2)}, u32[]{:S(2)}) collective-permute-start(bf16[128,2048]{1,0:T(8,128)(2,1)S(1)} %get-tuple-element.94), channel_id=1, source_target_pairs={{0,8},{4,12},{8,0},{12,4},{16,24},{20,28},{24,16},{28,20},{1,9},{5... | collective-permute-start | bytes 1572872 | tf_op jit(solution)/shard_map/ppermute | solution.py:69
  513.9 24.9 %collective-permute-start.67 = (bf16[128,2048]{1,0:T(8,128)(2,1)S(1)}, bf16[128,2048]{1,0:T(8,128)(2,1)S(1)}, u32[]{:S(2)}, u32[]{:S(2)}) collective-permute-start(bf16[128,2048]{1,0:T(8,128)(2,1)S(1)} %get-tuple-element.95), channel_id=1, source_target_pairs={{0,16},{4,20},{8,24},{12,28},{16,0},{20,4},{24,8},{28,12},{1,17},{... | collective-permute-start | bytes 1572872 | tf_op jit(solution)/shard_map/ppermute | solution.py:69
  514.7 33.2 %collective-permute-start.71 = (bf16[256,2048]{1,0:T(8,128)(2,1)S(1)}, bf16[256,2048]{1,0:T(8,128)(2,1)S(1)}, u32[]{:S(2)}, u32[]{:S(2)}) collective-permute-start(bf16[256,2048]{1,0:T(8,128)(2,1)S(1)} %get-tuple-element.57), channel_id=1, source_target_pairs={{0,4},{4,0},{8,12},{12,8},{16,20},{20,16},{24,28},{28,24},{1,5},{5... | collective-permute-start | bytes 3145736 | tf_op jit(solution)/shard_map/ppermute | solution.py:69
  525.5 24.4 %collective-permute-start.75 = (bf16[128,2048]{1,0:T(8,128)(2,1)S(1)}, bf16[128,2048]{1,0:T(8,128)(2,1)S(1)}, u32[]{:S(2)}, u32[]{:S(2)}) collective-permute-start(bf16[128,2048]{1,0:T(8,128)(2,1)S(1)} %collective-permute-done.68), channel_id=1, source_target_pairs={{0,4},{4,0},{8,12},{12,8},{16,20},{20,16},{24,28},{28,24},{1,5},{5... | collective-permute-start | bytes 1572872 | tf_op jit(solution)/shard_map/ppermute | solution.py:69
  526.8 20.5 %collective-permute-start.70 = (bf16[128,2048]{1,0:T(8,128)(2,1)S(1)}, bf16[128,2048]{1,0:T(8,128)(2,1)S(1)}, u32[]{:S(2)}, u32[]{:S(2)}) collective-permute-start(bf16[128,2048]{1,0:T(8,128)(2,1)S(1)} %collective-permute-done.68), channel_id=1, source_target_pairs={{0,8},{4,12},{8,0},{12,4},{16,24},{20,28},{24,16},{28,20},{1,9},{5... | collective-permute-start | bytes 1572872 | tf_op jit(solution)/shard_map/ppermute | solution.py:69
  558.1 182.8 %reduce-scatter.9.cloned.1.call-start = ((), (), s32[]{:S(2)}) async-start(), calls=%async_computation.12 | async-start | bytes 7208960 | tf_op jit(solution)/shard_map/reduce_scatter | solution.py:509
  615.1 168.9 %reduce-scatter.5.cloned.1.call-start = ((), (), s32[]{:S(2)}) async-start(), calls=%async_computation.10 | async-start | bytes 3932160 | tf_op jit(solution)/shard_map/reduce_scatter | solution.py:509
  696.2 25.0 %collective-permute-start.79 = (bf16[128,2048]{1,0:T(8,128)(2,1)S(1)}, bf16[128,2048]{1,0:T(8,128)(2,1)S(1)}, u32[]{:S(2)}, u32[]{:S(2)}) collective-permute-start(bf16[128,2048]{1,0:T(8,128)(2,1)S(1)} %get-tuple-element.77), channel_id=1, source_target_pairs={{0,8},{4,12},{8,0},{12,4},{16,24},{20,28},{24,16},{28,20},{1,9},{5... | collective-permute-start | bytes 1572872 | tf_op jit(solution)/shard_map/ppermute | solution.py:69
  711.3 15.1 %collective-permute-start.81 = (bf16[128,2048]{1,0:T(8,128)(2,1)}, bf16[128,2048]{1,0:T(8,128)(2,1)S(1)}, u32[]{:S(2)}, u32[]{:S(2)}) collective-permute-start(bf16[128,2048]{1,0:T(8,128)(2,1)} %get-tuple-element.69), channel_id=1, source_target_pairs={{0,16},{4,20},{8,24},{12,28},{16,0},{20,4},{24,8},{28,12},{1,17},{... | collective-permute-start | bytes 1572872 | tf_op jit(solution)/shard_map/ppermute | solution.py:69
  716.9 18.0 %collective-permute-start.84 = (bf16[128,2048]{1,0:T(8,128)(2,1)S(1)}, bf16[128,2048]{1,0:T(8,128)(2,1)S(1)}, u32[]{:S(2)}, u32[]{:S(2)}) collective-permute-start(bf16[128,2048]{1,0:T(8,128)(2,1)S(1)} %get-tuple-element.78), channel_id=1, source_target_pairs={{0,16},{4,20},{8,24},{12,28},{16,0},{20,4},{24,8},{28,12},{1,17},{... | collective-permute-start | bytes 1572872 | tf_op jit(solution)/shard_map/ppermute | solution.py:69
  718.0 17.0 %collective-permute-start.83 = (bf16[128,2048]{1,0:T(8,128)(2,1)}, bf16[128,2048]{1,0:T(8,128)(2,1)S(1)}, u32[]{:S(2)}, u32[]{:S(2)}) collective-permute-start(bf16[128,2048]{1,0:T(8,128)(2,1)} %get-tuple-element.70), channel_id=1, source_target_pairs={{0,8},{4,12},{8,0},{12,4},{16,24},{20,28},{24,16},{28,20},{1,9},{5... | collective-permute-start | bytes 1572872 | tf_op jit(solution)/shard_map/ppermute | solution.py:69
  741.0 68.2 %all-to-all-start.3 = ((bf16[8,64,1408]{2,1,0:T(8,128)(2,1)}), bf16[8,64,1408]{2,1,0:T(8,128)(2,1)}, u32[]{:S(2)}, u32[]{:S(2)}) async-start(bf16[8,64,1408]{2,1,0:T(8,128)(2,1)} %bitcast.152), calls=%async_computation.7 | async-start | bytes 2883584 | tf_op jit(solution)/shard_map/all_to_all | solution.py:516
  745.3 20.0 %collective-permute-start.86 = (f32[7,2048]{1,0:T(8,128)S(1)}, f32[7,2048]{1,0:T(8,128)S(1)}, u32[]{:S(2)}, u32[]{:S(2)}) collective-permute-start(f32[7,2048]{1,0:T(8,128)S(1)} %add.412), channel_id=1, source_target_pairs={{0,8},{4,12},{8,0},{12,4},{16,24},{20,28},{24,16},{28,20},{1,9},{5... | collective-permute-start | bytes 172040 | tf_op jit(solution)/shard_map/ppermute | solution.py:69
  809.2 32.3 %all-to-all-start.2 = ((bf16[8,64,768]{2,1,0:T(8,128)(2,1)}), bf16[8,64,768]{2,1,0:T(8,128)(2,1)}, u32[]{:S(2)}, u32[]{:S(2)}) async-start(bf16[8,64,768]{2,1,0:T(8,128)(2,1)} %bitcast.163), calls=%async_computation.6 | async-start | bytes 1572864 | tf_op jit(solution)/shard_map/all_to_all | solution.py:516
  (96 other events, 1019.4 us)
Sparse Core Ops, SparseCore 0:
  31.6 64.5 all-gather.10
  98.4 26.5 all-gather.6
  127.2 106.1 all-gather.12
  235.4 57.4 all-gather.8
  420.2 57.6 reduce-scatter.10
  558.3 27.5 reduce-scatter.6
  615.2 102.6 reduce-scatter.8
  720.3 62.4 reduce-scatter.4

commit v2 on v1

--- a/solution.py
+++ b/solution.py
@@ -30,6 +30,7 @@
 SCALE_LOG2 = SCALE * math.log2(math.e)
 VMEM_LIMIT = 52 * 1024 * 1024
 BF16 = jnp.bfloat16
+SHORT = pl.CostEstimate(flops=1000000, bytes_accessed=1000000, transcendentals=0)
 F32 = jnp.float32
 
 ORDER = (0, 2, 4, 6, 1, 3, 5, 7)
@@ -80,48 +81,189 @@
     return jnp.arange(size, dtype=jnp.int32)
 
 
-def gather_tokens(own):
-    if not cube():
-        return lax.all_gather(own, "ctx", axis=0, tiled=True)
-    half = own.shape[0] // 2
-    top, low = own[:half], own[half:]
+def tie(*values):
+    return lax.optimization_barrier(values)
+
+
+def window(begun, *others):
+    if not cube():
+        return (begun, *others)
+    tied = tie(*begun[-2:], *others)
+    return (begun[:-2] + tied[:2], *tied[2:])
+
+
+def gather_start(top, low):
+    if not cube():
+        return (lax.all_gather(jnp.concatenate([top, low]), "ctx", axis=0, tiled=True),)
     x_top = swap(top, 2)
     y_low = swap(low, 4)
-    x_low = swap(low, 2)
-    y_top = swap(top, 4)
-    d_top = swap(x_top, 4)
-    d_low = swap(y_low, 2)
-    first = jnp.concatenate([own, x_top, x_low, y_top, y_low, d_top, d_low], axis=0)
-    pieces = [own, x_top, x_low, y_top, y_low, d_top, d_low]
-    other = [swap(piece, 1) for piece in pieces]
-    return jnp.concatenate([first] + other, axis=0)
-
-
-def scatter_tokens(make):
+    c_top = swap(top, 1)
+    c_low = swap(low, 1)
+    c_top, c_low, top, low = tie(c_top, c_low, top, low)
+    return (top, low, c_top, c_low, x_top, y_low, swap(low, 2), swap(top, 4))
+
+
+def gather_far(begun):
+    if not cube():
+        return ()
+    return (swap(begun[4], 4), swap(begun[5], 2))
+
+
+def gather_near(begun):
+    top, low, c_top, c_low, x_top, y_low, x_low, y_top = begun
+    near = (x_top, x_low, y_top, y_low)
+    return (top, low, *near, c_top, c_low) + tuple(swap(piece, 1) for piece in near)
+
+
+def gather_late(far):
+    return far + tuple(swap(piece, 1) for piece in far)
+
+
+def gather_pieces(begun, far=None):
+    if not cube():
+        return begun
+    near = gather_near(begun)
+    late = gather_late(gather_far(begun) if far is None else far)
+    return near[:6] + late[:2] + near[6:] + late[2:]
+
+
+def chip_kernel(right_dim, left_ref, right_ref, other_ref, own, x_top, x_low, y_top, y_low, d_top, d_low):
+    total = dot(left_ref[...], right_ref[...], 1, right_dim) + other_ref[...].astype(F32)
+    low = total.astype(BF16)
+    half = BLOCK // 2
+
+    @pl.when(pl.program_id(0) == 0)
+    def _():
+        own[...] = low[:BLOCK]
+        x_top[...] = low[BLOCK : BLOCK + half]
+        x_low[...] = low[BLOCK + half :]
+
+    @pl.when(pl.program_id(0) == 1)
+    def _():
+        y_top[...] = low[:half]
+        y_low[...] = low[half:BLOCK]
+        d_top[...] = low[BLOCK : BLOCK + half]
+        d_low[...] = low[BLOCK + half :]
+
+
+def chip_sums(left, right, right_dim, other):
+    depth = left.shape[1]
+    half = BLOCK // 2
+    cuts = (BLOCK,) + (half,) * 6
+    return pl.pallas_call(
+        functools.partial(chip_kernel, right_dim),
+        grid=(2,),
+        out_shape=tuple(jax.ShapeDtypeStruct((cut, D), BF16) for cut in cuts),
+        in_specs=[
+            pl.BlockSpec((2 * BLOCK, depth), lambda i: (i, 0)),
+            pl.BlockSpec(right.shape, lambda i: (0, 0), pipeline_mode=pl.Buffered(1)),
+            pl.BlockSpec((2 * BLOCK, D), lambda i: (i, 0)),
+        ],
+        out_specs=tuple(pl.BlockSpec((cut, D), lambda i: (0, 0)) for cut in cuts),
+        compiler_params=pltpu.CompilerParams(vmem_limit_bytes=VMEM_LIMIT),
+        cost_estimate=SHORT,
+        name="chip_sums",
+    )(left, right, other)
+
+
+def scatter_away(left, right, right_dim):
+    if not cube():
+        return None
+    return swap(dot(left[4 * BLOCK :], right, 1, right_dim).astype(BF16), 1)
+
+
+def scatter_sums(left, right, right_dim, away):
+    if not cube():
+        part = dot(left, right, 1, right_dim).astype(BF16)
+        return (lax.psum_scatter(part, "ctx", scatter_dimension=0, tiled=True),)
+    return tuple(chip_sums(left, right, right_dim, away))
+
+
+def scatter_start(sums):
+    if not cube():
+        return sums
+    own, x_top, x_low, y_top, y_low, d_top, d_low = sums
+    return (own, x_low, y_top, swap(d_top, 2), swap(d_low, 4), swap(x_top, 2), swap(y_low, 4))
+
+
+def scatter_end(begun):
+    if not cube():
+        return begun
+    own, x_low, y_top, d_top, d_low, x_top, y_low = begun
+    x_low = swap((x_low.astype(F32) + d_low.astype(F32)).astype(BF16), 2)
+    y_top = swap((y_top.astype(F32) + d_top.astype(F32)).astype(BF16), 4)
+    return (own, x_top, y_top, x_low, y_low)
+
+
+def total_of(parts):
+    parts = [part.astype(F32) for part in parts]
+    if len(parts) == 1:
+        return parts[0]
+    own, x_top, y_top, x_low, y_low = parts
+    return own + jnp.concatenate([x_top + y_top, x_low + y_low], axis=0)
+
+
+def split_kernel(parts, size, width, w_ref, *refs):
+    rows = w_ref.shape[0]
+    out_ref = refs[-1]
+    for c in range(size):
+        for p in range(parts):
+            column = (p * size + c) * width
+            block = w_ref[:, column : column + width].astype(BF16)
+            out_ref[c, :rows, p * width : (p + 1) * width] = block
+        if len(refs) > 1:
+            out_ref[c, rows:, :] = refs[0][...]
+
+
+def join_kernel(parts, size, width, share_ref, out_ref):
+    for c in range(size):
+        for p in range(parts):
+            column = (p * size + c) * width
+            out_ref[:, column : column + width] = share_ref[c, :, p * width : (p + 1) * width]
+
+
+def relayout(kernel, values, shape, name):
+    return pl.pallas_call(
+        kernel,
+        out_shape=jax.ShapeDtypeStruct(shape, BF16),
+        in_specs=[pl.BlockSpec(memory_space=pltpu.VMEM)] * len(values),
+        out_specs=pl.BlockSpec(memory_space=pltpu.VMEM),
+        compiler_params=pltpu.CompilerParams(vmem_limit_bytes=VMEM_LIMIT),
+        cost_estimate=SHORT,
+        name=name,
+    )(*values)
+
+
+def split_columns(weight, parts, *below):
     size = lax.axis_size("ctx")
-    if not cube():
-        return lax.psum_scatter(
-            make(0, size * BLOCK).astype(BF16), "ctx", scatter_dimension=0, tiled=True
-        ).astype(F32)
-    half = BLOCK // 2
-    away = make(4 * BLOCK, 8 * BLOCK).astype(BF16)
-    near = make(0, 4 * BLOCK)
-    total = near + swap(away, 1).astype(F32)
-    own = total[:BLOCK]
-    x_part = total[BLOCK : 2 * BLOCK]
-    y_part = total[2 * BLOCK : 3 * BLOCK]
-    diag = total[3 * BLOCK :].astype(BF16)
-    d_top = swap(diag[:half], 2).astype(F32)
-    d_low = swap(diag[half:], 4).astype(F32)
-    x_top = swap(x_part[:half].astype(BF16), 2).astype(F32)
-    y_low = swap(y_part[half:].astype(BF16), 4).astype(F32)
-    x_low = swap((x_part[half:] + d_low).astype(BF16), 2).astype(F32)
-    y_top = swap((y_part[:half] + d_top).astype(BF16), 4).astype(F32)
-    return own + jnp.concatenate([x_top + y_top, x_low + y_low], axis=0)
-
-
-def sum_everywhere(value):
-    for axis in ("ctx", "fsdp"):
+    rows = weight.shape[0]
+    width = weight.shape[1] // (parts * size)
+    if not cube():
+        split = weight.astype(BF16).reshape(rows, parts, size, width)
+        split = split.transpose(2, 0, 1, 3).reshape(size, rows, parts * width)
+        below = [jnp.broadcast_to(value, (size, *value.shape)) for value in below]
+        return jnp.concatenate([split, *below], axis=1)
+    kernel = functools.partial(split_kernel, parts, size, width)
+    total = rows + sum(value.shape[0] for value in below)
+    return relayout(kernel, (weight, *below), (size, total, parts * width), "split_columns")
+
+
+def join_columns(share, parts):
+    size, rows, width = share.shape
+    width = width // parts
+    if not cube():
+        split = share.reshape(size, rows, parts, width)
+        return split.transpose(1, 2, 0, 3).reshape(rows, parts * size * width)
+    kernel = functools.partial(join_kernel, parts, size, width)
+    return relayout(kernel, (share,), (rows, parts * size * width), "join_columns")
+
+
+def exchange(split):
+    return lax.all_to_all(split, "ctx", 0, 0)
+
+
+def sum_everywhere(value, axes=("ctx", "fsdp")):
+    for axis in axes:
         bit = 1
         while bit < lax.axis_size(axis):
             value = value + swap(value, bit, axis)
@@ -159,6 +301,10 @@
     return value.astype(F32).T.astype(BF16)
 
 
+def fold(value):
+    return value.reshape(value.shape[0] // 8, 8, value.shape[1])
+
+
 def split_rows(pair):
     zero = jnp.zeros((HEAD_DIM, pair.shape[1]), pair.dtype)
     return (
@@ -174,11 +320,12 @@
 
 
 def attend_kernel(
-    pairs, blocks, inv_ref, proj_ref, bias_ref, cos_ref, sin_ref, q_ref, k_ref, v_ref, mix_ref, lse_ref, vt_ref
+    pairs, blocks, inv_ref, proj_ref, bias_ref, cos_ref, sin_ref, q_ref, k_ref, v_ref, mix_ref, lse_ref, vt_ref, s_ref
 ):
     prompt_blocks = blocks // 2
     wide = pairs * LANES
     lanes = [slice(p * LANES, (p + 1) * LANES) for p in range(pairs)]
+    count = 2 * pairs
 
     def prepare(code, carry):
         rows = aligned(inv_ref[code])
@@ -204,46 +351,50 @@
         for p in range(pairs):
             heads.extend(split_rows(transposed(q_ref[place, lanes[p]])))
 
-        def scores(h, at):
-            return dot(k_ref[at, lanes[h // 2]], heads[h], 1, 0) * SCALE_LOG2
-
-        def mixing(h, at, probs):
-            return dot(
-                vt_ref[h * HEAD_DIM : (h + 1) * HEAD_DIM, at], probs.astype(BF16), 1, 0
-            )
-
-        state = []
-        for h in range(2 * pairs):
-            logits = jnp.where(allowed, scores(h, place), MASKED)
-            top = jnp.max(logits, axis=0, keepdims=True)
-            probs = jnp.exp2(logits - top)
-            state.append((top, jnp.sum(probs, axis=0, keepdims=True), mixing(h, place, probs)))
+        def scores(slot, at, mask, tops):
+            fresh = []
+            for h in range(count):
+                logits = dot(k_ref[at, lanes[h // 2]], heads[h], 1, 0) * SCALE_LOG2
+                if mask is not None:
+                    logits = jnp.where(mask, logits, MASKED)
+                s_ref[h, aligned(slot), :] = logits
+                fresh.append(jnp.maximum(tops[h], jnp.max(fold(logits), axis=0)))
+            return tuple(fresh)
+
+        full = full_blocks(code, prompt_blocks)
+        tops = scores(full, place, allowed, (jnp.full((8, BLOCK), MASKED, F32),) * count)
+        tops = lax.fori_loop(
+            0,
+            full,
+            lambda index, tops: scores(
+                index, aligned(key_block(code, index, prompt_blocks)), None, tops
+            ),
+            tops,
+        )
+        tops = [jnp.max(top, axis=0, keepdims=True) for top in tops]
 
         def step(index, state):
-            at = aligned(key_block(code, index, prompt_blocks))
+            at = aligned(jnp.where(index == full, code, key_block(code, index, prompt_blocks)))
             fresh = []
-            for h in range(2 * pairs):
-                top, total, mixed = state[h]
-                logits = scores(h, at)
-                higher = jnp.maximum(top, jnp.max(logits, axis=0, keepdims=True))
-                probs = jnp.exp2(logits - higher)
-                fade = jnp.exp2(top - higher)
-                fresh.append(
-                    (
-                        higher,
-                        total * fade + jnp.sum(probs, axis=0, keepdims=True),
-                        mixed * fade + mixing(h, at, probs),
-                    )
+            for h in range(count):
+                total, mixed = state[h]
+                probs = jnp.exp2(s_ref[h, aligned(index), :] - tops[h])
+                total = total + jnp.sum(fold(probs), axis=0)
+                mixed = mixed + dot(
+                    vt_ref[h * HEAD_DIM : (h + 1) * HEAD_DIM, at], probs.astype(BF16), 1, 0
                 )
+                fresh.append((total, mixed))
             return tuple(fresh)
 
-        state = lax.fori_loop(0, full_blocks(code, prompt_blocks), step, tuple(state))
+        state = ((jnp.zeros((8, BLOCK), F32), jnp.zeros((HEAD_DIM, BLOCK), F32)),) * count
+        state = lax.fori_loop(0, full + 1, step, state)
         for p in range(pairs):
             both = []
             for h in (2 * p, 2 * p + 1):
-                top, total, mixed = state[h]
+                total, mixed = state[h]
+                total = jnp.sum(total, axis=0, keepdims=True)
                 both.append(mixed / total)
-                lse_ref[h : h + 1, place] = top + jnp.log2(total)
+                lse_ref[h : h + 1, place] = tops[h] + jnp.log2(total)
             mix_ref[rows, lanes[p]] = jnp.concatenate(both, axis=0).T.astype(BF16)
         return carry
 
@@ -260,13 +411,12 @@
         out_shape=(low, low, low, low, jax.ShapeDtypeStruct((2 * pairs, tokens), F32)),
         in_specs=[pl.BlockSpec(memory_space=pltpu.SMEM)] + [vmem] * 4,
         out_specs=(vmem,) * 5,
-        scratch_shapes=[pltpu.VMEM((wide, tokens), BF16)],
+        scratch_shapes=[
+            pltpu.VMEM((wide, tokens), BF16),
+            pltpu.VMEM((2 * pairs, tokens, BLOCK), F32),
+        ],
         compiler_params=pltpu.CompilerParams(vmem_limit_bytes=VMEM_LIMIT),
-        cost_estimate=pl.CostEstimate(
-            flops=20 * pairs * tokens * tokens * HEAD_DIM,
-            bytes_accessed=tokens * wide * 20,
-            transcendentals=pairs * tokens * tokens,
-        ),
+        cost_estimate=SHORT,
         name="attend",
     )(inv, project, bias, cosine, sine)
 
@@ -316,11 +466,11 @@
                 grads = dot(v_ref[at, lanes[h // 2]], do_heads[h], 1, 0)
                 p_ref[h, aligned(slot), :] = probs
                 dp_ref[h, aligned(slot), :] = grads
-                fresh.append(sums[h] + jnp.sum(probs * grads, axis=0, keepdims=True))
+                fresh.append(sums[h] + jnp.sum(fold(probs * grads), axis=0))
             return tuple(fresh)
 
         full = full_blocks(code, prompt_blocks)
-        sums = probs_and_grads(full, place, allowed, (jnp.zeros((1, BLOCK), F32),) * count)
+        sums = probs_and_grads(full, place, allowed, (jnp.zeros((8, BLOCK), F32),) * count)
         sums = lax.fori_loop(
             0,
             full,
@@ -329,6 +479,7 @@
             ),
             sums,
         )
+        sums = [jnp.sum(total, axis=0, keepdims=True) for total in sums]
 
         def step(index, grads):
             at = aligned(jnp.where(index == full, code, key_block(code, index, prompt_blocks)))
@@ -390,13 +541,225 @@
             pltpu.VMEM((2 * pairs, tokens, BLOCK), F32),
         ],
         compiler_params=pltpu.CompilerParams(vmem_limit_bytes=VMEM_LIMIT),
-        cost_estimate=pl.CostEstimate(
-            flops=60 * pairs * tokens * tokens * HEAD_DIM,
-            bytes_accessed=tokens * wide * 20,
-            transcendentals=pairs * tokens * tokens,
-        ),
+        cost_estimate=SHORT,
         name="attend_back",
     )(inv, query, key, value, grad, lse, cosine, sine)
+
+
+def load_tile(pieces, out_ref, tile):
+    start = 0
+    for piece in pieces:
+        cut = piece.shape[0]
+
+        @pl.when(pl.program_id(0) == start // tile)
+        def _(piece=piece, start=start % tile, cut=cut):
+            out_ref[start : start + cut, :] = piece[...]
+
+        start += cut
+
+
+def whole(value):
+    return pl.BlockSpec(value.shape, lambda i: (0, 0), pipeline_mode=pl.Buffered(1))
+
+
+def norm_kernel(gain_ref, shift_ref, *refs):
+    out_ref, held = refs[-2:]
+    load_tile(refs[:-2], held, BLOCK)
+    normed, _ = standardize(held[...].astype(F32))
+    out_ref[...] = (normed * gain_ref[...] + shift_ref[...]).astype(BF16)
+
+
+def norm_pieces(pieces, gain, shift):
+    if not cube():
+        return (standardize(pieces[0].astype(F32))[0] * gain + shift).astype(BF16)
+    tokens = sum(piece.shape[0] for piece in pieces)
+    values = (gain, shift, *pieces)
+    return pl.pallas_call(
+        norm_kernel,
+        grid=(tokens // BLOCK,),
+        out_shape=jax.ShapeDtypeStruct((tokens, D), BF16),
+        in_specs=[whole(value) for value in values],
+        out_specs=pl.BlockSpec((BLOCK, D), lambda i: (i, 0)),
+        scratch_shapes=[pltpu.VMEM((BLOCK, D), BF16)],
+        compiler_params=pltpu.CompilerParams(vmem_limit_bytes=VMEM_LIMIT),
+        cost_estimate=SHORT,
+        name="norm_pieces",
+    )(*values)
+
+
+def halves(value):
+    half = value.shape[0] // 2
+    return value[:half], value[half:]
+
+
+def enter_feed(inputs, gain, shift, *parts):
+    resid = inputs.astype(F32) + total_of(parts)
+    normed, _ = standardize(resid)
+    return (resid, *halves((normed * gain + shift).astype(BF16)))
+
+
+def leave_feed(cotangent, resid, gain, *parts):
+    grad = total_of(parts)
+    normed, scaled = standardize(resid)
+    grad_resid = cotangent.astype(F32) + norm_back(grad * gain, normed, scaled)
+    sums = [jnp.sum(grad * normed, axis=0, keepdims=True), jnp.sum(grad, axis=0, keepdims=True)]
+    return (grad_resid, *halves(grad_resid.astype(BF16)), *sums)
+
+
+def leave_layer(inputs, grad_resid, gain, *parts):
+    grad = total_of(parts)
+    normed, scaled = standardize(inputs.astype(F32))
+    sums = [jnp.sum(grad * normed, axis=0, keepdims=True), jnp.sum(grad, axis=0, keepdims=True)]
+    return (grad_resid + norm_back(grad * gain, normed, scaled), *sums)
+
+
+def own_kernel(step, count, *refs):
+    results = step(*(ref[...] for ref in refs[:count]))
+    for ref, result in zip(refs[count:], results):
+        ref[...] = result
+
+
+def own_rows(step, *values):
+    if not cube():
+        return step(*values)
+    vmem = pl.BlockSpec(memory_space=pltpu.VMEM)
+    shapes = jax.eval_shape(step, *values)
+    return pl.pallas_call(
+        functools.partial(own_kernel, step, len(values)),
+        out_shape=shapes,
+        in_specs=[vmem] * len(values),
+        out_specs=tuple(vmem for _ in shapes),
+        compiler_params=pltpu.CompilerParams(vmem_limit_bytes=VMEM_LIMIT),
+        cost_estimate=SHORT,
+        name=step.__name__,
+    )(*values)
+
+
+def ffn_up_kernel(units, count, w_ref, *refs):
+    act_ref, both_ref, hidden_ref = refs[-3:]
+    load_tile(refs[:count], act_ref, BLOCK)
+    both_ref[...] = dot(act_ref[...], w_ref[...], 1, 0)
+    gate = both_ref[:, :units]
+    upper = both_ref[:, units:]
+    hidden_ref[...] = (gate * jax.nn.sigmoid(gate) * upper).astype(BF16)
+
+
+def ffn_up_step(pieces, weight, units, place, before):
+    steps = sum(piece.shape[0] for piece in pieces) // BLOCK
+    tokens = lax.axis_size("ctx") * BLOCK
+    count = len(pieces)
+    return pl.pallas_call(
+        functools.partial(ffn_up_kernel, units, count),
+        grid=(steps,),
+        out_shape=(
+            jax.ShapeDtypeStruct((tokens, D), BF16),
+            jax.ShapeDtypeStruct((tokens, 2 * units), F32),
+            jax.ShapeDtypeStruct((tokens, units), BF16),
+        ),
+        in_specs=[whole(weight)]
+        + [whole(piece) for piece in pieces]
+        + [pl.BlockSpec(memory_space=pl.ANY)] * len(before),
+        out_specs=(
+            pl.BlockSpec((BLOCK, D), lambda i: (place(i), 0)),
+            pl.BlockSpec((BLOCK, 2 * units), lambda i: (place(i), 0)),
+            pl.BlockSpec((BLOCK, units), lambda i: (place(i), 0)),
+        ),
+        input_output_aliases={1 + count + k: k for k in range(len(before))},
+        compiler_params=pltpu.CompilerParams(vmem_limit_bytes=VMEM_LIMIT),
+        cost_estimate=SHORT,
+        name="ffn_up",
+    )(weight, *pieces, *before)
+
+
+def ffn_up(begun, weight, units):
+    if not cube():
+        act = begun[0]
+        both = dot(act, weight, 1, 0)
+        gate = both[:, :units]
+        return act, both, (gate * jax.nn.sigmoid(gate) * both[:, units:]).astype(BF16)
+    far = gather_far(begun)
+    early = ffn_up_step(gather_near(begun), weight, units, lambda i: i + i // 3, ())
+    far, early = tie(far, early)
+    return ffn_up_step(gather_late(far), weight, units, lambda i: 3 + 4 * i, early)
+
+
+def ffn_back_kernel(units, both_ref, cot_ref, down_ref, gb_ref):
+    grad = dot(cot_ref[...], down_ref[...], 1, 1)
+    gate = both_ref[:, :units]
+    upper = both_ref[:, units:]
+    sigma = jax.nn.sigmoid(gate)
+    gb_ref[:, :units] = (grad * upper * sigma * (1.0 + gate * (1.0 - sigma))).astype(BF16)
+    gb_ref[:, units:] = (grad * (gate * sigma)).astype(BF16)
+
+
+def ffn_back(both, cot, down, units):
+    if not cube():
+        grad = dot(cot, down, 1, 1)
+        gate = both[:, :units]
+        sigma = jax.nn.sigmoid(gate)
+        grad_gate = grad * both[:, units:] * sigma * (1.0 + gate * (1.0 - sigma))
+        return jnp.concatenate([grad_gate, grad * (gate * sigma)], axis=1).astype(BF16)
+    tokens = cot.shape[0]
+    tile = 2 * BLOCK
+    return pl.pallas_call(
+        functools.partial(ffn_back_kernel, units),
+        grid=(tokens // tile,),
+        out_shape=jax.ShapeDtypeStruct((tokens, 2 * units), BF16),
+        in_specs=[
+            pl.BlockSpec((tile, 2 * units), lambda i: (i, 0)),
+            pl.BlockSpec((tile, D), lambda i: (i, 0)),
+            pl.BlockSpec((units, D), lambda i: (0, 0), pipeline_mode=pl.Buffered(1)),
+        ],
+        out_specs=pl.BlockSpec((tile, 2 * units), lambda i: (i, 0)),
+        compiler_params=pltpu.CompilerParams(vmem_limit_bytes=VMEM_LIMIT),
+        cost_estimate=SHORT,
+        name="ffn_back",
+    )(both, cot, down)
+
+
+def branch_kernel(first, last, starts, mixed_ref, right_ref, *refs):
+    count = len(starts)
+    left_ref, grad_ref = refs[-2:]
+    total = jnp.zeros(grad_ref.shape, F32)
+    if not first:
+        left_ref[...] = refs[count][...]
+        total = refs[count + 1][...]
+    for start, ref in zip(starts, refs):
+        stop = start + ref.shape[0]
+        left_ref[start:stop, :] = dot(ref[...], right_ref[...], 1, 1).astype(BF16)
+        total += dot(mixed_ref[start:stop, :], ref[...], 0, 0)
+    grad_ref[...] = total.astype(grad_ref.dtype)
+
+
+def branch_step(mixed, right, pieces, starts, before, last):
+    vmem = pl.BlockSpec(memory_space=pltpu.VMEM)
+    values = (mixed, right, *pieces, *before)
+    return pl.pallas_call(
+        functools.partial(branch_kernel, not before, last, starts),
+        out_shape=(
+            jax.ShapeDtypeStruct(mixed.shape, BF16),
+            jax.ShapeDtypeStruct((mixed.shape[1], D), BF16 if last else F32),
+        ),
+        in_specs=[vmem] * len(values),
+        out_specs=(vmem, vmem),
+        compiler_params=pltpu.CompilerParams(vmem_limit_bytes=VMEM_LIMIT),
+        cost_estimate=SHORT,
+        name="branch_step",
+    )(*values)
+
+
+def branch_grads(mixed, right, begun):
+    if not cube():
+        (whole_branch,) = begun
+        left = dot(whole_branch, right, 1, 1).astype(BF16)
+        return left, dot(mixed, whole_branch, 0, 0).astype(BF16)
+    cut = BLOCK // 2
+    places = tuple(range(6)) + tuple(range(8, 14)) + (6, 7, 14, 15)
+    starts = tuple(place * cut for place in places)
+    far = gather_far(begun)
+    early = branch_step(mixed, right, gather_near(begun), starts[:12], (), False)
+    far, early = tie(far, early)
+    return branch_step(mixed, right, gather_late(far), starts[12:], early, True)
 
 
 def turn_tables(blocks):
@@ -450,116 +813,137 @@
     wide = D // cycle
     pairs = wide // LANES
     units = FF // cycle
-    padded = (units + LANES - 1) // LANES * LANES
-    gap = padded - units
-
-    mine = vectors.astype(BF16).T
-    vec = lax.dynamic_update_slice(jnp.zeros((7, D), BF16), mine, (0, owner * rows))
-    vec = sum_everywhere(vec).astype(F32)
-
-    def spread(weight, parts):
-        width = weight.shape[1] // (parts * cycle)
-        split = weight.astype(BF16).reshape(rows, parts, cycle, width)
-        split = split.transpose(2, 0, 1, 3).reshape(cycle, rows, parts * width)
-        return lax.all_to_all(split, "ctx", 0, 0)
 
     def rows_of(split):
         full = lax.all_gather(split, "fsdp", axis=0, tiled=False)
         return full.transpose(1, 0, 2, 3).reshape(D, split.shape[2])
 
-    w_qkv = rows_of(spread(attn_in, 3))
     w_attn = lax.all_gather(attn_out.astype(BF16), "fsdp", axis=0, tiled=True)
-    both_in = rows_of(spread(ffn_in, 2))
-    w_up = jnp.pad(both_in.reshape(D, 2, units), ((0, 0), (0, 0), (0, gap))).reshape(D, 2 * padded)
-    w_down = lax.all_gather(ffn_out.astype(BF16), "fsdp", axis=0, tiled=True)
-    w_down = jnp.pad(w_down, ((0, gap), (0, 0)))
-
-    inputs = layer_in[0].astype(F32)
-    normed_one, scaled_one = standardize(inputs)
-    attn_act = gather_tokens((normed_one * vec[0] + vec[1]).astype(BF16))
-    cot_low = gather_tokens(cotangent[0])
+    mine = vectors.astype(BF16).T.reshape(1, 7 * rows)
+    below = jnp.pad(mine, ((0, 15), (0, 3 * wide - 7 * rows)))
+    qkv_split = exchange(split_columns(attn_in, 3, below))
+    w_qkv = rows_of(qkv_split[:, :rows])
+
+    vec = qkv_split[:, rows, : 7 * rows].reshape(1, cycle, 7, rows)
+    vec = lax.dynamic_update_slice(
+        jnp.zeros((groups, cycle, 7, rows), BF16), vec, (lax.axis_index("fsdp"), 0, 0, 0)
+    )
+    vec = sum_everywhere(vec, ("fsdp",)).transpose(2, 1, 0, 3).reshape(7, D).astype(F32)
+
+    x_pieces, vec, w_attn, ffn_in_late, cot_own = tie(
+        gather_pieces(gather_start(*halves(layer_in[0]))), vec, w_attn, ffn_in, cotangent[0]
+    )
+    attn_act = norm_pieces(x_pieces, vec[0:1], vec[1:2])
+    cot_begun = gather_start(*halves(cot_own))
+    up_split, down_own, attn_act, first = tie(
+        exchange(split_columns(ffn_in_late, 2)), ffn_out.astype(BF16), attn_act, cot_begun[4:6]
+    )
+    cot_begun = (*cot_begun[:4], *first, *cot_begun[6:])
+    w_up = rows_of(up_split)
+    w_down = lax.all_gather(down_own, "fsdp", axis=0, tiled=True)
+
     codes = block_map[0][places()]
     inv = jnp.argsort(codes).astype(jnp.int32)
     cosine, sine = turn_tables(blocks)
     bias = lax.dynamic_slice_in_dim(vec[2:5], here * wide, wide, 1).reshape(1, 3 * wide)
     project = dot(attn_act, w_qkv, 1, 0)
+    project, cot_begun = tie(project, cot_begun)
     query, key, value, mixed, lse = attend(inv, project, bias, cosine, sine, pairs, blocks)
-    resid = inputs + scatter_tokens(lambda a, b: dot(mixed[a:b], w_attn, 1, 0))
-
-    normed_two, scaled_two = standardize(resid)
-    ffn_act = gather_tokens((normed_two * vec[5] + vec[6]).astype(BF16))
-    grad_hidden = dot(cot_low, w_down, 1, 1)
-    both = dot(ffn_act, w_up, 1, 0)
-    gate = both[:, :padded]
-    upper = both[:, padded:]
-    sigma = jax.nn.sigmoid(gate)
-    active = gate * sigma
-    hidden = (active * upper).astype(BF16)
-    grad_gate = grad_hidden * upper * sigma * (1.0 + gate * (1.0 - sigma))
-    grad_upper = grad_hidden * active
-    grad_both = jnp.concatenate([grad_gate, grad_upper], axis=1).astype(BF16)
-    grad_ffn_act = scatter_tokens(lambda a, b: dot(grad_both[a:b], w_up, 1, 1))
+    cot_far = gather_far(cot_begun)
+    mixed, cot_far = tie(mixed, cot_far)
+    away = scatter_away(mixed, w_attn, 0)
+    begun = scatter_start(scatter_sums(mixed, w_attn, 0, away))
+    cot_low = jnp.concatenate(gather_pieces(cot_begun, cot_far), axis=0)
+    begun, cot_low, w_up = window(begun, cot_low, w_up)
+    parts = scatter_end(begun)
+    resid, act_top, act_low = own_rows(enter_feed, layer_in[0], vec[5:6], vec[6:7], *parts)
 
     def owners(grad):
-        return lax.psum_scatter(grad, "fsdp", scatter_dimension=0, tiled=True).astype(F32)
+        return lax.psum_scatter(grad, "fsdp", scatter_dimension=0, tiled=True)
+
+    def by_owner(grad):
+        wider = grad.shape[1]
+        return grad.reshape(-1, groups, rows, wider).transpose(1, 0, 2, 3).reshape(-1, wider)
 
     def owners_of_rows(grad):
-        wider = grad.shape[1]
-        split = grad.reshape(cycle, groups, rows, wider).transpose(1, 0, 2, 3)
-        share = lax.psum_scatter(
-            split.reshape(groups * cycle * rows, wider), "fsdp", scatter_dimension=0, tiled=True
-        )
-        return share.reshape(cycle, rows, wider)
-
-    def collect(share, parts):
-        width = share.shape[2] // parts
-        split = lax.all_to_all(share, "ctx", 0, 0).reshape(cycle, rows, parts, width)
-        return split.transpose(1, 2, 0, 3).reshape(rows, parts * cycle * width).astype(F32)
-
-    grad_in = dot(ffn_act, grad_both, 0, 0).astype(BF16)
-    grad_in = grad_in.reshape(D, 2, padded)[:, :, :units].reshape(D, 2 * units)
+        return owners(grad).reshape(-1, rows, grad.shape[1])
+
+    ffn_act, both, hidden = ffn_up(gather_start(act_top, act_low), w_up, units)
+    grad_both = ffn_back(both, cot_low, w_down, units)
+    away = scatter_away(grad_both, w_up, 1)
+    away, grad_down = tie(away, dot(hidden, cot_low, 0, 0).astype(BF16))
+    share_down = owners(grad_down)
+    begun = scatter_start(scatter_sums(grad_both, w_up, 1, away))
+    grad_in = by_owner(dot(ffn_act, grad_both, 0, 0).astype(BF16))
+    parts, grad_in = tie(scatter_end(begun), grad_in)
     share_in = owners_of_rows(grad_in)
-    grad_down = dot(hidden, cot_low, 0, 0)[:units].astype(BF16)
-    share_down = owners(grad_down)
-    result = resid + scatter_tokens(lambda a, b: dot(hidden[a:b], w_down, 1, 0))
-    layer_out = result.astype(BF16)[None]
-
-    grad_resid = cotangent[0].astype(F32) + norm_back(
-        grad_ffn_act * vec[5], normed_two, scaled_two
-    )
-    grad_branch = gather_tokens(grad_resid.astype(BF16))
-    grad_mixed = dot(grad_branch, w_attn, 1, 1).astype(BF16)
+    grad_resid, branch_top, branch_low, gain_two, shift_two = own_rows(
+        leave_feed, cotangent[0], resid, vec[5:6], *parts
+    )
+
+    begun = gather_start(branch_top, branch_low)
+    if cube():
+        c_top, hidden = tie(begun[2], hidden)
+        begun = (*begun[:2], c_top, *begun[3:])
+    out_sums = scatter_sums(hidden, w_down, 0, scatter_away(hidden, w_down, 0))
+    begun, out_sums = window(begun, out_sums)
+    grad_mixed, grad_out = branch_grads(mixed, w_attn, begun)
+    share_out = owners(grad_out)
+    grad_mixed, out_sums, share_down = tie(grad_mixed, out_sums, share_down)
+    out_begun = scatter_start(out_sums)
     grad_project = attend_back(
         inv, query, key, value, grad_mixed, lse, cosine, sine, pairs, blocks
     )
-    grad_attn_act = scatter_tokens(lambda a, b: dot(grad_project[a:b], w_qkv, 1, 1))
-    input_grad = (grad_resid + norm_back(grad_attn_act * vec[0], normed_one, scaled_one))[None]
-    share_out = owners(dot(mixed, grad_branch, 0, 0).astype(BF16))
-    share_qkv = owners_of_rows(dot(attn_act, grad_project, 0, 0).astype(BF16))
-
+    grad_project, out_begun, share_in = tie(grad_project, out_begun, share_in)
+    out_parts = scatter_end(out_begun)
+    away = scatter_away(grad_project, w_qkv, 1)
+    grad_qkv = by_owner(dot(attn_act, grad_project, 0, 0).astype(BF16))
+    away, grad_qkv = tie(away, grad_qkv)
+    share_qkv = owners_of_rows(grad_qkv)
+    sums = scatter_sums(grad_project, w_qkv, 1, away)
+    sums, share_in, share_out, grad_project = tie(sums, share_in, share_out, grad_project)
+    begun = scatter_start(sums)
+    begun, out_parts, split_in = window(begun, out_parts, exchange(share_in))
+    layer_out = (resid + total_of(out_parts)).astype(BF16)[None]
+    parts = scatter_end(begun)
+    input_grad, gain_one, shift_one = own_rows(
+        leave_layer, layer_in[0], grad_resid, vec[0:1], *parts
+    )
+    split_qkv = exchange(share_qkv)
+
+    squares = F32(0.0)
+    for share in (share_qkv, share_out, share_in, share_down):
+        wide_share = share.astype(F32)
+        squares = squares + jnp.sum(wide_share * wide_share)
     bias_grads = jnp.sum(grad_project.astype(F32), axis=0).reshape(3, wide)
     bias_grads = lax.dynamic_update_slice(jnp.zeros((3, D), F32), bias_grads, (0, here * wide))
-    vector_grads = jnp.concatenate(
+    sums = jnp.concatenate(
         [
-            jnp.sum(grad_attn_act * normed_one, axis=0)[None],
-            jnp.sum(grad_attn_act, axis=0)[None],
+            gain_one,
+            shift_one,
             bias_grads,
-            jnp.sum(grad_ffn_act * normed_two, axis=0)[None],
-            jnp.sum(grad_ffn_act, axis=0)[None],
+            gain_two,
+            shift_two,
+            jnp.where(jnp.arange(D)[None] == 0, squares, 0.0),
         ],
         axis=0,
     )
-    vector_grads = lax.dynamic_slice_in_dim(
-        sum_everywhere(vector_grads), owner * rows, rows, 1
-    ).T
-
-    squares = F32(0.0)
-    for grad in (share_qkv, share_out, share_in, share_down, vector_grads):
-        wide_grad = grad.astype(F32)
-        squares = squares + jnp.sum(wide_grad * wide_grad)
-    grad_norm = jnp.sqrt(sum_everywhere(squares.reshape(1, 1)))[0, 0]
+    sums, split_qkv = tie(sum_everywhere(sums, ("ctx",)), split_qkv)
+    sums = sum_everywhere(sums, ("fsdp",))
+    vector_sums = sums[:7]
+    grad_norm = jnp.sqrt(jnp.sum(vector_sums * vector_sums) + sums[7, 0])
+    mine = jnp.arange(D)[:, None] == owner * rows + jnp.arange(rows)[None]
+    vector_grads = lax.dot_general(
+        mine.astype(F32), vector_sums, (((0,), (1,)), ((), ())), precision=lax.Precision.HIGHEST
+    )
     clip = jnp.minimum(1.0, CLIP_LIMIT / (grad_norm + 1e-06))
-    grad_list = (collect(share_qkv, 3), share_out, collect(share_in, 2), share_down, vector_grads)
+    grad_list = (
+        join_columns(split_qkv, 3),
+        share_out,
+        join_columns(split_in, 2),
+        share_down,
+        vector_grads,
+    )
     rates = (D ** (-0.5), 0.6 * max(D // 64, 32) ** (-0.5), D ** (-0.5), (FF // 4) ** (-0.5), 0.3)
     weights = (attn_in, attn_out, ffn_in, ffn_out, vectors)
     firsts = (first_attn_in, first_attn_out, first_ffn_in, first_ffn_out, first_vectors)
@@ -568,10 +952,10 @@
     for index in range(5):
         updated.extend(
             adam(
-                weights[index], clip * grad_list[index], firsts[index], seconds[index], rates[index]
+                weights[index], clip * grad_list[index].astype(F32), firsts[index], seconds[index], rates[index]
             )
         )
-    return (layer_out, input_grad, grad_norm, *updated)
+    return (layer_out, input_grad[None], grad_norm, *updated)
 
 
 def solution(mesh):

time: 870 us -> 678 us (0.78)
  local copies, waits for them, and re-layouts: 178 us -> 49.8 us
  Pallas kernels: 98.6 us -> 206 us
  matrix products: 148 us -> 75.8 us
  waiting for transfers between devices: 239 us -> 178 us
  other arithmetic: 62.1 us -> 40.8 us
  starting transfers between devices: 92.7 us -> 79.1 us
    pallas_call x0 -> x17, Pallas kernels: none -> 129 us  [the longest x4 35.5 us: chip_sums(): pl.pallas_call(functools.partial(chip_kernel, right_dim), grid=(2,), out_...]
    dot_general x16 -> x8, matrix products: 148 us -> 74.7 us  [dot(): lax.dot_general(left, right, (((left_dim,), (right_dim,)), ((), ())), pre...]
    ppermute x95 -> x91, waiting for transfers between devices: 239 us -> 170 us  [swap(): return lax.ppermute(value, axis, [(i, i ^ bit) for i in range(size)])]
    unnamed x163 -> x153, local copies, waits for them, and re-layouts: 80 us -> 28 us
    another operation x2 -> x1, local copies, waits for them, and re-layouts: 29.2 us -> 0.09 us  [local(): vec = qkv_split[:, rows, :7 * rows].reshape(1, cycle, 7, rows)]
    pallas_call x1, Pallas kernels: 53.6 us -> 31.6 us  [attend(): pl.pallas_call(functools.partial(attend_kernel, pairs, blocks), out_shape...]
    mul x5 -> x0, local copies, waits for them, and re-layouts: 16.1 us -> none  [local(): clip * grad_list[index]]
    ppermute x95 -> x91, starting transfers between devices: 79.9 us -> 66.1 us  [swap(): return lax.ppermute(value, axis, [(i, i ^ bit) for i in range(size)])]
  transfers between devices with their start and end apart: 106 -> 102, of which waited for: 46 -> 43; matrix products, arithmetic and copies ran while one was open for 39% -> 17% of each run, Pallas kernels for 11% -> 28%
where the time goes in v2:
time: 678 us; the launch traced here: 669 us
  Pallas kernels  206 us (30%)
  waiting for transfers between devices  178 us (26%)
  starting transfers between devices  79.1 us (12%)
  matrix products  75.8 us (11%)
  local copies, waits for them, and re-layouts  49.8 us (7%)
  other arithmetic  40.8 us (6%)
  between operations  20.4 us (3%)
  blocking collectives  19.6 us (3%)
    ppermute x91, waiting for transfers between devices, swap(): return lax.ppermute(value, axis, [(i, i ^ bit) for i in range(size)])  170 us
    dot_general x8, matrix products, dot(): lax.dot_general(left, right, (((left_dim,), (right_dim,)), ((), ())), pre...  74.7 us
    ppermute x91, starting transfers between devices, swap(): return lax.ppermute(value, axis, [(i, i ^ bit) for i in range(size)])  66.1 us
    pallas_call x1, Pallas kernels, attend_back(): pl.pallas_call(functools.partial(attend_back_kernel, pairs, blocks), out_...  45.3 us
    pallas_call x4, Pallas kernels, chip_sums(): pl.pallas_call(functools.partial(chip_kernel, right_dim), grid=(2,), out_...  35.5 us
    pallas_call x1, Pallas kernels, attend(): pl.pallas_call(functools.partial(attend_kernel, pairs, blocks), out_shape...  31.6 us
    unnamed x153, local copies, waits for them, and re-layouts  28 us
    pallas_call x2, Pallas kernels, ffn_up_step(): pl.pallas_call(functools.partial(ffn_up_kernel, units, count), grid=(step...  26.1 us
  transfers between devices with their start and end apart: 102, of which 43 were waited for; matrix products, arithmetic and copies ran while one was open for 17% of the time, Pallas kernels for 28%

profile of v2, /device:TPU:0, one launch (start us, length us, event | category | flops | bytes accessed | tf_op | source)
XLA Modules:
  0.0 668.6 jit_solution(6218347084961985478)
XLA Ops:
  11.5 19.6 %all_to_all.20 = bf16[8,80,768]{2,1,0:T(8,128)(2,1)S(1)} all-to-all(bf16[8,80,768]{2,1,0:T(8,128)(2,1)S(1)} %split_columns.2), channel_id=1, replica_groups=mesh['ctx'=8,'fsdp'=4] {'ctx'}, dimensions={0} | all-to-all | bytes 1966080 | tf_op jit(solution)/shard_map/all_to_all | solution.py:262
  35.7 5.7 collective-permute-done.14
  45.6 2.0 collective-permute-done.2.refs_2_
  49.7 9.1 %collective-permute-done.3.refs_3_ = bf16[128,2048]{1,0:T(8,128)(2,1)S(1)} collective-permute-done((bf16[128,2048]{1,0:T(8,128)(2,1)S(1)}, bf16[128,2048]{1,0:T(8,128)(2,1)S(1)}, u32[]{:S(2)}, u32[]{:S(2)}) %collective-permute-start.3) | collective-permute-done | bytes 524320 | tf_op jit(solution)/shard_map/ppermute | solution.py:70
  59.4 10.0 %collective-permute-done.6.refs_6_ = bf16[128,2048]{1,0:T(8,128)(2,1)S(1)} collective-permute-done((bf16[128,2048]{1,0:T(8,128)(2,1)S(1)}, bf16[128,2048]{1,0:T(8,128)(2,1)S(1)}, u32[]{:S(2)}, u32[]{:S(2)}) %collective-permute-start.6) | collective-permute-done | bytes 524320 | tf_op jit(solution)/shard_map/ppermute | solution.py:70
  73.2 3.2 split_columns.3
  76.4 4.4 all-to-all-start.1
  80.9 2.3 fusion.42
  87.5 10.9 %norm_pieces.1 = bf16[2048,2048]{1,0:T(8,128)(2,1)} custom-call(f32[1,2048]{1,0:T(1,128)S(1)} %get-tuple-element.398.gain_ref.refs_2_, f32[1,2048]{1,0:T(1,128)S(1)} %get-tuple-element.397.shift_ref, bf16[128,2048]{1,0:T(8,128)(2,1)S(1)} %get-tuple-element.205.refs_0_, bf16[128,2048]{1,0:T(8,128)(2,1)S(1)} %get-tuple-element.206.refs_1_, ...), custom_call_target="tpu_custom_call" | custom-call | flops 1000000 | bytes 1000000 | tf_op jit(solution)/shard_map/norm_pieces/pallas_call | solution.py:577
  98.3 12.5 %collective-permute-done.16 = bf16[128,2048]{1,0:T(8,128)(2,1)} collective-permute-done((bf16[128,2048]{1,0:T(8,128)(2,1)}, bf16[128,2048]{1,0:T(8,128)(2,1)}, u32[]{:S(2)}, u32[]{:S(2)}) %collective-permute-start.16) | collective-permute-done | bytes 524320 | tf_op jit(solution)/shard_map/ppermute | solution.py:70
  116.0 2.3 copy.65
  118.3 12.2 %fusion.44.proj_ref = f32[2048,768]{1,0:T(8,128)} fusion(bf16[2048,2048]{1,0:T(8,128)(2,1)} %norm_pieces.1, bf16[2048,768]{1,0:T(8,128)(2,1)S(1)} %bitcast.59), kind=kOutput, calls=%fused_computation.123 | convolution fusion | flops 6442450944 | bytes 17825792 | tf_op jit(solution)/shard_map/dot_general | solution.py:63
  137.4 31.6 %attend.1 = (bf16[2048,256]{1,0:T(8,128)(2,1)S(1)}, bf16[2048,256]{1,0:T(8,128)(2,1)}, bf16[2048,256]{1,0:T(8,128)(2,1)}, bf16[2048,256]{1,0:T(8,128)(2,1)}, f32[4,2048]{1,0:T(4,128)S(1)}) custom-call(s32[8]{0:T(128)S(1)} %get-tuple-element.203.inv_ref, f32[2048,768]{1,0:T(8,128)} %fusion.44.proj_ref, f32[1,768]{1,0:T(1,128)S(1)} %bitcast.52, ...), custom_call_target="tpu_custom_call" | custom-call | flops 1000000 | bytes 1000000 | tf_op jit(solution)/shard_map/attend/pallas_call | solution.py:409
  169.0 4.4 convolution_convert_fusion.3
  183.9 2.0 copy-done.8
  186.4 5.3 chip_sums.4
  196.2 9.6 %collective-permute-done.33 = bf16[128,2048]{1,0:T(8,128)(2,1)S(1)} collective-permute-done((bf16[128,2048]{1,0:T(8,128)(2,1)}, bf16[128,2048]{1,0:T(8,128)(2,1)S(1)}, u32[]{:S(2)}, u32[]{:S(2)}) %collective-permute-start.33) | collective-permute-done | bytes 524320 | tf_op jit(solution)/shard_map/ppermute | solution.py:70
  207.2 2.0 collective-permute-done.35
  214.8 3.2 all-gather.13.cloned.1.call-done
  218.0 5.6 copy.68
  224.3 10.1 %collective-permute-done.34.refs_5_ = bf16[128,2048]{1,0:T(8,128)(2,1)} collective-permute-done((bf16[128,2048]{1,0:T(8,128)(2,1)S(1)}, bf16[128,2048]{1,0:T(8,128)(2,1)}, u32[]{:S(2)}, u32[]{:S(2)}) %collective-permute-start.34) | collective-permute-done | bytes 524320 | tf_op jit(solution)/shard_map/ppermute | solution.py:70
  234.4 3.9 enter_feed.1
  243.1 10.6 %collective-permute-done.37.refs_2_ = bf16[128,2048]{1,0:T(8,128)(2,1)S(1)} collective-permute-done((bf16[128,2048]{1,0:T(8,128)(2,1)S(1)}, bf16[128,2048]{1,0:T(8,128)(2,1)S(1)}, u32[]{:S(2)}, u32[]{:S(2)}) %collective-permute-start.37) | collective-permute-done | bytes 524320 | tf_op jit(solution)/shard_map/ppermute | solution.py:70
  254.4 9.5 %collective-permute-done.43.refs_3_ = bf16[128,2048]{1,0:T(8,128)(2,1)S(1)} collective-permute-done((bf16[128,2048]{1,0:T(8,128)(2,1)S(1)}, bf16[128,2048]{1,0:T(8,128)(2,1)S(1)}, u32[]{:S(2)}, u32[]{:S(2)}) %collective-permute-start.43) | collective-permute-done | bytes 524320 | tf_op jit(solution)/shard_map/ppermute | solution.py:70
  268.3 17.8 %ffn_up.2 = (bf16[2048,2048]{1,0:T(8,128)(2,1)}, f32[2048,1408]{1,0:T(8,128)}, bf16[2048,704]{1,0:T(8,128)(2,1)}) custom-call(bf16[2048,1408]{1,0:T(8,128)(2,1)} %bitcast.53, bf16[128,2048]{1,0:T(8,128)(2,1)S(1)} %get-tuple-element.260.refs_0_, bf16[128,2048]{1,0:T(8,128)(2,1)S(1)} %get-tuple-element.261.refs_1_, ...), custom_call_target="tpu_custom_call" | custom-call | flops 1000000 | bytes 1000000 | tf_op jit(solution)/shard_map/ffn_up/pallas_call | solution.py:651
  289.6 8.3 %ffn_up.3 = (bf16[2048,2048]{1,0:T(8,128)(2,1)}, f32[2048,1408]{1,0:T(8,128)}, bf16[2048,704]{1,0:T(8,128)(2,1)}) custom-call(bf16[2048,1408]{1,0:T(8,128)(2,1)} %bitcast.54, bf16[128,2048]{1,0:T(8,128)(2,1)S(1)} %collective-permute-done.38.refs_0_, ...), custom_call_target="tpu_custom_call", output_to_operand_aliasing={{0}: (5, {}), {1}: (6, {}), {2}: (7, {})} | custom-call | flops 1000000 | bytes 1000000 | tf_op jit(solution)/shard_map/ffn_up/pallas_call | solution.py:651
  297.9 15.4 %ffn_back.1.left_ref = bf16[2048,1408]{1,0:T(8,128)(2,1)} custom-call(f32[2048,1408]{1,0:T(8,128)} %get-tuple-element.272.both_ref, bf16[2048,2048]{1,0:T(8,128)(2,1)} %constant_dynamic-update-slice_fusion.cot_ref, bf16[704,2048]{1,0:T(8,128)(2,1)} %all-gather.9.cloned.1.call-done.down_ref.right_ref), custom_call_target="tpu_custom_call" | custom-call | flops 1000000 | bytes 1000000 | tf_op jit(solution)/shard_map/ffn_back/pallas_call | solution.py:704
  313.2 11.6 %convolution_convert_fusion.2 = bf16[1024,2048]{1,0:T(8,128)(2,1)} fusion(bf16[2048,1408]{1,0:T(8,128)(2,1)} %bitcast.55, bf16[2048,1408]{1,0:T(8,128)(2,1)} %ffn_back.1.left_ref), kind=kOutput, calls=%fused_computation.5 | convolution fusion | flops 5907677184 | bytes 12845056 | tf_op jit(solution)/shard_map/dot_general | solution.py:63
  324.9 7.6 %convolution_convert_fusion.6 = bf16[704,2048]{1,0:T(8,128)(2,1)} fusion(bf16[2048,704]{1,0:T(8,128)(2,1)S(1)} %copy-done.3, bf16[2048,2048]{1,0:T(8,128)(2,1)S(1)} %bitcast.63), kind=kOutput, calls=%fused_computation.9 | convolution fusion | flops 5907021824 | bytes 14155776 | tf_op jit(solution)/shard_map/dot_general | solution.py:63
  332.6 13.0 %chip_sums.5 = (bf16[256,2048]{1,0:T(8,128)(2,1)}, bf16[128,2048]{1,0:T(8,128)(2,1)S(1)}, bf16[128,2048]{1,0:T(8,128)(2,1)S(1)}, bf16[128,2048]{1,0:T(8,128)(2,1...) custom-call(bf16[2048,1408]{1,0:T(8,128)(2,1)} %ffn_back.1.left_ref, ...), custom_call_target="tpu_custom_call" | custom-call | flops 1000000 | bytes 1000000 | tf_op jit(solution)/shard_map/chip_sums/pallas_call | solution.py:153
  349.7 10.9 %collective-permute-done.53 = bf16[128,2048]{1,0:T(8,128)(2,1)S(1)} collective-permute-done((bf16[128,2048]{1,0:T(8,128)(2,1)}, bf16[128,2048]{1,0:T(8,128)(2,1)S(1)}, u32[]{:S(2)}, u32[]{:S(2)}) %collective-permute-start.53) | collective-permute-done | bytes 524320 | tf_op jit(solution)/shard_map/ppermute | solution.py:70
  362.9 17.2 %convolution_convert_fusion = bf16[2048,1408]{1,0:T(8,128)(2,1)S(1)} fusion(bf16[2048,2048]{1,0:T(8,128)(2,1)} %get-tuple-element.284, bf16[2048,1408]{1,0:T(8,128)(2,1)} %ffn_back.1.left_ref), kind=kOutput, calls=%fused_computation.1 | convolution fusion | flops 11814043648 | bytes 19922944 | tf_op jit(solution)/shard_map/dot_general | solution.py:63
  380.1 3.0 copy.69
  384.6 6.4 leave_feed.1
  393.7 3.6 convolution_convert_fusion.1
  401.6 10.7 %collective-permute-done.58.refs_2_ = bf16[128,2048]{1,0:T(8,128)(2,1)S(1)} collective-permute-done((bf16[128,2048]{1,0:T(8,128)(2,1)S(1)}, bf16[128,2048]{1,0:T(8,128)(2,1)S(1)}, u32[]{:S(2)}, u32[]{:S(2)}) %collective-permute-start.58) | collective-permute-done | bytes 524320 | tf_op jit(solution)/shard_map/ppermute | solution.py:70
  413.5 2.0 copy-done.14
  415.5 8.6 %chip_sums.6 = (bf16[256,2048]{1,0:T(8,128)(2,1)}, bf16[128,2048]{1,0:T(8,128)(2,1)S(1)}, bf16[128,2048]{1,0:T(8,128)(2,1)S(1)}, bf16[128,2048]{1,0:T(8,128)(2,1...) custom-call(bf16[2048,704]{1,0:T(8,128)(2,1)} %get-tuple-element.295.left_ref, ...), custom_call_target="tpu_custom_call" | custom-call | flops 1000000 | bytes 1000000 | tf_op jit(solution)/shard_map/chip_sums/pallas_call | solution.py:153
  428.6 11.3 %branch_step.2 = (bf16[2048,256]{1,0:T(8,128)(2,1)}, f32[256,2048]{1,0:T(8,128)}) custom-call(bf16[2048,256]{1,0:T(8,128)(2,1)} %get-tuple-element.233.left_ref.mixed_ref, bf16[256,2048]{1,0:T(8,128)(2,1)} %all-gather.7.cloned.1.call-done.right_ref, bf16[128,2048]{1,0:T(8,128)(2,1)S(1)} %get-tuple-element.292.refs_0_, ...), custom_call_target="tpu_custom_call" | custom-call | flops 1000000 | bytes 1000000 | tf_op jit(solution)/shard_map/branch_step/pallas_call | solution.py:737
  443.4 6.7 branch_step.3
  454.1 45.3 %attend_back.1.left_ref = bf16[2048,768]{1,0:T(8,128)(2,1)} custom-call(s32[8]{0:T(128)S(1)} %get-tuple-element.203.inv_ref, bf16[2048,256]{1,0:T(8,128)(2,1)S(1)} %get-tuple-element.254.q_ref, bf16[2048,256]{1,0:T(8,128)(2,1)} %get-tuple-element.255.k_ref, bf16[2048,256]{1,0:T(8,128)(2,1)} %get-tuple-element.256.v_ref, ...), custom_call_target="tpu_custom_call" | custom-call | flops 1000000 | bytes 1000000 | tf_op jit(solution)/shard_map/attend_back/pallas_call | solution.py:531
  501.2 7.9 %convolution_convert_fusion.4 = bf16[1024,2048]{1,0:T(8,128)(2,1)} fusion(bf16[2048,768]{1,0:T(8,128)(2,1)} %bitcast.60, bf16[2048,768]{1,0:T(8,128)(2,1)} %attend_back.1.left_ref), kind=kOutput, calls=%fused_computation.7 | convolution fusion | flops 3223322624 | bytes 8912896 | tf_op jit(solution)/shard_map/dot_general | solution.py:63
  509.2 10.2 %convolution_convert_fusion.5 = bf16[2048,768]{1,0:T(8,128)(2,1)S(1)} fusion(bf16[2048,2048]{1,0:T(8,128)(2,1)} %norm_pieces.1, bf16[2048,768]{1,0:T(8,128)(2,1)} %attend_back.1.left_ref), kind=kOutput, calls=%fused_computation.8 | convolution fusion | flops 6444023808 | bytes 14680064 | tf_op jit(solution)/shard_map/dot_general | solution.py:63
  523.5 8.7 %chip_sums.7 = (bf16[256,2048]{1,0:T(8,128)(2,1)}, bf16[128,2048]{1,0:T(8,128)(2,1)S(1)}, bf16[128,2048]{1,0:T(8,128)(2,1)S(1)}, bf16[128,2048]{1,0:T(8,128)(2,1...) custom-call(bf16[2048,768]{1,0:T(8,128)(2,1)} %attend_back.1.left_ref, ...), custom_call_target="tpu_custom_call" | custom-call | flops 1000000 | bytes 1000000 | tf_op jit(solution)/shard_map/chip_sums/pallas_call | solution.py:153
  532.2 4.4 reduce-scatter.9.cloned.1.call-done
  538.0 2.0 add_convert_fusion.3
  544.9 4.5 all-to-all-start.2
  549.4 2.3 collective-permute-done.82
  553.2 2.0 add_convert_fusion.1
  555.1 11.2 %collective-permute-done.84 = bf16[128,2048]{1,0:T(8,128)(2,1)S(1)} collective-permute-done((bf16[128,2048]{1,0:T(8,128)(2,1)}, bf16[128,2048]{1,0:T(8,128)(2,1)S(1)}, u32[]{:S(2)}, u32[]{:S(2)}) %collective-permute-start.84) | collective-permute-done | bytes 524320 | tf_op jit(solution)/shard_map/ppermute | solution.py:70
  568.5 2.4 convert_reduce_fusion
  571.7 2.7 multiply_reduce_fusion
  574.4 18.6 %collective-permute-done.79.refs_7_ = bf16[128,2048]{1,0:T(8,128)(2,1)} collective-permute-done((bf16[128,2048]{1,0:T(8,128)(2,1)}, bf16[128,2048]{1,0:T(8,128)(2,1)}, u32[]{:S(2)}, u32[]{:S(2)}) %collective-permute-start.79) | collective-permute-done | bytes 524320 | tf_op jit(solution)/shard_map/ppermute | solution.py:70
  593.1 9.5 %collective-permute-done.83.refs_5_ = bf16[128,2048]{1,0:T(8,128)(2,1)S(1)} collective-permute-done((bf16[128,2048]{1,0:T(8,128)(2,1)}, bf16[128,2048]{1,0:T(8,128)(2,1)S(1)}, u32[]{:S(2)}, u32[]{:S(2)}) %collective-permute-start.83) | collective-permute-done | bytes 524320 | tf_op jit(solution)/shard_map/ppermute | solution.py:70
  602.6 5.9 leave_layer.1
  608.5 3.5 all-to-all-start.3
  612.1 2.3 multiply_reduce_fusion.1
  620.4 4.7 collective-permute-done.87
  626.6 2.3 convert_add_fusion
  631.0 2.8 collective-permute-done.89
  641.7 2.8 multiply_subtract_fusion.3
  644.6 4.4 multiply_subtract_fusion.2
  649.1 3.1 multiply_subtract_fusion.1
  654.3 5.1 multiply_subtract_fusion
  (404 shorter events, 133.9 us)
Async XLA Ops:
  7.2 66.0 %all-gather.7.cloned.1.call-start = ((), (), s32[]{:S(2)}) async-start(), calls=%async_computation.8 | async-start | bytes 1310720 | tf_op jit(solution)/shard_map/all_gather | solution.py:821
  9.1 106.9 %all-gather.11.cloned.1.call-start = ((), (), s32[]{:S(2)}) async-start(), calls=%async_computation.14 | async-start | bytes 3932160 | tf_op jit(solution)/shard_map/all_gather | solution.py:818
  32.8 14.8 %collective-permute-start.2 = (bf16[128,2048]{1,0:T(8,128)(2,1)S(1)}, bf16[128,2048]{1,0:T(8,128)(2,1)S(1)}, u32[]{:S(2)}, u32[]{:S(2)}) collective-permute-start(bf16[128,2048]{1,0:T(8,128)(2,1)S(1)} %get-tuple-element.205.refs_0_), channel_id=1, source_target_pairs={{0,8},{4,12},{8,0},{12,4},{16,24},{20,28},{24,16},{28,20},{1,9},{5... | collective-permute-start | bytes 1572872 | tf_op jit(solution)/shard_map/ppermute | solution.py:70
  33.3 14.9 %collective-permute-start.5 = (bf16[128,2048]{1,0:T(8,128)(2,1)S(1)}, bf16[128,2048]{1,0:T(8,128)(2,1)}, u32[]{:S(2)}, u32[]{:S(2)}) collective-permute-start(bf16[128,2048]{1,0:T(8,128)(2,1)S(1)} %get-tuple-element.206.refs_1_), channel_id=1, source_target_pairs={{0,16},{4,20},{8,24},{12,28},{16,0},{20,4},{24,8},{28,12},{1,17},{... | collective-permute-start | bytes 1572872 | tf_op jit(solution)/shard_map/ppermute | solution.py:70
  42.7 16.1 %collective-permute-start.3 = (bf16[128,2048]{1,0:T(8,128)(2,1)S(1)}, bf16[128,2048]{1,0:T(8,128)(2,1)S(1)}, u32[]{:S(2)}, u32[]{:S(2)}) collective-permute-start(bf16[128,2048]{1,0:T(8,128)(2,1)S(1)} %get-tuple-element.206.refs_1_), channel_id=1, source_target_pairs={{0,8},{4,12},{8,0},{12,4},{16,24},{20,28},{24,16},{28,20},{1,9},{5... | collective-permute-start | bytes 1572872 | tf_op jit(solution)/shard_map/ppermute | solution.py:70
  44.1 15.3 %collective-permute-start.4 = (bf16[128,2048]{1,0:T(8,128)(2,1)S(1)}, bf16[128,2048]{1,0:T(8,128)(2,1)S(1)}, u32[]{:S(2)}, u32[]{:S(2)}) collective-permute-start(bf16[128,2048]{1,0:T(8,128)(2,1)S(1)} %get-tuple-element.205.refs_0_), channel_id=1, source_target_pairs={{0,16},{4,20},{8,24},{12,28},{16,0},{20,4},{24,8},{28,12},{1,17},{... | collective-permute-start | bytes 1572872 | tf_op jit(solution)/shard_map/ppermute | solution.py:70
  47.5 21.9 %collective-permute-start.6 = (bf16[128,2048]{1,0:T(8,128)(2,1)S(1)}, bf16[128,2048]{1,0:T(8,128)(2,1)S(1)}, u32[]{:S(2)}, u32[]{:S(2)}) collective-permute-start(bf16[128,2048]{1,0:T(8,128)(2,1)S(1)} %collective-permute-done.2.refs_2_), channel_id=1, source_target_pairs={{0,16},{4,20},{8,24},{12,28},{16,0},{20,4},{24,8},{28,12},{1,17},{... | collective-permute-start | bytes 1572872 | tf_op jit(solution)/shard_map/ppermute | solution.py:70
  48.3 21.2 %collective-permute-start.7 = (bf16[128,2048]{1,0:T(8,128)(2,1)}, bf16[128,2048]{1,0:T(8,128)(2,1)}, u32[]{:S(2)}, u32[]{:S(2)}) collective-permute-start(bf16[128,2048]{1,0:T(8,128)(2,1)} %collective-permute-done.5.refs_5_), channel_id=1, source_target_pairs={{0,8},{4,12},{8,0},{12,4},{16,24},{20,28},{24,16},{28,20},{1,9},{5... | collective-permute-start | bytes 1572872 | tf_op jit(solution)/shard_map/ppermute | solution.py:70
  49.7 20.2 %collective-permute-start.8 = (bf16[128,2048]{1,0:T(8,128)(2,1)S(1)}, bf16[128,2048]{1,0:T(8,128)(2,1)S(1)}, u32[]{:S(2)}, u32[]{:S(2)}) collective-permute-start(bf16[128,2048]{1,0:T(8,128)(2,1)S(1)} %collective-permute-done.2.refs_2_), channel_id=1, source_target_pairs={{0,4},{4,0},{8,12},{12,8},{16,20},{20,16},{24,28},{28,24},{1,5},{5... | collective-permute-start | bytes 1572872 | tf_op jit(solution)/shard_map/ppermute | solution.py:70
  76.4 34.4 %all-to-all-start.1 = ((bf16[8,64,1408]{2,1,0:T(8,128)(2,1)}), bf16[8,64,1408]{2,1,0:T(8,128)(2,1)}, u32[]{:S(2)}, u32[]{:S(2)}) async-start(bf16[8,64,1408]{2,1,0:T(8,128)(2,1)} %split_columns.3), calls=%async_computation.1 | async-start | bytes 2883584 | tf_op jit(solution)/shard_map/all_to_all | solution.py:262
  80.8 137.2 %all-gather.13.cloned.1.call-start = ((), (), s32[]{:S(2)}) async-start(), calls=%async_computation.15 | async-start | bytes 7208960 | tf_op jit(solution)/shard_map/all_gather | solution.py:818
  83.2 27.7 %collective-permute-start.16 = (bf16[128,2048]{1,0:T(8,128)(2,1)}, bf16[128,2048]{1,0:T(8,128)(2,1)}, u32[]{:S(2)}, u32[]{:S(2)}) collective-permute-start(bf16[128,2048]{1,0:T(8,128)(2,1)} %get-tuple-element.238), channel_id=1, source_target_pairs={{0,8},{4,12},{8,0},{12,4},{16,24},{20,28},{24,16},{28,20},{1,9},{5... | collective-permute-start | bytes 1572872 | tf_op jit(solution)/shard_map/ppermute | solution.py:70
  85.0 25.8 %collective-permute-start.17 = (bf16[128,2048]{1,0:T(8,128)(2,1)}, bf16[128,2048]{1,0:T(8,128)(2,1)}, u32[]{:S(2)}, u32[]{:S(2)}) collective-permute-start(bf16[128,2048]{1,0:T(8,128)(2,1)} %get-tuple-element.239), channel_id=1, source_target_pairs={{0,16},{4,20},{8,24},{12,28},{16,0},{20,4},{24,8},{28,12},{1,17},{... | collective-permute-start | bytes 1572872 | tf_op jit(solution)/shard_map/ppermute | solution.py:70
  110.8 187.0 %all-gather.9.cloned.1.call-start = ((), (), s32[]{:S(2)}) async-start(), calls=%async_computation.9 | async-start | bytes 3604480 | tf_op jit(solution)/shard_map/all_gather | solution.py:843
  113.9 16.6 %collective-permute-start.20 = (bf16[128,2048]{1,0:T(8,128)(2,1)}, bf16[128,2048]{1,0:T(8,128)(2,1)}, u32[]{:S(2)}, u32[]{:S(2)}) collective-permute-start(bf16[128,2048]{1,0:T(8,128)(2,1)} %get-tuple-element.239), channel_id=1, source_target_pairs={{0,8},{4,12},{8,0},{12,4},{16,24},{20,28},{24,16},{28,20},{1,9},{5... | collective-permute-start | bytes 1572872 | tf_op jit(solution)/shard_map/ppermute | solution.py:70
  115.3 15.2 %collective-permute-start.21 = (bf16[128,2048]{1,0:T(8,128)(2,1)}, bf16[128,2048]{1,0:T(8,128)(2,1)S(1)}, u32[]{:S(2)}, u32[]{:S(2)}) collective-permute-start(bf16[128,2048]{1,0:T(8,128)(2,1)} %get-tuple-element.238), channel_id=1, source_target_pairs={{0,16},{4,20},{8,24},{12,28},{16,0},{20,4},{24,8},{28,12},{1,17},{... | collective-permute-start | bytes 1572872 | tf_op jit(solution)/shard_map/ppermute | solution.py:70
  130.6 38.4 %collective-permute-start.22 = (bf16[128,2048]{1,0:T(8,128)(2,1)}, bf16[128,2048]{1,0:T(8,128)(2,1)}, u32[]{:S(2)}, u32[]{:S(2)}) collective-permute-start(bf16[128,2048]{1,0:T(8,128)(2,1)} %collective-permute-done.16), channel_id=1, source_target_pairs={{0,16},{4,20},{8,24},{12,28},{16,0},{20,4},{24,8},{28,12},{1,17},{... | collective-permute-start | bytes 1572872 | tf_op jit(solution)/shard_map/ppermute | solution.py:70
  131.9 37.1 %collective-permute-start.23 = (bf16[128,2048]{1,0:T(8,128)(2,1)}, bf16[128,2048]{1,0:T(8,128)(2,1)}, u32[]{:S(2)}, u32[]{:S(2)}) collective-permute-start(bf16[128,2048]{1,0:T(8,128)(2,1)} %collective-permute-done.17), channel_id=1, source_target_pairs={{0,8},{4,12},{8,0},{12,4},{16,24},{20,28},{24,16},{28,20},{1,9},{5... | collective-permute-start | bytes 1572872 | tf_op jit(solution)/shard_map/ppermute | solution.py:70
  173.4 276.7 %reduce-scatter.5.cloned.1.call-start = ((), (), s32[]{:S(2)}) async-start(), calls=%async_computation.10 | async-start | bytes 3604480 | tf_op jit(solution)/shard_map/reduce_scatter | solution.py:862
  173.6 18.0 %collective-permute-start.27 = (bf16[128,2048]{1,0:T(8,128)(2,1)}, bf16[128,2048]{1,0:T(8,128)(2,1)S(1)}, u32[]{:S(2)}, u32[]{:S(2)}) collective-permute-start(bf16[128,2048]{1,0:T(8,128)(2,1)} %collective-permute-done.16), channel_id=1, source_target_pairs={{0,4},{4,0},{8,12},{12,8},{16,20},{20,16},{24,28},{28,24},{1,5},{5... | collective-permute-start | bytes 1572872 | tf_op jit(solution)/shard_map/ppermute | solution.py:70
  174.2 35.9 %collective-permute-start.30 = (bf16[128,2048]{1,0:T(8,128)(2,1)}, bf16[128,2048]{1,0:T(8,128)(2,1)S(1)}, u32[]{:S(2)}, u32[]{:S(2)}) collective-permute-start(bf16[128,2048]{1,0:T(8,128)(2,1)} %collective-permute-done.17), channel_id=1, source_target_pairs={{0,4},{4,0},{8,12},{12,8},{16,20},{20,16},{24,28},{28,24},{1,5},{5... | collective-permute-start | bytes 1572872 | tf_op jit(solution)/shard_map/ppermute | solution.py:70
  174.3 19.5 %collective-permute-start.28 = (bf16[128,2048]{1,0:T(8,128)(2,1)}, bf16[128,2048]{1,0:T(8,128)(2,1)S(1)}, u32[]{:S(2)}, u32[]{:S(2)}) collective-permute-start(bf16[128,2048]{1,0:T(8,128)(2,1)} %collective-permute-done.20), channel_id=1, source_target_pairs={{0,4},{4,0},{8,12},{12,8},{16,20},{20,16},{24,28},{28,24},{1,5},{5... | collective-permute-start | bytes 1572872 | tf_op jit(solution)/shard_map/ppermute | solution.py:70
  174.7 19.9 %collective-permute-start.29 = (bf16[128,2048]{1,0:T(8,128)(2,1)S(1)}, bf16[128,2048]{1,0:T(8,128)(2,1)S(1)}, u32[]{:S(2)}, u32[]{:S(2)}) collective-permute-start(bf16[128,2048]{1,0:T(8,128)(2,1)S(1)} %collective-permute-done.21), channel_id=1, source_target_pairs={{0,4},{4,0},{8,12},{12,8},{16,20},{20,16},{24,28},{28,24},{1,5},{5... | collective-permute-start | bytes 1572872 | tf_op jit(solution)/shard_map/ppermute | solution.py:70
  185.9 25.5 %collective-permute-start.31 = (bf16[128,2048]{1,0:T(8,128)(2,1)}, bf16[128,2048]{1,0:T(8,128)(2,1)S(1)}, u32[]{:S(2)}, u32[]{:S(2)}) collective-permute-start(bf16[128,2048]{1,0:T(8,128)(2,1)} %collective-permute-done.22), channel_id=1, source_target_pairs={{0,4},{4,0},{8,12},{12,8},{16,20},{20,16},{24,28},{28,24},{1,5},{5... | collective-permute-start | bytes 1572872 | tf_op jit(solution)/shard_map/ppermute | solution.py:70
  193.8 20.2 %collective-permute-start.32 = (bf16[128,2048]{1,0:T(8,128)(2,1)}, bf16[128,2048]{1,0:T(8,128)(2,1)S(1)}, u32[]{:S(2)}, u32[]{:S(2)}) collective-permute-start(bf16[128,2048]{1,0:T(8,128)(2,1)} %collective-permute-done.23), channel_id=1, source_target_pairs={{0,4},{4,0},{8,12},{12,8},{16,20},{20,16},{24,28},{28,24},{1,5},{5... | collective-permute-start | bytes 1572872 | tf_op jit(solution)/shard_map/ppermute | solution.py:70
  205.8 17.9 %collective-permute-start.25 = (bf16[128,2048]{1,0:T(8,128)(2,1)S(1)}, bf16[128,2048]{1,0:T(8,128)(2,1)S(1)}, u32[]{:S(2)}, u32[]{:S(2)}) collective-permute-start(bf16[128,2048]{1,0:T(8,128)(2,1)S(1)} %get-tuple-element.236), channel_id=1, source_target_pairs={{0,8},{4,12},{8,0},{12,4},{16,24},{20,28},{24,16},{28,20},{1,9},{5... | collective-permute-start | bytes 1572872 | tf_op jit(solution)/shard_map/ppermute | solution.py:70
  209.2 15.1 %collective-permute-start.26 = (bf16[128,2048]{1,0:T(8,128)(2,1)}, bf16[128,2048]{1,0:T(8,128)(2,1)}, u32[]{:S(2)}, u32[]{:S(2)}) collective-permute-start(bf16[128,2048]{1,0:T(8,128)(2,1)} %get-tuple-element.237), channel_id=1, source_target_pairs={{0,16},{4,20},{8,24},{12,28},{16,0},{20,4},{24,8},{28,12},{1,17},{... | collective-permute-start | bytes 1572872 | tf_op jit(solution)/shard_map/ppermute | solution.py:70
  210.1 24.3 %collective-permute-start.34 = (bf16[128,2048]{1,0:T(8,128)(2,1)S(1)}, bf16[128,2048]{1,0:T(8,128)(2,1)}, u32[]{:S(2)}, u32[]{:S(2)}) collective-permute-start(bf16[128,2048]{1,0:T(8,128)(2,1)S(1)} %add_convert_fusion.7), channel_id=1, source_target_pairs={{0,16},{4,20},{8,24},{12,28},{16,0},{20,4},{24,8},{28,12},{1,17},{... | collective-permute-start | bytes 1572872 | tf_op jit(solution)/shard_map/ppermute | solution.py:70
  211.4 23.0 %collective-permute-start.36 = (bf16[128,2048]{1,0:T(8,128)(2,1)S(1)}, bf16[128,2048]{1,0:T(8,128)(2,1)}, u32[]{:S(2)}, u32[]{:S(2)}) collective-permute-start(bf16[128,2048]{1,0:T(8,128)(2,1)S(1)} %add_convert_fusion.6), channel_id=1, source_target_pairs={{0,8},{4,12},{8,0},{12,4},{16,24},{20,28},{24,16},{28,20},{1,9},{5... | collective-permute-start | bytes 1572872 | tf_op jit(solution)/shard_map/ppermute | solution.py:70
  238.8 14.8 %collective-permute-start.37 = (bf16[128,2048]{1,0:T(8,128)(2,1)S(1)}, bf16[128,2048]{1,0:T(8,128)(2,1)S(1)}, u32[]{:S(2)}, u32[]{:S(2)}) collective-permute-start(bf16[128,2048]{1,0:T(8,128)(2,1)S(1)} %get-tuple-element.260.refs_0_), channel_id=1, source_target_pairs={{0,8},{4,12},{8,0},{12,4},{16,24},{20,28},{24,16},{28,20},{1,9},{5... | collective-permute-start | bytes 1572872 | tf_op jit(solution)/shard_map/ppermute | solution.py:70
  239.6 14.8 %collective-permute-start.39 = (bf16[128,2048]{1,0:T(8,128)(2,1)S(1)}, bf16[128,2048]{1,0:T(8,128)(2,1)S(1)}, u32[]{:S(2)}, u32[]{:S(2)}) collective-permute-start(bf16[128,2048]{1,0:T(8,128)(2,1)S(1)} %get-tuple-element.261.refs_1_), channel_id=1, source_target_pairs={{0,16},{4,20},{8,24},{12,28},{16,0},{20,4},{24,8},{28,12},{1,17},{... | collective-permute-start | bytes 1572872 | tf_op jit(solution)/shard_map/ppermute | solution.py:70
  241.0 22.9 %collective-permute-start.43 = (bf16[128,2048]{1,0:T(8,128)(2,1)S(1)}, bf16[128,2048]{1,0:T(8,128)(2,1)S(1)}, u32[]{:S(2)}, u32[]{:S(2)}) collective-permute-start(bf16[128,2048]{1,0:T(8,128)(2,1)S(1)} %get-tuple-element.261.refs_1_), channel_id=1, source_target_pairs={{0,8},{4,12},{8,0},{12,4},{16,24},{20,28},{24,16},{28,20},{1,9},{5... | collective-permute-start | bytes 1572872 | tf_op jit(solution)/shard_map/ppermute | solution.py:70
  241.7 22.6 %collective-permute-start.44 = (bf16[128,2048]{1,0:T(8,128)(2,1)S(1)}, bf16[128,2048]{1,0:T(8,128)(2,1)S(1)}, u32[]{:S(2)}, u32[]{:S(2)}) collective-permute-start(bf16[128,2048]{1,0:T(8,128)(2,1)S(1)} %get-tuple-element.260.refs_0_), channel_id=1, source_target_pairs={{0,16},{4,20},{8,24},{12,28},{16,0},{20,4},{24,8},{28,12},{1,17},{... | collective-permute-start | bytes 1572872 | tf_op jit(solution)/shard_map/ppermute | solution.py:70
  264.4 21.7 %collective-permute-start.38 = (bf16[128,2048]{1,0:T(8,128)(2,1)S(1)}, bf16[128,2048]{1,0:T(8,128)(2,1)S(1)}, u32[]{:S(2)}, u32[]{:S(2)}) collective-permute-start(bf16[128,2048]{1,0:T(8,128)(2,1)S(1)} %collective-permute-done.37.refs_2_), channel_id=1, source_target_pairs={{0,16},{4,20},{8,24},{12,28},{16,0},{20,4},{24,8},{28,12},{1,17},{... | collective-permute-start | bytes 1572872 | tf_op jit(solution)/shard_map/ppermute | solution.py:70
  265.7 20.4 %collective-permute-start.40 = (bf16[128,2048]{1,0:T(8,128)(2,1)S(1)}, bf16[128,2048]{1,0:T(8,128)(2,1)S(1)}, u32[]{:S(2)}, u32[]{:S(2)}) collective-permute-start(bf16[128,2048]{1,0:T(8,128)(2,1)S(1)} %collective-permute-done.39.refs_5_), channel_id=1, source_target_pairs={{0,8},{4,12},{8,0},{12,4},{16,24},{20,28},{24,16},{28,20},{1,9},{5... | collective-permute-start | bytes 1572872 | tf_op jit(solution)/shard_map/ppermute | solution.py:70
  332.6 168.6 %reduce-scatter.7.cloned.1.call-start = ((), (), s32[]{:S(2)}) async-start(), calls=%async_computation.11 | async-start | bytes 7208960 | tf_op jit(solution)/shard_map/reduce_scatter | solution.py:862
  345.6 15.0 %collective-permute-start.53 = (bf16[128,2048]{1,0:T(8,128)(2,1)}, bf16[128,2048]{1,0:T(8,128)(2,1)S(1)}, u32[]{:S(2)}, u32[]{:S(2)}) collective-permute-start(bf16[128,2048]{1,0:T(8,128)(2,1)} %get-tuple-element.280), channel_id=1, source_target_pairs={{0,8},{4,12},{8,0},{12,4},{16,24},{20,28},{24,16},{28,20},{1,9},{5... | collective-permute-start | bytes 1572872 | tf_op jit(solution)/shard_map/ppermute | solution.py:70
  346.9 15.1 %collective-permute-start.55 = (bf16[128,2048]{1,0:T(8,128)(2,1)}, bf16[128,2048]{1,0:T(8,128)(2,1)S(1)}, u32[]{:S(2)}, u32[]{:S(2)}) collective-permute-start(bf16[128,2048]{1,0:T(8,128)(2,1)} %get-tuple-element.282), channel_id=1, source_target_pairs={{0,16},{4,20},{8,24},{12,28},{16,0},{20,4},{24,8},{28,12},{1,17},{... | collective-permute-start | bytes 1572872 | tf_op jit(solution)/shard_map/ppermute | solution.py:70
  347.6 35.5 %collective-permute-start.52 = (bf16[128,2048]{1,0:T(8,128)(2,1)S(1)}, bf16[128,2048]{1,0:T(8,128)(2,1)S(1)}, u32[]{:S(2)}, u32[]{:S(2)}) collective-permute-start(bf16[128,2048]{1,0:T(8,128)(2,1)S(1)} %get-tuple-element.278), channel_id=1, source_target_pairs={{0,8},{4,12},{8,0},{12,4},{16,24},{20,28},{24,16},{28,20},{1,9},{5... | collective-permute-start | bytes 1572872 | tf_op jit(solution)/shard_map/ppermute | solution.py:70
  348.8 34.3 %collective-permute-start.57 = (bf16[128,2048]{1,0:T(8,128)(2,1)}, bf16[128,2048]{1,0:T(8,128)(2,1)S(1)}, u32[]{:S(2)}, u32[]{:S(2)}) collective-permute-start(bf16[128,2048]{1,0:T(8,128)(2,1)} %get-tuple-element.283), channel_id=1, source_target_pairs={{0,16},{4,20},{8,24},{12,28},{16,0},{20,4},{24,8},{28,12},{1,17},{... | collective-permute-start | bytes 1572872 | tf_op jit(solution)/shard_map/ppermute | solution.py:70
  360.7 22.7 %collective-permute-start.54 = (bf16[128,2048]{1,0:T(8,128)(2,1)S(1)}, bf16[128,2048]{1,0:T(8,128)(2,1)S(1)}, u32[]{:S(2)}, u32[]{:S(2)}) collective-permute-start(bf16[128,2048]{1,0:T(8,128)(2,1)S(1)} %add_convert_fusion.5), channel_id=1, source_target_pairs={{0,16},{4,20},{8,24},{12,28},{16,0},{20,4},{24,8},{28,12},{1,17},{... | collective-permute-start | bytes 1572872 | tf_op jit(solution)/shard_map/ppermute | solution.py:70
  362.1 21.4 %collective-permute-start.56 = (bf16[128,2048]{1,0:T(8,128)(2,1)S(1)}, bf16[128,2048]{1,0:T(8,128)(2,1)S(1)}, u32[]{:S(2)}, u32[]{:S(2)}) collective-permute-start(bf16[128,2048]{1,0:T(8,128)(2,1)S(1)} %add_convert_fusion.4), channel_id=1, source_target_pairs={{0,8},{4,12},{8,0},{12,4},{16,24},{20,28},{24,16},{28,20},{1,9},{5... | collective-permute-start | bytes 1572872 | tf_op jit(solution)/shard_map/ppermute | solution.py:70
  384.4 152.1 %reduce-scatter.9.cloned.1.call-start = ((), (), s32[]{:S(2)}) async-start(), calls=%async_computation.12 | async-start | bytes 1310720 | tf_op jit(solution)/shard_map/reduce_scatter | solution.py:862
  397.3 16.2 %collective-permute-start.66 = (bf16[1024,2048]{1,0:T(8,128)(2,1)S(1)}, bf16[1024,2048]{1,0:T(8,128)(2,1)S(1)}, u32[]{:S(2)}, u32[]{:S(2)}) collective-permute-start(bf16[1024,2048]{1,0:T(8,128)(2,1)S(1)} %convolution_convert_fusion.1), channel_id=1, source_target_pairs={{0,4},{4,0},{8,12},{12,8},{16,20},{20,16},{24,28},{28,24},{1,5},{5... | collective-permute-start | bytes 12582920 | tf_op jit(solution)/shard_map/ppermute | solution.py:70
  397.5 14.8 %collective-permute-start.58 = (bf16[128,2048]{1,0:T(8,128)(2,1)S(1)}, bf16[128,2048]{1,0:T(8,128)(2,1)S(1)}, u32[]{:S(2)}, u32[]{:S(2)}) collective-permute-start(bf16[128,2048]{1,0:T(8,128)(2,1)S(1)} %get-tuple-element.292.refs_0_), channel_id=1, source_target_pairs={{0,8},{4,12},{8,0},{12,4},{16,24},{20,28},{24,16},{28,20},{1,9},{5... | collective-permute-start | bytes 1572872 | tf_op jit(solution)/shard_map/ppermute | solution.py:70
  398.7 14.8 %collective-permute-start.60 = (bf16[128,2048]{1,0:T(8,128)(2,1)S(1)}, bf16[128,2048]{1,0:T(8,128)(2,1)S(1)}, u32[]{:S(2)}, u32[]{:S(2)}) collective-permute-start(bf16[128,2048]{1,0:T(8,128)(2,1)S(1)} %get-tuple-element.293.refs_1_), channel_id=1, source_target_pairs={{0,16},{4,20},{8,24},{12,28},{16,0},{20,4},{24,8},{28,12},{1,17},{... | collective-permute-start | bytes 1572872 | tf_op jit(solution)/shard_map/ppermute | solution.py:70
  399.6 24.5 %collective-permute-start.64 = (bf16[128,2048]{1,0:T(8,128)(2,1)S(1)}, bf16[128,2048]{1,0:T(8,128)(2,1)S(1)}, u32[]{:S(2)}, u32[]{:S(2)}) collective-permute-start(bf16[128,2048]{1,0:T(8,128)(2,1)S(1)} %get-tuple-element.293.refs_1_), channel_id=1, source_target_pairs={{0,8},{4,12},{8,0},{12,4},{16,24},{20,28},{24,16},{28,20},{1,9},{5... | collective-permute-start | bytes 1572872 | tf_op jit(solution)/shard_map/ppermute | solution.py:70
  400.8 23.3 %collective-permute-start.65 = (bf16[128,2048]{1,0:T(8,128)(2,1)S(1)}, bf16[128,2048]{1,0:T(8,128)(2,1)S(1)}, u32[]{:S(2)}, u32[]{:S(2)}) collective-permute-start(bf16[128,2048]{1,0:T(8,128)(2,1)S(1)} %get-tuple-element.292.refs_0_), channel_id=1, source_target_pairs={{0,16},{4,20},{8,24},{12,28},{16,0},{20,4},{24,8},{28,12},{1,17},{... | collective-permute-start | bytes 1572872 | tf_op jit(solution)/shard_map/ppermute | solution.py:70
  424.7 15.2 %collective-permute-start.59 = (bf16[128,2048]{1,0:T(8,128)(2,1)S(1)}, bf16[128,2048]{1,0:T(8,128)(2,1)S(1)}, u32[]{:S(2)}, u32[]{:S(2)}) collective-permute-start(bf16[128,2048]{1,0:T(8,128)(2,1)S(1)} %collective-permute-done.58.refs_2_), channel_id=1, source_target_pairs={{0,16},{4,20},{8,24},{12,28},{16,0},{20,4},{24,8},{28,12},{1,17},{... | collective-permute-start | bytes 1572872 | tf_op jit(solution)/shard_map/ppermute | solution.py:70
  450.1 49.4 %collective-permute-start.73 = (bf16[128,2048]{1,0:T(8,128)(2,1)}, bf16[128,2048]{1,0:T(8,128)(2,1)S(1)}, u32[]{:S(2)}, u32[]{:S(2)}) collective-permute-start(bf16[128,2048]{1,0:T(8,128)(2,1)} %get-tuple-element.327), channel_id=1, source_target_pairs={{0,8},{4,12},{8,0},{12,4},{16,24},{20,28},{24,16},{28,20},{1,9},{5... | collective-permute-start | bytes 1572872 | tf_op jit(solution)/shard_map/ppermute | solution.py:70
  450.9 48.6 %collective-permute-start.74 = (bf16[128,2048]{1,0:T(8,128)(2,1)}, bf16[128,2048]{1,0:T(8,128)(2,1)S(1)}, u32[]{:S(2)}, u32[]{:S(2)}) collective-permute-start(bf16[128,2048]{1,0:T(8,128)(2,1)} %get-tuple-element.328), channel_id=1, source_target_pairs={{0,16},{4,20},{8,24},{12,28},{16,0},{20,4},{24,8},{28,12},{1,17},{... | collective-permute-start | bytes 1572872 | tf_op jit(solution)/shard_map/ppermute | solution.py:70
  451.9 47.6 %collective-permute-start.75 = (bf16[128,2048]{1,0:T(8,128)(2,1)S(1)}, bf16[128,2048]{1,0:T(8,128)(2,1)S(1)}, u32[]{:S(2)}, u32[]{:S(2)}) collective-permute-start(bf16[128,2048]{1,0:T(8,128)(2,1)S(1)} %get-tuple-element.329), channel_id=1, source_target_pairs={{0,8},{4,12},{8,0},{12,4},{16,24},{20,28},{24,16},{28,20},{1,9},{5... | collective-permute-start | bytes 1572872 | tf_op jit(solution)/shard_map/ppermute | solution.py:70
  452.8 48.4 %collective-permute-start.76 = (bf16[128,2048]{1,0:T(8,128)(2,1)S(1)}, bf16[128,2048]{1,0:T(8,128)(2,1)}, u32[]{:S(2)}, u32[]{:S(2)}) collective-permute-start(bf16[128,2048]{1,0:T(8,128)(2,1)S(1)} %copy-done.62), channel_id=1, source_target_pairs={{0,16},{4,20},{8,24},{12,28},{16,0},{20,4},{24,8},{28,12},{1,17},{... | collective-permute-start | bytes 1572872 | tf_op jit(solution)/shard_map/ppermute | solution.py:70
  509.1 99.3 %reduce-scatter.11.cloned.1.call-start = ((), (), s32[]{:S(2)}) async-start(), calls=%async_computation.13 | async-start | bytes 3932160 | tf_op jit(solution)/shard_map/reduce_scatter | solution.py:862
  536.5 15.2 %collective-permute-start.82 = (bf16[128,2048]{1,0:T(8,128)(2,1)}, bf16[128,2048]{1,0:T(8,128)(2,1)}, u32[]{:S(2)}, u32[]{:S(2)}) collective-permute-start(bf16[128,2048]{1,0:T(8,128)(2,1)} %get-tuple-element.362), channel_id=1, source_target_pairs={{0,8},{4,12},{8,0},{12,4},{16,24},{20,28},{24,16},{28,20},{1,9},{5... | collective-permute-start | bytes 1572872 | tf_op jit(solution)/shard_map/ppermute | solution.py:70
  540.0 27.9 %collective-permute-start.80 = (bf16[128,2048]{1,0:T(8,128)(2,1)}, bf16[128,2048]{1,0:T(8,128)(2,1)}, u32[]{:S(2)}, u32[]{:S(2)}) collective-permute-start(bf16[128,2048]{1,0:T(8,128)(2,1)} %add_convert_fusion.3), channel_id=1, source_target_pairs={{0,16},{4,20},{8,24},{12,28},{16,0},{20,4},{24,8},{28,12},{1,17},{... | collective-permute-start | bytes 1572872 | tf_op jit(solution)/shard_map/ppermute | solution.py:70
  541.4 24.8 %collective-permute-start.84 = (bf16[128,2048]{1,0:T(8,128)(2,1)}, bf16[128,2048]{1,0:T(8,128)(2,1)S(1)}, u32[]{:S(2)}, u32[]{:S(2)}) collective-permute-start(bf16[128,2048]{1,0:T(8,128)(2,1)} %get-tuple-element.364), channel_id=1, source_target_pairs={{0,16},{4,20},{8,24},{12,28},{16,0},{20,4},{24,8},{28,12},{1,17},{... | collective-permute-start | bytes 1572872 | tf_op jit(solution)/shard_map/ppermute | solution.py:70
  542.9 31.5 %collective-permute-start.81 = (bf16[128,2048]{1,0:T(8,128)(2,1)}, bf16[128,2048]{1,0:T(8,128)(2,1)}, u32[]{:S(2)}, u32[]{:S(2)}) collective-permute-start(bf16[128,2048]{1,0:T(8,128)(2,1)} %add_convert_fusion.2), channel_id=1, source_target_pairs={{0,8},{4,12},{8,0},{12,4},{16,24},{20,28},{24,16},{28,20},{1,9},{5... | collective-permute-start | bytes 1572872 | tf_op jit(solution)/shard_map/ppermute | solution.py:70
  543.5 31.0 %collective-permute-start.78 = (bf16[128,2048]{1,0:T(8,128)(2,1)S(1)}, bf16[128,2048]{1,0:T(8,128)(2,1)S(1)}, u32[]{:S(2)}, u32[]{:S(2)}) collective-permute-start(bf16[128,2048]{1,0:T(8,128)(2,1)S(1)} %get-tuple-element.343), channel_id=1, source_target_pairs={{0,8},{4,12},{8,0},{12,4},{16,24},{20,28},{24,16},{28,20},{1,9},{5... | collective-permute-start | bytes 1572872 | tf_op jit(solution)/shard_map/ppermute | solution.py:70
  544.9 48.1 %all-to-all-start.2 = ((bf16[8,64,1408]{2,1,0:T(8,128)(2,1)}), bf16[8,64,1408]{2,1,0:T(8,128)(2,1)}, u32[]{:S(2)}, u32[]{:S(2)}) async-start(bf16[8,64,1408]{2,1,0:T(8,128)(2,1)} %bitcast.68), calls=%async_computation.5 | async-start | bytes 2883584 | tf_op jit(solution)/shard_map/all_to_all | solution.py:262
  551.7 41.4 %collective-permute-start.79 = (bf16[128,2048]{1,0:T(8,128)(2,1)}, bf16[128,2048]{1,0:T(8,128)(2,1)}, u32[]{:S(2)}, u32[]{:S(2)}) collective-permute-start(bf16[128,2048]{1,0:T(8,128)(2,1)} %get-tuple-element.344), channel_id=1, source_target_pairs={{0,16},{4,20},{8,24},{12,28},{16,0},{20,4},{24,8},{28,12},{1,17},{... | collective-permute-start | bytes 1572872 | tf_op jit(solution)/shard_map/ppermute | solution.py:70
  566.3 36.3 %collective-permute-start.83 = (bf16[128,2048]{1,0:T(8,128)(2,1)}, bf16[128,2048]{1,0:T(8,128)(2,1)S(1)}, u32[]{:S(2)}, u32[]{:S(2)}) collective-permute-start(bf16[128,2048]{1,0:T(8,128)(2,1)} %add_convert_fusion.1), channel_id=1, source_target_pairs={{0,16},{4,20},{8,24},{12,28},{16,0},{20,4},{24,8},{28,12},{1,17},{... | collective-permute-start | bytes 1572872 | tf_op jit(solution)/shard_map/ppermute | solution.py:70
  567.9 34.7 %collective-permute-start.85 = (bf16[128,2048]{1,0:T(8,128)(2,1)S(1)}, bf16[128,2048]{1,0:T(8,128)(2,1)S(1)}, u32[]{:S(2)}, u32[]{:S(2)}) collective-permute-start(bf16[128,2048]{1,0:T(8,128)(2,1)S(1)} %add_convert_fusion), channel_id=1, source_target_pairs={{0,8},{4,12},{8,0},{12,4},{16,24},{20,28},{24,16},{28,20},{1,9},{5... | collective-permute-start | bytes 1572872 | tf_op jit(solution)/shard_map/ppermute | solution.py:70
  608.5 20.9 %all-to-all-start.3 = ((bf16[8,64,768]{2,1,0:T(8,128)(2,1)}), bf16[8,64,768]{2,1,0:T(8,128)(2,1)S(1)}, u32[]{:S(2)}, u32[]{:S(2)}) async-start(bf16[8,64,768]{2,1,0:T(8,128)(2,1)} %bitcast.76), calls=%async_computation.7 | async-start | bytes 1572864 | tf_op jit(solution)/shard_map/all_to_all | solution.py:262
  (106 other events, 841.6 us)
Sparse Core Ops, SparseCore 0:
  10.2 31.5 all-gather.6
  43.9 63.4 all-gather.10
  111.0 106.9 all-gather.12
  220.0 57.4 all-gather.8
  332.7 56.4 reduce-scatter.4
  391.4 102.0 reduce-scatter.6
  509.3 27.2 reduce-scatter.8
  538.9 58.8 reduce-scatter.10

commit v3 on v2

--- a/solution.py
+++ b/solution.py
@@ -28,7 +28,8 @@
 LANES = 128
 SCALE = HEAD_DIM**-0.5
 SCALE_LOG2 = SCALE * math.log2(math.e)
-VMEM_LIMIT = 52 * 1024 * 1024
+VMEM_LIMIT = 32 * 1024 * 1024
+VMEM_MOST = 40 * 1024 * 1024
 BF16 = jnp.bfloat16
 SHORT = pl.CostEstimate(flops=1000000, bytes_accessed=1000000, transcendentals=0)
 F32 = jnp.float32
@@ -92,14 +93,17 @@
     return (begun[:-2] + tied[:2], *tied[2:])
 
 
-def gather_start(top, low):
+def gather_start(top, low, strict=False):
     if not cube():
         return (lax.all_gather(jnp.concatenate([top, low]), "ctx", axis=0, tiled=True),)
     x_top = swap(top, 2)
     y_low = swap(low, 4)
     c_top = swap(top, 1)
     c_low = swap(low, 1)
-    c_top, c_low, top, low = tie(c_top, c_low, top, low)
+    if strict:
+        x_top, y_low, top, low = tie(x_top, y_low, top, low)
+    else:
+        c_top, c_low, top, low = tie(c_top, c_low, top, low)
     return (top, low, c_top, c_low, x_top, y_low, swap(low, 2), swap(top, 4))
 
 
@@ -179,11 +183,14 @@
     return tuple(chip_sums(left, right, right_dim, away))
 
 
-def scatter_start(sums):
+def scatter_start(sums, urgent=True):
     if not cube():
         return sums
     own, x_top, x_low, y_top, y_low, d_top, d_low = sums
-    return (own, x_low, y_top, swap(d_top, 2), swap(d_low, 4), swap(x_top, 2), swap(y_low, 4))
+    d_top, d_low = swap(d_top, 2), swap(d_low, 4)
+    if urgent:
+        d_top, d_low, x_top, y_low = tie(d_top, d_low, x_top, y_low)
+    return (own, x_low, y_top, d_top, d_low, swap(x_top, 2), swap(y_low, 4))
 
 
 def scatter_end(begun):
@@ -258,6 +265,11 @@
     return relayout(kernel, (share,), (rows, parts * size * width), "join_columns")
 
 
+def squared(share):
+    share = share.astype(F32)
+    return jnp.sum(share * share)
+
+
 def exchange(split):
     return lax.all_to_all(split, "ctx", 0, 0)
 
@@ -273,6 +285,23 @@
 
 def aligned(index, step=BLOCK):
     return pl.ds(pl.multiple_of(index * step, step), step)
+
+
+def span(start, count):
+    return pl.ds(pl.multiple_of(start * BLOCK, BLOCK), count * BLOCK)
+
+
+def over_blocks(full, step, state):
+    for count in (4, 2, 1):
+        start = full - lax.rem(full, 2 * count) if count < 4 else 0
+        steps = lax.rem(full, 2 * count) // count if count < 4 else full // count
+        state = lax.fori_loop(
+            0,
+            steps,
+            lambda i, state, start=start, count=count: step(start + i * count, count, state),
+            state,
+        )
+    return state
 
 
 def turn(field, cosine, sine):
@@ -351,34 +380,35 @@
         for p in range(pairs):
             heads.extend(split_rows(transposed(q_ref[place, lanes[p]])))
 
+        def keys_at(index, number):
+            return span(key_block(code, index, prompt_blocks), number)
+
         def scores(slot, at, mask, tops):
             fresh = []
             for h in range(count):
                 logits = dot(k_ref[at, lanes[h // 2]], heads[h], 1, 0) * SCALE_LOG2
                 if mask is not None:
                     logits = jnp.where(mask, logits, MASKED)
-                s_ref[h, aligned(slot), :] = logits
+                s_ref[h, slot, :] = logits
                 fresh.append(jnp.maximum(tops[h], jnp.max(fold(logits), axis=0)))
             return tuple(fresh)
 
         full = full_blocks(code, prompt_blocks)
-        tops = scores(full, place, allowed, (jnp.full((8, BLOCK), MASKED, F32),) * count)
-        tops = lax.fori_loop(
-            0,
+        tops = scores(span(full, 1), place, allowed, (jnp.full((8, BLOCK), MASKED, F32),) * count)
+        tops = over_blocks(
             full,
-            lambda index, tops: scores(
-                index, aligned(key_block(code, index, prompt_blocks)), None, tops
+            lambda index, number, tops: scores(
+                span(index, number), keys_at(index, number), None, tops
             ),
             tops,
         )
         tops = [jnp.max(top, axis=0, keepdims=True) for top in tops]
 
-        def step(index, state):
-            at = aligned(jnp.where(index == full, code, key_block(code, index, prompt_blocks)))
+        def step(slot, at, state):
             fresh = []
             for h in range(count):
                 total, mixed = state[h]
-                probs = jnp.exp2(s_ref[h, aligned(index), :] - tops[h])
+                probs = jnp.exp2(s_ref[h, slot, :] - tops[h])
                 total = total + jnp.sum(fold(probs), axis=0)
                 mixed = mixed + dot(
                     vt_ref[h * HEAD_DIM : (h + 1) * HEAD_DIM, at], probs.astype(BF16), 1, 0
@@ -387,7 +417,14 @@
             return tuple(fresh)
 
         state = ((jnp.zeros((8, BLOCK), F32), jnp.zeros((HEAD_DIM, BLOCK), F32)),) * count
-        state = lax.fori_loop(0, full + 1, step, state)
+        state = step(span(full, 1), place, state)
+        state = over_blocks(
+            full,
+            lambda index, number, state: step(
+                span(index, number), keys_at(index, number), state
+            ),
+            state,
+        )
         for p in range(pairs):
             both = []
             for h in (2 * p, 2 * p + 1):
@@ -456,6 +493,9 @@
                 q_rows.append(jnp.where(mine, query, jnp.zeros_like(query)))
                 do_rows.append(jnp.where(mine, grad, jnp.zeros_like(grad)))
 
+        def keys_at(index, number):
+            return span(key_block(code, index, prompt_blocks), number)
+
         def probs_and_grads(slot, at, mask, sums):
             fresh = []
             for h in range(count):
@@ -464,32 +504,31 @@
                 if mask is not None:
                     probs = jnp.where(mask, probs, 0.0)
                 grads = dot(v_ref[at, lanes[h // 2]], do_heads[h], 1, 0)
-                p_ref[h, aligned(slot), :] = probs
-                dp_ref[h, aligned(slot), :] = grads
+                p_ref[h, slot, :] = probs
+                dp_ref[h, slot, :] = grads
                 fresh.append(sums[h] + jnp.sum(fold(probs * grads), axis=0))
             return tuple(fresh)
 
         full = full_blocks(code, prompt_blocks)
-        sums = probs_and_grads(full, place, allowed, (jnp.zeros((8, BLOCK), F32),) * count)
-        sums = lax.fori_loop(
-            0,
+        sums = (jnp.zeros((8, BLOCK), F32),) * count
+        sums = probs_and_grads(span(full, 1), place, allowed, sums)
+        sums = over_blocks(
             full,
-            lambda index, sums: probs_and_grads(
-                index, aligned(key_block(code, index, prompt_blocks)), None, sums
+            lambda index, number, sums: probs_and_grads(
+                span(index, number), keys_at(index, number), None, sums
             ),
             sums,
         )
         sums = [jnp.sum(total, axis=0, keepdims=True) for total in sums]
 
-        def step(index, grads):
-            at = aligned(jnp.where(index == full, code, key_block(code, index, prompt_blocks)))
+        def step(slot, at, grads):
             fresh = []
             for p in range(pairs):
                 for_key = dk_ref[at, lanes[p]]
                 for_value = dv_ref[at, lanes[p]]
                 for h in (2 * p, 2 * p + 1):
-                    probs = p_ref[h, aligned(index), :]
-                    low = (probs * (dp_ref[h, aligned(index), :] - sums[h])).astype(BF16)
+                    probs = p_ref[h, slot, :]
+                    low = (probs * (dp_ref[h, slot, :] - sums[h])).astype(BF16)
                     for_key += dot(low, q_rows[h], 1, 0)
                     for_value += dot(probs.astype(BF16), do_rows[h], 1, 0)
                     fresh.append(
@@ -500,8 +539,13 @@
                 dv_ref[at, lanes[p]] = for_value
             return tuple(fresh)
 
-        grads = lax.fori_loop(
-            0, full + 1, step, (jnp.zeros((HEAD_DIM, BLOCK), F32),) * count
+        grads = step(span(full, 1), place, (jnp.zeros((HEAD_DIM, BLOCK), F32),) * count)
+        grads = over_blocks(
+            full,
+            lambda index, number, grads: step(
+                span(index, number), keys_at(index, number), grads
+            ),
+            grads,
         )
         for p in range(pairs):
             pair = jnp.concatenate([grads[2 * p], grads[2 * p + 1]], axis=0).T * SCALE
@@ -540,7 +584,7 @@
             pltpu.VMEM((2 * pairs, tokens, BLOCK), F32),
             pltpu.VMEM((2 * pairs, tokens, BLOCK), F32),
         ],
-        compiler_params=pltpu.CompilerParams(vmem_limit_bytes=VMEM_LIMIT),
+        compiler_params=pltpu.CompilerParams(vmem_limit_bytes=VMEM_MOST),
         cost_estimate=SHORT,
         name="attend_back",
     )(inv, query, key, value, grad, lse, cosine, sine)
@@ -830,24 +874,26 @@
     )
     vec = sum_everywhere(vec, ("fsdp",)).transpose(2, 1, 0, 3).reshape(7, D).astype(F32)
 
-    x_pieces, vec, w_attn, ffn_in_late, cot_own = tie(
-        gather_pieces(gather_start(*halves(layer_in[0]))), vec, w_attn, ffn_in, cotangent[0]
+    inv = jnp.argsort(block_map[0][places()]).astype(jnp.int32)
+    x_pieces, vec, w_attn, ffn_in_late, cot_own, inv, cosine, sine = tie(
+        gather_pieces(gather_start(*halves(layer_in[0]))),
+        vec,
+        w_attn,
+        ffn_in,
+        cotangent[0],
+        inv,
+        *turn_tables(blocks),
     )
     attn_act = norm_pieces(x_pieces, vec[0:1], vec[1:2])
-    cot_begun = gather_start(*halves(cot_own))
-    up_split, down_own, attn_act, first = tie(
-        exchange(split_columns(ffn_in_late, 2)), ffn_out.astype(BF16), attn_act, cot_begun[4:6]
-    )
-    cot_begun = (*cot_begun[:4], *first, *cot_begun[6:])
+    up_split, down_own, attn_act = tie(
+        exchange(split_columns(ffn_in_late, 2)), ffn_out.astype(BF16), attn_act
+    )
     w_up = rows_of(up_split)
     w_down = lax.all_gather(down_own, "fsdp", axis=0, tiled=True)
 
-    codes = block_map[0][places()]
-    inv = jnp.argsort(codes).astype(jnp.int32)
-    cosine, sine = turn_tables(blocks)
     bias = lax.dynamic_slice_in_dim(vec[2:5], here * wide, wide, 1).reshape(1, 3 * wide)
     project = dot(attn_act, w_qkv, 1, 0)
-    project, cot_begun = tie(project, cot_begun)
+    project, cot_begun = tie(project, gather_start(*halves(cot_own)))
     query, key, value, mixed, lse = attend(inv, project, bias, cosine, sine, pairs, blocks)
     cot_far = gather_far(cot_begun)
     mixed, cot_far = tie(mixed, cot_far)
@@ -881,7 +927,7 @@
         leave_feed, cotangent[0], resid, vec[5:6], *parts
     )
 
-    begun = gather_start(branch_top, branch_low)
+    begun = gather_start(branch_top, branch_low, True)
     if cube():
         c_top, hidden = tie(begun[2], hidden)
         begun = (*begun[:2], c_top, *begun[3:])
@@ -890,7 +936,7 @@
     grad_mixed, grad_out = branch_grads(mixed, w_attn, begun)
     share_out = owners(grad_out)
     grad_mixed, out_sums, share_down = tie(grad_mixed, out_sums, share_down)
-    out_begun = scatter_start(out_sums)
+    out_begun = scatter_start(out_sums, False)
     grad_project = attend_back(
         inv, query, key, value, grad_mixed, lse, cosine, sine, pairs, blocks
     )
@@ -901,22 +947,24 @@
     away, grad_qkv = tie(away, grad_qkv)
     share_qkv = owners_of_rows(grad_qkv)
     sums = scatter_sums(grad_project, w_qkv, 1, away)
-    sums, share_in, share_out, grad_project = tie(sums, share_in, share_out, grad_project)
-    begun = scatter_start(sums)
-    begun, out_parts, split_in = window(begun, out_parts, exchange(share_in))
+    sums, grad_project, out_parts, share_in, share_out, share_down = tie(
+        sums, grad_project, out_parts, share_in, share_out, share_down
+    )
     layer_out = (resid + total_of(out_parts)).astype(BF16)[None]
-    parts = scatter_end(begun)
+    bias_grads = jnp.sum(grad_project.astype(F32), axis=0).reshape(3, wide)
+    bias_grads = lax.dynamic_update_slice(jnp.zeros((3, D), F32), bias_grads, (0, here * wide))
+    squares = squared(share_in) + squared(share_out) + squared(share_down)
+    parts, layer_out, bias_grads, squares, share_in = tie(
+        scatter_end(scatter_start(sums)), layer_out, bias_grads, squares, share_in
+    )
+    split_in = exchange(share_in)
     input_grad, gain_one, shift_one = own_rows(
         leave_layer, layer_in[0], grad_resid, vec[0:1], *parts
     )
+    gain_one, shift_one, share_qkv = tie(gain_one, shift_one, share_qkv)
     split_qkv = exchange(share_qkv)
 
-    squares = F32(0.0)
-    for share in (share_qkv, share_out, share_in, share_down):
-        wide_share = share.astype(F32)
-        squares = squares + jnp.sum(wide_share * wide_share)
-    bias_grads = jnp.sum(grad_project.astype(F32), axis=0).reshape(3, wide)
-    bias_grads = lax.dynamic_update_slice(jnp.zeros((3, D), F32), bias_grads, (0, here * wide))
+    squares = squares + squared(share_qkv)
     sums = jnp.concatenate(
         [
             gain_one,
@@ -928,8 +976,7 @@
         ],
         axis=0,
     )
-    sums, split_qkv = tie(sum_everywhere(sums, ("ctx",)), split_qkv)
-    sums = sum_everywhere(sums, ("fsdp",))
+    sums = sum_everywhere(sums)
     vector_sums = sums[:7]
     grad_norm = jnp.sqrt(jnp.sum(vector_sums * vector_sums) + sums[7, 0])
     mine = jnp.arange(D)[:, None] == owner * rows + jnp.arange(rows)[None]

time: 678 us -> 650 us (0.959)
  Pallas kernels: 206 us -> 144 us
  local copies, waits for them, and re-layouts: 49.8 us -> 105 us
  waiting for transfers between devices: 178 us -> 156 us
  other arithmetic: 40.8 us -> 50 us
    unnamed x153 -> x241, local copies, waits for them, and re-layouts: 28 us -> 82.2 us
    ppermute x91, waiting for transfers between devices: 170 us -> 140 us  [swap(): return lax.ppermute(value, axis, [(i, i ^ bit) for i in range(size)])]
    pallas_call x4, Pallas kernels: 35.5 us -> 24.9 us  [chip_sums(): pl.pallas_call(functools.partial(chip_kernel, right_dim), grid=(2,), out_...]
    pallas_call x1, Pallas kernels: 45.3 us -> 36.6 us  [attend_back(): pl.pallas_call(functools.partial(attend_back_kernel, pairs, blocks), out_...]
    pallas_call x1, Pallas kernels: 31.6 us -> 22.9 us  [attend(): pl.pallas_call(functools.partial(attend_kernel, pairs, blocks), out_shape...]
    pallas_call x2, Pallas kernels: 18 us -> 9.42 us  [branch_step(): pl.pallas_call(functools.partial(branch_kernel, not before, last, starts)...]
    pallas_call x2, Pallas kernels: 26.1 us -> 18.5 us  [ffn_up_step(): pl.pallas_call(functools.partial(ffn_up_kernel, units, count), grid=(step...]
    pallas_call x3, Pallas kernels: 16.2 us -> 8.75 us  [own_rows(): pl.pallas_call(functools.partial(own_kernel, step, len(values)), out_shap...]
  transfers between devices with their start and end apart: 102 -> 102, of which waited for: 43 -> 45; matrix products, arithmetic and copies ran while one was open for 17% -> 20% of each run, Pallas kernels for 28% -> 20%
where the time goes in v3:
time: 650 us; the launch traced here: 643 us
  waiting for transfers between devices  156 us (24%)
  Pallas kernels  144 us (22%)
  local copies, waits for them, and re-layouts  105 us (16%)
  starting transfers between devices  77.9 us (12%)
  matrix products  69.1 us (11%)
  other arithmetic  50 us (8%)
  between operations  21.2 us (3%)
  blocking collectives  19.8 us (3%)
    ppermute x91, waiting for transfers between devices, swap(): return lax.ppermute(value, axis, [(i, i ^ bit) for i in range(size)])  140 us
    unnamed x241, local copies, waits for them, and re-layouts  82.2 us
    dot_general x8, matrix products, dot(): lax.dot_general(left, right, (((left_dim,), (right_dim,)), ((), ())), pre...  68 us
    ppermute x91, starting transfers between devices, swap(): return lax.ppermute(value, axis, [(i, i ^ bit) for i in range(size)])  64.3 us
    pallas_call x1, Pallas kernels, attend_back(): pl.pallas_call(functools.partial(attend_back_kernel, pairs, blocks), out_...  36.6 us
    pallas_call x4, Pallas kernels, chip_sums(): pl.pallas_call(functools.partial(chip_kernel, right_dim), grid=(2,), out_...  24.9 us
    pallas_call x1, Pallas kernels, attend(): pl.pallas_call(functools.partial(attend_kernel, pairs, blocks), out_shape...  22.9 us
    all_to_all x1, blocking collectives, exchange(): return lax.all_to_all(split, 'ctx', 0, 0)  19.8 us
  transfers between devices with their start and end apart: 102, of which 45 were waited for; matrix products, arithmetic and copies ran while one was open for 20% of the time, Pallas kernels for 20%

profile of v3, /device:TPU:0, one launch (start us, length us, event | category | flops | bytes accessed | tf_op | source)
XLA Modules:
  0.0 642.7 jit_solution(5290734365025464940)
XLA Ops:
  11.4 19.8 %all_to_all.20 = bf16[8,80,768]{2,1,0:T(8,128)(2,1)S(1)} all-to-all(bf16[8,80,768]{2,1,0:T(8,128)(2,1)S(1)} %split_columns.2), channel_id=1, replica_groups=mesh['ctx'=8,'fsdp'=4] {'ctx'}, dimensions={0} | all-to-all | bytes 1966080 | tf_op jit(solution)/shard_map/all_to_all | solution.py:274
  36.2 5.2 collective-permute-done.14
  50.5 9.6 %collective-permute-done.3.refs_3_ = bf16[128,2048]{1,0:T(8,128)(2,1)} collective-permute-done((bf16[128,2048]{1,0:T(8,128)(2,1)S(1)}, bf16[128,2048]{1,0:T(8,128)(2,1)}, u32[]{:S(2)}, u32[]{:S(2)}) %collective-permute-start.3) | collective-permute-done | bytes 524320 | tf_op jit(solution)/shard_map/ppermute | solution.py:71
  61.7 8.9 %collective-permute-done.6.refs_6_ = bf16[128,2048]{1,0:T(8,128)(2,1)} collective-permute-done((bf16[128,2048]{1,0:T(8,128)(2,1)}, bf16[128,2048]{1,0:T(8,128)(2,1)}, u32[]{:S(2)}, u32[]{:S(2)}) %collective-permute-start.6) | collective-permute-done | bytes 524320 | tf_op jit(solution)/shard_map/ppermute | solution.py:71
  81.4 4.4 all-to-all-start.1
  85.9 2.3 convert_element_type.174
  88.2 9.7 %norm_pieces.1 = bf16[2048,2048]{1,0:T(8,128)(2,1)S(1)} custom-call(f32[1,2048]{1,0:T(1,128)S(1)} %get-tuple-element.442.gain_ref.refs_2_, f32[1,2048]{1,0:T(1,128)S(1)} %get-tuple-element.441.shift_ref, bf16[128,2048]{1,0:T(8,128)(2,1)} %get-tuple-element.227.refs_0_, bf16[128,2048]{1,0:T(8,128)(2,1)S(1)} %get-tuple-element.228.refs_1_, ...), custom_call_target="tpu_custom_call" | custom-call | flops 1000000 | bytes 1000000 | tf_op jit(solution)/shard_map/norm_pieces/pallas_call | solution.py:621
  98.0 3.3 copy-done.26
  101.2 4.2 all-to-all-done.1
  113.5 12.3 %fusion.44.proj_ref = f32[2048,768]{1,0:T(8,128)} fusion(bf16[2048,2048]{1,0:T(8,128)(2,1)} %copy-done.26, bf16[2048,768]{1,0:T(8,128)(2,1)S(1)} %bitcast.56), kind=kOutput, calls=%fused_computation.123 | convolution fusion | flops 6442450944 | bytes 17825792 | tf_op jit(solution)/shard_map/dot_general | solution.py:64
  125.9 5.8 collective-permute-done.20
  136.9 2.8 copy-done.32
  139.7 22.9 %attend.1 = (bf16[2048,256]{1,0:T(8,128)(2,1)S(1)}, bf16[2048,256]{1,0:T(8,128)(2,1)S(1)}, bf16[2048,256]{1,0:T(8,128)(2,1)S(1)}, bf16[2048,256]{1,0:T(8,128)(2,1)S(1)}, f32[4,2048]{1,0:T(4,128)S(1)}) custom-call(s32[8]{0:T(128)S(1)} %get-tuple-element.224.inv_ref, f32[2048,768]{1,0:T(8,128)S(1)} %copy-done.32, f32[1,768]{1,0:T(1,128)S(1)} %bitcast.63, ...), custom_call_target="tpu_custom_call" | custom-call | flops 1000000 | bytes 1000000 | tf_op jit(solution)/shard_map/attend/pallas_call | solution.py:446
  162.8 3.3 convolution_convert_fusion.3
  176.0 4.4 chip_sums.4
  183.2 11.2 %collective-permute-done.25 = bf16[128,2048]{1,0:T(8,128)(2,1)S(1)} collective-permute-done((bf16[128,2048]{1,0:T(8,128)(2,1)S(1)}, bf16[128,2048]{1,0:T(8,128)(2,1)S(1)}, u32[]{:S(2)}, u32[]{:S(2)}) %collective-permute-start.25) | collective-permute-done | bytes 524320 | tf_op jit(solution)/shard_map/ppermute | solution.py:71
  200.8 3.3 copy-done.17
  204.1 10.3 %all-gather.13.cloned.1.call-done = bf16[32,64,1408]{2,1,0:T(8,128)(2,1)} async-done(((bf16[8,64,1408]{2,1,0:T(8,128)(2,1)}), bf16[32,64,1408]{2,1,0:T(8,128)(2,1)}) %all-gather.13.cloned.1.call-update) | async-done | bytes 5767184 | tf_op jit(solution)/shard_map/all_gather | solution.py:862
  214.4 3.3 copy.68
  217.7 2.6 collective-permute-done.35.refs_5_
  220.3 3.0 enter_feed.1
  229.4 10.6 %collective-permute-done.37.refs_2_ = bf16[128,2048]{1,0:T(8,128)(2,1)S(1)} collective-permute-done((bf16[128,2048]{1,0:T(8,128)(2,1)S(1)}, bf16[128,2048]{1,0:T(8,128)(2,1)S(1)}, u32[]{:S(2)}, u32[]{:S(2)}) %collective-permute-start.37) | collective-permute-done | bytes 524320 | tf_op jit(solution)/shard_map/ppermute | solution.py:71
  240.6 9.7 %collective-permute-done.43.refs_3_ = bf16[128,2048]{1,0:T(8,128)(2,1)S(1)} collective-permute-done((bf16[128,2048]{1,0:T(8,128)(2,1)S(1)}, bf16[128,2048]{1,0:T(8,128)(2,1)S(1)}, u32[]{:S(2)}, u32[]{:S(2)}) %collective-permute-start.43) | collective-permute-done | bytes 524320 | tf_op jit(solution)/shard_map/ppermute | solution.py:71
  253.5 13.4 %ffn_up.2 = (bf16[2048,2048]{1,0:T(8,128)(2,1)}, f32[2048,1408]{1,0:T(8,128)}, bf16[2048,704]{1,0:T(8,128)(2,1)S(1)}) custom-call(bf16[2048,1408]{1,0:T(8,128)(2,1)S(1)} %bitcast.52, bf16[128,2048]{1,0:T(8,128)(2,1)S(1)} %get-tuple-element.286.refs_0_, bf16[128,2048]{1,0:T(8,128)(2,1)S(1)} %get-tuple-element.287.refs_1_, ...), custom_call_target="tpu_custom_call" | custom-call | flops 1000000 | bytes 1000000 | tf_op jit(solution)/shard_map/ffn_up/pallas_call | solution.py:695
  269.7 3.4 copy-done.30
  273.1 5.0 ffn_up.3
  279.7 3.3 copy-done.31
  284.8 3.4 copy-done.18
  288.2 11.4 %ffn_back.1.left_ref = bf16[2048,1408]{1,0:T(8,128)(2,1)S(1)} custom-call(f32[2048,1408]{1,0:T(8,128)} %get-tuple-element.298.both_ref, bf16[2048,2048]{1,0:T(8,128)(2,1)S(1)} %copy-done.18, bf16[704,2048]{1,0:T(8,128)(2,1)S(1)} %copy-done.13), custom_call_target="tpu_custom_call" | custom-call | flops 1000000 | bytes 1000000 | tf_op jit(solution)/shard_map/ffn_back/pallas_call | solution.py:748
  299.7 8.7 %convolution_convert_fusion.2 = bf16[1024,2048]{1,0:T(8,128)(2,1)} fusion(bf16[2048,1408]{1,0:T(8,128)(2,1)S(1)} %bitcast.54, bf16[2048,1408]{1,0:T(8,128)(2,1)S(1)} %ffn_back.1.left_ref), kind=kOutput, calls=%fused_computation.5 | convolution fusion | flops 5907677184 | bytes 12845056 | tf_op jit(solution)/shard_map/dot_general | solution.py:64
  308.5 7.7 %convolution_convert_fusion.6 = bf16[704,2048]{1,0:T(8,128)(2,1)} fusion(bf16[2048,704]{1,0:T(8,128)(2,1)S(1)} %copy-done.9, bf16[2048,2048]{1,0:T(8,128)(2,1)S(1)} %copy-done.18), kind=kOutput, calls=%fused_computation.9 | convolution fusion | flops 5907021824 | bytes 14155776 | tf_op jit(solution)/shard_map/dot_general | solution.py:64
  316.3 2.6 copy-done.4
  318.9 2.6 copy-done.6
  321.6 9.4 %chip_sums.5 = (bf16[256,2048]{1,0:T(8,128)(2,1)S(1)}, bf16[128,2048]{1,0:T(8,128)(2,1)S(1)}, bf16[128,2048]{1,0:T(8,128)(2,1)S(1)}, bf16[128,2048]{1,0:T(8,128)...) custom-call(bf16[2048,1408]{1,0:T(8,128)(2,1)S(1)} %copy-done.6, ...), custom_call_target="tpu_custom_call" | custom-call | flops 1000000 | bytes 1000000 | tf_op jit(solution)/shard_map/chip_sums/pallas_call | solution.py:157
  332.4 12.8 %collective-permute-done.52 = bf16[128,2048]{1,0:T(8,128)(2,1)S(1)} collective-permute-done((bf16[128,2048]{1,0:T(8,128)(2,1)S(1)}, bf16[128,2048]{1,0:T(8,128)(2,1)S(1)}, u32[]{:S(2)}, u32[]{:S(2)}) %collective-permute-start.52) | collective-permute-done | bytes 524320 | tf_op jit(solution)/shard_map/ppermute | solution.py:71
  349.8 15.7 %convolution_convert_fusion = bf16[2048,1408]{1,0:T(8,128)(2,1)S(1)} fusion(bf16[2048,2048]{1,0:T(8,128)(2,1)} %copy-done.31, bf16[2048,1408]{1,0:T(8,128)(2,1)S(1)} %copy-done.6), kind=kOutput, calls=%fused_computation.1 | convolution fusion | flops 11814043648 | bytes 19922944 | tf_op jit(solution)/shard_map/dot_general | solution.py:64
  365.5 3.0 copy.69
  384.9 3.6 convolution_convert_fusion.1
  390.4 12.6 %collective-permute-done.58.refs_2_ = bf16[128,2048]{1,0:T(8,128)(2,1)S(1)} collective-permute-done((bf16[128,2048]{1,0:T(8,128)(2,1)S(1)}, bf16[128,2048]{1,0:T(8,128)(2,1)S(1)}, u32[]{:S(2)}, u32[]{:S(2)}) %collective-permute-start.58) | collective-permute-done | bytes 524320 | tf_op jit(solution)/shard_map/ppermute | solution.py:71
  405.7 5.3 chip_sums.6
  412.0 5.0 collective-permute-done.62.refs_3_
  420.2 7.0 %branch_step.2 = (bf16[2048,256]{1,0:T(8,128)(2,1)S(1)}, f32[256,2048]{1,0:T(8,128)S(1)}) custom-call(bf16[2048,256]{1,0:T(8,128)(2,1)S(1)} %get-tuple-element.258.left_ref.mixed_ref, bf16[256,2048]{1,0:T(8,128)(2,1)S(1)} %copy-done.7, bf16[128,2048]{1,0:T(8,128)(2,1)S(1)} %get-tuple-element.324.refs_0_, bf16[128,2048]{1,0:T(8,128)(2,1)S(1)} %get-tuple-element.325.refs_1_, ...), custom_call_target="tpu_custom_call" | custom-call | flops 1000000 | bytes 1000000 | tf_op jit(solution)/shard_map/branch_step/pallas_call | solution.py:781
  427.2 4.7 collective-permute-done.60.refs_0_
  434.8 2.4 branch_step.3
  450.7 36.6 %attend_back.1.left_ref = bf16[2048,768]{1,0:T(8,128)(2,1)S(1)} custom-call(s32[8]{0:T(128)S(1)} %get-tuple-element.224.inv_ref, bf16[2048,256]{1,0:T(8,128)(2,1)S(1)} %copy-done.43, bf16[2048,256]{1,0:T(8,128)(2,1)S(1)} %copy-done.45, bf16[2048,256]{1,0:T(8,128)(2,1)S(1)} %copy-done.47, bf16[2048,256]{1,0:T(8,128)(2,1)S(1)} %copy-done.49, ...), custom_call_target="tpu_custom_call" | custom-call | flops 1000000 | bytes 1000000 | tf_op jit(solution)/shard_map/attend_back/pallas_call | solution.py:575
  487.3 7.0 %convolution_convert_fusion.4 = bf16[1024,2048]{1,0:T(8,128)(2,1)} fusion(bf16[2048,768]{1,0:T(8,128)(2,1)} %bitcast.57, bf16[2048,768]{1,0:T(8,128)(2,1)S(1)} %attend_back.1.left_ref), kind=kOutput, calls=%fused_computation.7 | convolution fusion | flops 3223322624 | bytes 8912896 | tf_op jit(solution)/shard_map/dot_general | solution.py:64
  494.4 9.8 %convolution_convert_fusion.5 = bf16[2048,768]{1,0:T(8,128)(2,1)S(1)} fusion(bf16[2048,2048]{1,0:T(8,128)(2,1)} %copy-done.26, bf16[2048,768]{1,0:T(8,128)(2,1)S(1)} %attend_back.1.left_ref), kind=kOutput, calls=%fused_computation.8 | convolution fusion | flops 6444023808 | bytes 14680064 | tf_op jit(solution)/shard_map/dot_general | solution.py:64
  515.2 5.7 chip_sums.7
  529.3 2.3 fusion.9
  531.6 2.7 multiply_reduce_fusion
  534.3 2.3 convert_add_fusion
  549.6 6.8 %collective-permute-done.82.refs_4_ = bf16[128,2048]{1,0:T(8,128)(2,1)S(1)} collective-permute-done((bf16[128,2048]{1,0:T(8,128)(2,1)}, bf16[128,2048]{1,0:T(8,128)(2,1)S(1)}, u32[]{:S(2)}, u32[]{:S(2)}) %collective-permute-start.82) | collective-permute-done | bytes 524320 | tf_op jit(solution)/shard_map/ppermute | solution.py:71
  559.6 5.6 collective-permute-done.84.refs_6_
  568.3 3.7 all-to-all-start.3
  577.8 3.7 leave_layer.1
  590.6 2.8 collective-permute-done.87
  594.9 2.8 collective-permute-done.88
  598.8 3.3 collective-permute-done.89
  602.1 2.8 collective-permute-start.90
  606.3 4.5 all-to-all-start.2
  614.2 2.8 multiply_subtract_fusion.3
  617.0 7.9 %multiply_subtract_fusion = (f32[64,11264]{1,0:T(8,128)}, f32[64,11264]{1,0:T(8,128)}, f32[64,11264]{1,0:T(8,128)}) fusion(f32[64,11264]{1,0:T(8,128)S(1)} %copy-done.16, bf16[64,11264]{1,0:T(8,128)(2,1)S(1)} %copy-done.37, f32[]{:T(128)S(6)} %min.3, f32[64,11264]{1,0:T(8,128)} %param.29, f32[64,11264]{1,0:T(8,128)} %param.34), kind=kLoop, calls=%fused_computation.12 | loop fusion | flops 12255232 | bytes 18743300 | tf_op jit(solution)/shard_map/sub | solution.py:59
  626.0 2.8 multiply_subtract_fusion.2
  630.1 4.4 multiply_subtract_fusion.1
  (491 shorter events, 185.1 us)
Async XLA Ops:
  7.2 68.5 %all-gather.7.cloned.1.call-start = ((), (), s32[]{:S(2)}) async-start(), calls=%async_computation.8 | async-start | bytes 1310720 | tf_op jit(solution)/shard_map/all_gather | solution.py:865
  9.1 102.2 %all-gather.11.cloned.1.call-start = ((), (), s32[]{:S(2)}) async-start(), calls=%async_computation.14 | async-start | bytes 3932160 | tf_op jit(solution)/shard_map/all_gather | solution.py:862
  33.0 15.0 %collective-permute-start.2 = (bf16[128,2048]{1,0:T(8,128)(2,1)}, bf16[128,2048]{1,0:T(8,128)(2,1)}, u32[]{:S(2)}, u32[]{:S(2)}) collective-permute-start(bf16[128,2048]{1,0:T(8,128)(2,1)} %get-tuple-element.227.refs_0_), channel_id=1, source_target_pairs={{0,8},{4,12},{8,0},{12,4},{16,24},{20,28},{24,16},{28,20},{1,9},{5... | collective-permute-start | bytes 1572872 | tf_op jit(solution)/shard_map/ppermute | solution.py:71
  33.8 14.8 %collective-permute-start.5 = (bf16[128,2048]{1,0:T(8,128)(2,1)S(1)}, bf16[128,2048]{1,0:T(8,128)(2,1)}, u32[]{:S(2)}, u32[]{:S(2)}) collective-permute-start(bf16[128,2048]{1,0:T(8,128)(2,1)S(1)} %get-tuple-element.228.refs_1_), channel_id=1, source_target_pairs={{0,16},{4,20},{8,24},{12,28},{16,0},{20,4},{24,8},{28,12},{1,17},{... | collective-permute-start | bytes 1572872 | tf_op jit(solution)/shard_map/ppermute | solution.py:71
  45.1 15.0 %collective-permute-start.3 = (bf16[128,2048]{1,0:T(8,128)(2,1)S(1)}, bf16[128,2048]{1,0:T(8,128)(2,1)}, u32[]{:S(2)}, u32[]{:S(2)}) collective-permute-start(bf16[128,2048]{1,0:T(8,128)(2,1)S(1)} %get-tuple-element.228.refs_1_), channel_id=1, source_target_pairs={{0,8},{4,12},{8,0},{12,4},{16,24},{20,28},{24,16},{28,20},{1,9},{5... | collective-permute-start | bytes 1572872 | tf_op jit(solution)/shard_map/ppermute | solution.py:71
  46.6 15.2 %collective-permute-start.4 = (bf16[128,2048]{1,0:T(8,128)(2,1)}, bf16[128,2048]{1,0:T(8,128)(2,1)}, u32[]{:S(2)}, u32[]{:S(2)}) collective-permute-start(bf16[128,2048]{1,0:T(8,128)(2,1)} %get-tuple-element.227.refs_0_), channel_id=1, source_target_pairs={{0,16},{4,20},{8,24},{12,28},{16,0},{20,4},{24,8},{28,12},{1,17},{... | collective-permute-start | bytes 1572872 | tf_op jit(solution)/shard_map/ppermute | solution.py:71
  48.1 22.6 %collective-permute-start.6 = (bf16[128,2048]{1,0:T(8,128)(2,1)}, bf16[128,2048]{1,0:T(8,128)(2,1)}, u32[]{:S(2)}, u32[]{:S(2)}) collective-permute-start(bf16[128,2048]{1,0:T(8,128)(2,1)} %collective-permute-done.2.refs_2_), channel_id=1, source_target_pairs={{0,16},{4,20},{8,24},{12,28},{16,0},{20,4},{24,8},{28,12},{1,17},{... | collective-permute-start | bytes 1572872 | tf_op jit(solution)/shard_map/ppermute | solution.py:71
  48.6 22.6 %collective-permute-start.8 = (bf16[128,2048]{1,0:T(8,128)(2,1)}, bf16[128,2048]{1,0:T(8,128)(2,1)S(1)}, u32[]{:S(2)}, u32[]{:S(2)}) collective-permute-start(bf16[128,2048]{1,0:T(8,128)(2,1)} %collective-permute-done.2.refs_2_), channel_id=1, source_target_pairs={{0,4},{4,0},{8,12},{12,8},{16,20},{20,16},{24,28},{28,24},{1,5},{5... | collective-permute-start | bytes 1572872 | tf_op jit(solution)/shard_map/ppermute | solution.py:71
  48.6 22.0 %collective-permute-start.7 = (bf16[128,2048]{1,0:T(8,128)(2,1)}, bf16[128,2048]{1,0:T(8,128)(2,1)}, u32[]{:S(2)}, u32[]{:S(2)}) collective-permute-start(bf16[128,2048]{1,0:T(8,128)(2,1)} %collective-permute-done.5.refs_5_), channel_id=1, source_target_pairs={{0,8},{4,12},{8,0},{12,4},{16,24},{20,28},{24,16},{28,20},{1,9},{5... | collective-permute-start | bytes 1572872 | tf_op jit(solution)/shard_map/ppermute | solution.py:71
  60.1 15.6 %collective-permute-start.11 = (bf16[128,2048]{1,0:T(8,128)(2,1)}, bf16[128,2048]{1,0:T(8,128)(2,1)}, u32[]{:S(2)}, u32[]{:S(2)}) collective-permute-start(bf16[128,2048]{1,0:T(8,128)(2,1)} %collective-permute-done.5.refs_5_), channel_id=1, source_target_pairs={{0,4},{4,0},{8,12},{12,8},{16,20},{20,16},{24,28},{28,24},{1,5},{5... | collective-permute-start | bytes 1572872 | tf_op jit(solution)/shard_map/ppermute | solution.py:71
  61.7 13.9 %collective-permute-start.9 = (bf16[128,2048]{1,0:T(8,128)(2,1)}, bf16[128,2048]{1,0:T(8,128)(2,1)}, u32[]{:S(2)}, u32[]{:S(2)}) collective-permute-start(bf16[128,2048]{1,0:T(8,128)(2,1)} %collective-permute-done.3.refs_3_), channel_id=1, source_target_pairs={{0,4},{4,0},{8,12},{12,8},{16,20},{20,16},{24,28},{28,24},{1,5},{5... | collective-permute-start | bytes 1572872 | tf_op jit(solution)/shard_map/ppermute | solution.py:71
  81.4 24.1 %all-to-all-start.1 = ((bf16[8,64,1408]{2,1,0:T(8,128)(2,1)}), bf16[8,64,1408]{2,1,0:T(8,128)(2,1)}, u32[]{:S(2)}, u32[]{:S(2)}) async-start(bf16[8,64,1408]{2,1,0:T(8,128)(2,1)} %copy-done.35), calls=%async_computation.1 | async-start | bytes 2883584 | tf_op jit(solution)/shard_map/all_to_all | solution.py:274
  85.8 128.6 %all-gather.13.cloned.1.call-start = ((), (), s32[]{:S(2)}) async-start(), calls=%async_computation.15 | async-start | bytes 7208960 | tf_op jit(solution)/shard_map/all_gather | solution.py:862
  105.5 177.6 %all-gather.9.cloned.1.call-start = ((), (), s32[]{:S(2)}) async-start(), calls=%async_computation.9 | async-start | bytes 3604480 | tf_op jit(solution)/shard_map/all_gather | solution.py:892
  106.4 19.4 %collective-permute-start.18 = (bf16[128,2048]{1,0:T(8,128)(2,1)S(1)}, bf16[128,2048]{1,0:T(8,128)(2,1)}, u32[]{:S(2)}, u32[]{:S(2)}) collective-permute-start(bf16[128,2048]{1,0:T(8,128)(2,1)S(1)} %get-tuple-element.267), channel_id=1, source_target_pairs={{0,8},{4,12},{8,0},{12,4},{16,24},{20,28},{24,16},{28,20},{1,9},{5... | collective-permute-start | bytes 1572872 | tf_op jit(solution)/shard_map/ppermute | solution.py:71
  106.9 18.9 %collective-permute-start.19 = (bf16[128,2048]{1,0:T(8,128)(2,1)S(1)}, bf16[128,2048]{1,0:T(8,128)(2,1)}, u32[]{:S(2)}, u32[]{:S(2)}) collective-permute-start(bf16[128,2048]{1,0:T(8,128)(2,1)S(1)} %get-tuple-element.268), channel_id=1, source_target_pairs={{0,16},{4,20},{8,24},{12,28},{16,0},{20,4},{24,8},{28,12},{1,17},{... | collective-permute-start | bytes 1572872 | tf_op jit(solution)/shard_map/ppermute | solution.py:71
  108.6 23.1 %collective-permute-start.20 = (bf16[128,2048]{1,0:T(8,128)(2,1)S(1)}, bf16[128,2048]{1,0:T(8,128)(2,1)}, u32[]{:S(2)}, u32[]{:S(2)}) collective-permute-start(bf16[128,2048]{1,0:T(8,128)(2,1)S(1)} %get-tuple-element.268), channel_id=1, source_target_pairs={{0,8},{4,12},{8,0},{12,4},{16,24},{20,28},{24,16},{28,20},{1,9},{5... | collective-permute-start | bytes 1572872 | tf_op jit(solution)/shard_map/ppermute | solution.py:71
  109.8 22.1 %collective-permute-start.21 = (bf16[128,2048]{1,0:T(8,128)(2,1)S(1)}, bf16[128,2048]{1,0:T(8,128)(2,1)}, u32[]{:S(2)}, u32[]{:S(2)}) collective-permute-start(bf16[128,2048]{1,0:T(8,128)(2,1)S(1)} %get-tuple-element.267), channel_id=1, source_target_pairs={{0,16},{4,20},{8,24},{12,28},{16,0},{20,4},{24,8},{28,12},{1,17},{... | collective-permute-start | bytes 1572872 | tf_op jit(solution)/shard_map/ppermute | solution.py:71
  131.9 30.8 %collective-permute-start.22 = (bf16[128,2048]{1,0:T(8,128)(2,1)}, bf16[128,2048]{1,0:T(8,128)(2,1)}, u32[]{:S(2)}, u32[]{:S(2)}) collective-permute-start(bf16[128,2048]{1,0:T(8,128)(2,1)} %collective-permute-done.18), channel_id=1, source_target_pairs={{0,16},{4,20},{8,24},{12,28},{16,0},{20,4},{24,8},{28,12},{1,17},{... | collective-permute-start | bytes 1572872 | tf_op jit(solution)/shard_map/ppermute | solution.py:71
  132.5 30.2 %collective-permute-start.23 = (bf16[128,2048]{1,0:T(8,128)(2,1)}, bf16[128,2048]{1,0:T(8,128)(2,1)}, u32[]{:S(2)}, u32[]{:S(2)}) collective-permute-start(bf16[128,2048]{1,0:T(8,128)(2,1)} %collective-permute-done.19), channel_id=1, source_target_pairs={{0,8},{4,12},{8,0},{12,4},{16,24},{20,28},{24,16},{28,20},{1,9},{5... | collective-permute-start | bytes 1572872 | tf_op jit(solution)/shard_map/ppermute | solution.py:71
  166.2 273.0 %reduce-scatter.5.cloned.1.call-start = ((), (), s32[]{:S(2)}) async-start(), calls=%async_computation.10 | async-start | bytes 3604480 | tf_op jit(solution)/shard_map/reduce_scatter | solution.py:908
  166.5 14.5 %collective-permute-start.29 = (bf16[128,2048]{1,0:T(8,128)(2,1)}, bf16[128,2048]{1,0:T(8,128)(2,1)S(1)}, u32[]{:S(2)}, u32[]{:S(2)}) collective-permute-start(bf16[128,2048]{1,0:T(8,128)(2,1)} %collective-permute-done.18), channel_id=1, source_target_pairs={{0,4},{4,0},{8,12},{12,8},{16,20},{20,16},{24,28},{28,24},{1,5},{5... | collective-permute-start | bytes 1572872 | tf_op jit(solution)/shard_map/ppermute | solution.py:71
  167.0 32.5 %collective-permute-start.32 = (bf16[128,2048]{1,0:T(8,128)(2,1)}, bf16[128,2048]{1,0:T(8,128)(2,1)S(1)}, u32[]{:S(2)}, u32[]{:S(2)}) collective-permute-start(bf16[128,2048]{1,0:T(8,128)(2,1)} %collective-permute-done.19), channel_id=1, source_target_pairs={{0,4},{4,0},{8,12},{12,8},{16,20},{20,16},{24,28},{28,24},{1,5},{5... | collective-permute-start | bytes 1572872 | tf_op jit(solution)/shard_map/ppermute | solution.py:71
  167.1 15.3 %collective-permute-start.30 = (bf16[128,2048]{1,0:T(8,128)(2,1)}, bf16[128,2048]{1,0:T(8,128)(2,1)S(1)}, u32[]{:S(2)}, u32[]{:S(2)}) collective-permute-start(bf16[128,2048]{1,0:T(8,128)(2,1)} %collective-permute-done.20), channel_id=1, source_target_pairs={{0,4},{4,0},{8,12},{12,8},{16,20},{20,16},{24,28},{28,24},{1,5},{5... | collective-permute-start | bytes 1572872 | tf_op jit(solution)/shard_map/ppermute | solution.py:71
  167.5 15.0 %collective-permute-start.31 = (bf16[128,2048]{1,0:T(8,128)(2,1)}, bf16[128,2048]{1,0:T(8,128)(2,1)S(1)}, u32[]{:S(2)}, u32[]{:S(2)}) collective-permute-start(bf16[128,2048]{1,0:T(8,128)(2,1)} %collective-permute-done.21), channel_id=1, source_target_pairs={{0,4},{4,0},{8,12},{12,8},{16,20},{20,16},{24,28},{28,24},{1,5},{5... | collective-permute-start | bytes 1572872 | tf_op jit(solution)/shard_map/ppermute | solution.py:71
  180.4 14.0 %collective-permute-start.25 = (bf16[128,2048]{1,0:T(8,128)(2,1)S(1)}, bf16[128,2048]{1,0:T(8,128)(2,1)S(1)}, u32[]{:S(2)}, u32[]{:S(2)}) collective-permute-start(bf16[128,2048]{1,0:T(8,128)(2,1)S(1)} %get-tuple-element.261), channel_id=1, source_target_pairs={{0,8},{4,12},{8,0},{12,4},{16,24},{20,28},{24,16},{28,20},{1,9},{5... | collective-permute-start | bytes 1572872 | tf_op jit(solution)/shard_map/ppermute | solution.py:71
  182.4 17.6 %collective-permute-start.33 = (bf16[128,2048]{1,0:T(8,128)(2,1)}, bf16[128,2048]{1,0:T(8,128)(2,1)S(1)}, u32[]{:S(2)}, u32[]{:S(2)}) collective-permute-start(bf16[128,2048]{1,0:T(8,128)(2,1)} %collective-permute-done.22), channel_id=1, source_target_pairs={{0,4},{4,0},{8,12},{12,8},{16,20},{20,16},{24,28},{28,24},{1,5},{5... | collective-permute-start | bytes 1572872 | tf_op jit(solution)/shard_map/ppermute | solution.py:71
  182.6 18.1 %collective-permute-start.34 = (bf16[128,2048]{1,0:T(8,128)(2,1)}, bf16[128,2048]{1,0:T(8,128)(2,1)S(1)}, u32[]{:S(2)}, u32[]{:S(2)}) collective-permute-start(bf16[128,2048]{1,0:T(8,128)(2,1)} %collective-permute-done.23), channel_id=1, source_target_pairs={{0,4},{4,0},{8,12},{12,8},{16,20},{20,16},{24,28},{28,24},{1,5},{5... | collective-permute-start | bytes 1572872 | tf_op jit(solution)/shard_map/ppermute | solution.py:71
  194.7 23.0 %collective-permute-start.27 = (bf16[128,2048]{1,0:T(8,128)(2,1)}, bf16[128,2048]{1,0:T(8,128)(2,1)}, u32[]{:S(2)}, u32[]{:S(2)}) collective-permute-start(bf16[128,2048]{1,0:T(8,128)(2,1)} %get-tuple-element.265), channel_id=1, source_target_pairs={{0,8},{4,12},{8,0},{12,4},{16,24},{20,28},{24,16},{28,20},{1,9},{5... | collective-permute-start | bytes 1572872 | tf_op jit(solution)/shard_map/ppermute | solution.py:71
  196.1 21.5 %collective-permute-start.28 = (bf16[128,2048]{1,0:T(8,128)(2,1)}, bf16[128,2048]{1,0:T(8,128)(2,1)}, u32[]{:S(2)}, u32[]{:S(2)}) collective-permute-start(bf16[128,2048]{1,0:T(8,128)(2,1)} %get-tuple-element.266), channel_id=1, source_target_pairs={{0,16},{4,20},{8,24},{12,28},{16,0},{20,4},{24,8},{28,12},{1,17},{... | collective-permute-start | bytes 1572872 | tf_op jit(solution)/shard_map/ppermute | solution.py:71
  199.5 20.8 %collective-permute-start.35 = (bf16[128,2048]{1,0:T(8,128)(2,1)}, bf16[128,2048]{1,0:T(8,128)(2,1)}, u32[]{:S(2)}, u32[]{:S(2)}) collective-permute-start(bf16[128,2048]{1,0:T(8,128)(2,1)} %add_convert_fusion.7), channel_id=1, source_target_pairs={{0,16},{4,20},{8,24},{12,28},{16,0},{20,4},{24,8},{28,12},{1,17},{... | collective-permute-start | bytes 1572872 | tf_op jit(solution)/shard_map/ppermute | solution.py:71
  200.0 20.3 %collective-permute-start.36 = (bf16[128,2048]{1,0:T(8,128)(2,1)}, bf16[128,2048]{1,0:T(8,128)(2,1)}, u32[]{:S(2)}, u32[]{:S(2)}) collective-permute-start(bf16[128,2048]{1,0:T(8,128)(2,1)} %add_convert_fusion.6), channel_id=1, source_target_pairs={{0,8},{4,12},{8,0},{12,4},{16,24},{20,28},{24,16},{28,20},{1,9},{5... | collective-permute-start | bytes 1572872 | tf_op jit(solution)/shard_map/ppermute | solution.py:71
  225.2 14.8 %collective-permute-start.37 = (bf16[128,2048]{1,0:T(8,128)(2,1)S(1)}, bf16[128,2048]{1,0:T(8,128)(2,1)S(1)}, u32[]{:S(2)}, u32[]{:S(2)}) collective-permute-start(bf16[128,2048]{1,0:T(8,128)(2,1)S(1)} %get-tuple-element.286.refs_0_), channel_id=1, source_target_pairs={{0,8},{4,12},{8,0},{12,4},{16,24},{20,28},{24,16},{28,20},{1,9},{5... | collective-permute-start | bytes 1572872 | tf_op jit(solution)/shard_map/ppermute | solution.py:71
  225.8 14.8 %collective-permute-start.39 = (bf16[128,2048]{1,0:T(8,128)(2,1)S(1)}, bf16[128,2048]{1,0:T(8,128)(2,1)S(1)}, u32[]{:S(2)}, u32[]{:S(2)}) collective-permute-start(bf16[128,2048]{1,0:T(8,128)(2,1)S(1)} %get-tuple-element.287.refs_1_), channel_id=1, source_target_pairs={{0,16},{4,20},{8,24},{12,28},{16,0},{20,4},{24,8},{28,12},{1,17},{... | collective-permute-start | bytes 1572872 | tf_op jit(solution)/shard_map/ppermute | solution.py:71
  227.4 22.9 %collective-permute-start.43 = (bf16[128,2048]{1,0:T(8,128)(2,1)S(1)}, bf16[128,2048]{1,0:T(8,128)(2,1)S(1)}, u32[]{:S(2)}, u32[]{:S(2)}) collective-permute-start(bf16[128,2048]{1,0:T(8,128)(2,1)S(1)} %get-tuple-element.287.refs_1_), channel_id=1, source_target_pairs={{0,8},{4,12},{8,0},{12,4},{16,24},{20,28},{24,16},{28,20},{1,9},{5... | collective-permute-start | bytes 1572872 | tf_op jit(solution)/shard_map/ppermute | solution.py:71
  228.7 21.9 %collective-permute-start.44 = (bf16[128,2048]{1,0:T(8,128)(2,1)S(1)}, bf16[128,2048]{1,0:T(8,128)(2,1)S(1)}, u32[]{:S(2)}, u32[]{:S(2)}) collective-permute-start(bf16[128,2048]{1,0:T(8,128)(2,1)S(1)} %get-tuple-element.286.refs_0_), channel_id=1, source_target_pairs={{0,16},{4,20},{8,24},{12,28},{16,0},{20,4},{24,8},{28,12},{1,17},{... | collective-permute-start | bytes 1572872 | tf_op jit(solution)/shard_map/ppermute | solution.py:71
  250.8 16.2 %collective-permute-start.38 = (bf16[128,2048]{1,0:T(8,128)(2,1)S(1)}, bf16[128,2048]{1,0:T(8,128)(2,1)S(1)}, u32[]{:S(2)}, u32[]{:S(2)}) collective-permute-start(bf16[128,2048]{1,0:T(8,128)(2,1)S(1)} %collective-permute-done.37.refs_2_), channel_id=1, source_target_pairs={{0,16},{4,20},{8,24},{12,28},{16,0},{20,4},{24,8},{28,12},{1,17},{... | collective-permute-start | bytes 1572872 | tf_op jit(solution)/shard_map/ppermute | solution.py:71
  252.3 14.7 %collective-permute-start.40 = (bf16[128,2048]{1,0:T(8,128)(2,1)S(1)}, bf16[128,2048]{1,0:T(8,128)(2,1)S(1)}, u32[]{:S(2)}, u32[]{:S(2)}) collective-permute-start(bf16[128,2048]{1,0:T(8,128)(2,1)S(1)} %collective-permute-done.39.refs_5_), channel_id=1, source_target_pairs={{0,8},{4,12},{8,0},{12,4},{16,24},{20,28},{24,16},{28,20},{1,9},{5... | collective-permute-start | bytes 1572872 | tf_op jit(solution)/shard_map/ppermute | solution.py:71
  316.2 171.1 %reduce-scatter.7.cloned.1.call-start = ((), (), s32[]{:S(2)}) async-start(), calls=%async_computation.11 | async-start | bytes 7208960 | tf_op jit(solution)/shard_map/reduce_scatter | solution.py:908
  331.0 14.3 %collective-permute-start.52 = (bf16[128,2048]{1,0:T(8,128)(2,1)S(1)}, bf16[128,2048]{1,0:T(8,128)(2,1)S(1)}, u32[]{:S(2)}, u32[]{:S(2)}) collective-permute-start(bf16[128,2048]{1,0:T(8,128)(2,1)S(1)} %get-tuple-element.304), channel_id=1, source_target_pairs={{0,8},{4,12},{8,0},{12,4},{16,24},{20,28},{24,16},{28,20},{1,9},{5... | collective-permute-start | bytes 1572872 | tf_op jit(solution)/shard_map/ppermute | solution.py:71
  331.4 14.0 %collective-permute-start.53 = (bf16[128,2048]{1,0:T(8,128)(2,1)S(1)}, bf16[128,2048]{1,0:T(8,128)(2,1)S(1)}, u32[]{:S(2)}, u32[]{:S(2)}) collective-permute-start(bf16[128,2048]{1,0:T(8,128)(2,1)S(1)} %get-tuple-element.305), channel_id=1, source_target_pairs={{0,16},{4,20},{8,24},{12,28},{16,0},{20,4},{24,8},{28,12},{1,17},{... | collective-permute-start | bytes 1572872 | tf_op jit(solution)/shard_map/ppermute | solution.py:71
  345.4 23.1 %collective-permute-start.54 = (bf16[128,2048]{1,0:T(8,128)(2,1)S(1)}, bf16[128,2048]{1,0:T(8,128)(2,1)S(1)}, u32[]{:S(2)}, u32[]{:S(2)}) collective-permute-start(bf16[128,2048]{1,0:T(8,128)(2,1)S(1)} %get-tuple-element.308), channel_id=1, source_target_pairs={{0,8},{4,12},{8,0},{12,4},{16,24},{20,28},{24,16},{28,20},{1,9},{5... | collective-permute-start | bytes 1572872 | tf_op jit(solution)/shard_map/ppermute | solution.py:71
  347.1 22.2 %collective-permute-start.55 = (bf16[128,2048]{1,0:T(8,128)(2,1)S(1)}, bf16[128,2048]{1,0:T(8,128)(2,1)S(1)}, u32[]{:S(2)}, u32[]{:S(2)}) collective-permute-start(bf16[128,2048]{1,0:T(8,128)(2,1)S(1)} %add_convert_fusion.5), channel_id=1, source_target_pairs={{0,16},{4,20},{8,24},{12,28},{16,0},{20,4},{24,8},{28,12},{1,17},{... | collective-permute-start | bytes 1572872 | tf_op jit(solution)/shard_map/ppermute | solution.py:71
  347.8 22.3 %collective-permute-start.56 = (bf16[128,2048]{1,0:T(8,128)(2,1)S(1)}, bf16[128,2048]{1,0:T(8,128)(2,1)S(1)}, u32[]{:S(2)}, u32[]{:S(2)}) collective-permute-start(bf16[128,2048]{1,0:T(8,128)(2,1)S(1)} %add_convert_fusion.4), channel_id=1, source_target_pairs={{0,8},{4,12},{8,0},{12,4},{16,24},{20,28},{24,16},{28,20},{1,9},{5... | collective-permute-start | bytes 1572872 | tf_op jit(solution)/shard_map/ppermute | solution.py:71
  348.8 22.5 %collective-permute-start.57 = (bf16[128,2048]{1,0:T(8,128)(2,1)S(1)}, bf16[128,2048]{1,0:T(8,128)(2,1)S(1)}, u32[]{:S(2)}, u32[]{:S(2)}) collective-permute-start(bf16[128,2048]{1,0:T(8,128)(2,1)S(1)} %get-tuple-element.313), channel_id=1, source_target_pairs={{0,16},{4,20},{8,24},{12,28},{16,0},{20,4},{24,8},{28,12},{1,17},{... | collective-permute-start | bytes 1572872 | tf_op jit(solution)/shard_map/ppermute | solution.py:71
  372.1 154.5 %reduce-scatter.9.cloned.1.call-start = ((), (), s32[]{:S(2)}) async-start(), calls=%async_computation.12 | async-start | bytes 1310720 | tf_op jit(solution)/shard_map/reduce_scatter | solution.py:908
  388.5 17.2 %collective-permute-start.65 = (bf16[1024,2048]{1,0:T(8,128)(2,1)S(1)}, bf16[1024,2048]{1,0:T(8,128)(2,1)S(1)}, u32[]{:S(2)}, u32[]{:S(2)}) collective-permute-start(bf16[1024,2048]{1,0:T(8,128)(2,1)S(1)} %convolution_convert_fusion.1), channel_id=1, source_target_pairs={{0,4},{4,0},{8,12},{12,8},{16,20},{20,16},{24,28},{28,24},{1,5},{5... | collective-permute-start | bytes 12582920 | tf_op jit(solution)/shard_map/ppermute | solution.py:71
  388.7 14.2 %collective-permute-start.58 = (bf16[128,2048]{1,0:T(8,128)(2,1)S(1)}, bf16[128,2048]{1,0:T(8,128)(2,1)S(1)}, u32[]{:S(2)}, u32[]{:S(2)}) collective-permute-start(bf16[128,2048]{1,0:T(8,128)(2,1)S(1)} %get-tuple-element.324.refs_0_), channel_id=1, source_target_pairs={{0,8},{4,12},{8,0},{12,4},{16,24},{20,28},{24,16},{28,20},{1,9},{5... | collective-permute-start | bytes 1572872 | tf_op jit(solution)/shard_map/ppermute | solution.py:71
  390.0 13.9 %collective-permute-start.59 = (bf16[128,2048]{1,0:T(8,128)(2,1)S(1)}, bf16[128,2048]{1,0:T(8,128)(2,1)S(1)}, u32[]{:S(2)}, u32[]{:S(2)}) collective-permute-start(bf16[128,2048]{1,0:T(8,128)(2,1)S(1)} %get-tuple-element.325.refs_1_), channel_id=1, source_target_pairs={{0,16},{4,20},{8,24},{12,28},{16,0},{20,4},{24,8},{28,12},{1,17},{... | collective-permute-start | bytes 1572872 | tf_op jit(solution)/shard_map/ppermute | solution.py:71
  405.7 14.0 %collective-permute-start.70 = (bf16[128,2048]{1,0:T(8,128)(2,1)S(1)}, bf16[128,2048]{1,0:T(8,128)(2,1)S(1)}, u32[]{:S(2)}, u32[]{:S(2)}) collective-permute-start(bf16[128,2048]{1,0:T(8,128)(2,1)S(1)} %collective-permute-done.59.refs_5_), channel_id=1, source_target_pairs={{0,4},{4,0},{8,12},{12,8},{16,20},{20,16},{24,28},{28,24},{1,5},{5... | collective-permute-start | bytes 1572872 | tf_op jit(solution)/shard_map/ppermute | solution.py:71
  439.2 48.0 %collective-permute-start.73 = (bf16[128,2048]{1,0:T(8,128)(2,1)}, bf16[128,2048]{1,0:T(8,128)(2,1)}, u32[]{:S(2)}, u32[]{:S(2)}) collective-permute-start(bf16[128,2048]{1,0:T(8,128)(2,1)} %get-tuple-element.357), channel_id=1, source_target_pairs={{0,8},{4,12},{8,0},{12,4},{16,24},{20,28},{24,16},{28,20},{1,9},{5... | collective-permute-start | bytes 1572872 | tf_op jit(solution)/shard_map/ppermute | solution.py:71
  440.3 46.9 %collective-permute-start.74 = (bf16[128,2048]{1,0:T(8,128)(2,1)}, bf16[128,2048]{1,0:T(8,128)(2,1)}, u32[]{:S(2)}, u32[]{:S(2)}) collective-permute-start(bf16[128,2048]{1,0:T(8,128)(2,1)} %get-tuple-element.358), channel_id=1, source_target_pairs={{0,16},{4,20},{8,24},{12,28},{16,0},{20,4},{24,8},{28,12},{1,17},{... | collective-permute-start | bytes 1572872 | tf_op jit(solution)/shard_map/ppermute | solution.py:71
  441.9 45.3 %collective-permute-start.75 = (bf16[128,2048]{1,0:T(8,128)(2,1)}, bf16[128,2048]{1,0:T(8,128)(2,1)}, u32[]{:S(2)}, u32[]{:S(2)}) collective-permute-start(bf16[128,2048]{1,0:T(8,128)(2,1)} %get-tuple-element.359), channel_id=1, source_target_pairs={{0,8},{4,12},{8,0},{12,4},{16,24},{20,28},{24,16},{28,20},{1,9},{5... | collective-permute-start | bytes 1572872 | tf_op jit(solution)/shard_map/ppermute | solution.py:71
  442.7 44.5 %collective-permute-start.76 = (bf16[128,2048]{1,0:T(8,128)(2,1)}, bf16[128,2048]{1,0:T(8,128)(2,1)}, u32[]{:S(2)}, u32[]{:S(2)}) collective-permute-start(bf16[128,2048]{1,0:T(8,128)(2,1)} %get-tuple-element.360), channel_id=1, source_target_pairs={{0,16},{4,20},{8,24},{12,28},{16,0},{20,4},{24,8},{28,12},{1,17},{... | collective-permute-start | bytes 1572872 | tf_op jit(solution)/shard_map/ppermute | solution.py:71
  494.3 89.6 %reduce-scatter.11.cloned.1.call-start = ((), (), s32[]{:S(2)}) async-start(), calls=%async_computation.13 | async-start | bytes 3932160 | tf_op jit(solution)/shard_map/reduce_scatter | solution.py:908
  508.4 18.2 %collective-permute-start.78 = (bf16[128,2048]{1,0:T(8,128)(2,1)}, bf16[128,2048]{1,0:T(8,128)(2,1)}, u32[]{:S(2)}, u32[]{:S(2)}) collective-permute-start(bf16[128,2048]{1,0:T(8,128)(2,1)} %add_convert_fusion.3), channel_id=1, source_target_pairs={{0,16},{4,20},{8,24},{12,28},{16,0},{20,4},{24,8},{28,12},{1,17},{... | collective-permute-start | bytes 1572872 | tf_op jit(solution)/shard_map/ppermute | solution.py:71
  512.0 14.6 %collective-permute-start.79 = (bf16[128,2048]{1,0:T(8,128)(2,1)}, bf16[128,2048]{1,0:T(8,128)(2,1)}, u32[]{:S(2)}, u32[]{:S(2)}) collective-permute-start(bf16[128,2048]{1,0:T(8,128)(2,1)} %add_convert_fusion.2), channel_id=1, source_target_pairs={{0,8},{4,12},{8,0},{12,4},{16,24},{20,28},{24,16},{28,20},{1,9},{5... | collective-permute-start | bytes 1572872 | tf_op jit(solution)/shard_map/ppermute | solution.py:71
  526.7 14.1 %collective-permute-start.80 = (bf16[128,2048]{1,0:T(8,128)(2,1)}, bf16[128,2048]{1,0:T(8,128)(2,1)}, u32[]{:S(2)}, u32[]{:S(2)}) collective-permute-start(bf16[128,2048]{1,0:T(8,128)(2,1)} %copy-done.88), channel_id=1, source_target_pairs={{0,8},{4,12},{8,0},{12,4},{16,24},{20,28},{24,16},{28,20},{1,9},{5... | collective-permute-start | bytes 1572872 | tf_op jit(solution)/shard_map/ppermute | solution.py:71
  541.3 15.1 %collective-permute-start.82 = (bf16[128,2048]{1,0:T(8,128)(2,1)}, bf16[128,2048]{1,0:T(8,128)(2,1)S(1)}, u32[]{:S(2)}, u32[]{:S(2)}) collective-permute-start(bf16[128,2048]{1,0:T(8,128)(2,1)} %copy-done.86), channel_id=1, source_target_pairs={{0,8},{4,12},{8,0},{12,4},{16,24},{20,28},{24,16},{28,20},{1,9},{5... | collective-permute-start | bytes 1572872 | tf_op jit(solution)/shard_map/ppermute | solution.py:71
  543.9 14.9 %collective-permute-start.83 = (bf16[128,2048]{1,0:T(8,128)(2,1)S(1)}, bf16[128,2048]{1,0:T(8,128)(2,1)S(1)}, u32[]{:S(2)}, u32[]{:S(2)}) collective-permute-start(bf16[128,2048]{1,0:T(8,128)(2,1)S(1)} %add_convert_fusion.1), channel_id=1, source_target_pairs={{0,16},{4,20},{8,24},{12,28},{16,0},{20,4},{24,8},{28,12},{1,17},{... | collective-permute-start | bytes 1572872 | tf_op jit(solution)/shard_map/ppermute | solution.py:71
  545.9 19.4 %collective-permute-start.84 = (bf16[128,2048]{1,0:T(8,128)(2,1)S(1)}, bf16[128,2048]{1,0:T(8,128)(2,1)S(1)}, u32[]{:S(2)}, u32[]{:S(2)}) collective-permute-start(bf16[128,2048]{1,0:T(8,128)(2,1)S(1)} %add_convert_fusion), channel_id=1, source_target_pairs={{0,8},{4,12},{8,0},{12,4},{16,24},{20,28},{24,16},{28,20},{1,9},{5... | collective-permute-start | bytes 1572872 | tf_op jit(solution)/shard_map/ppermute | solution.py:71
  546.9 20.6 %collective-permute-start.85 = (bf16[128,2048]{1,0:T(8,128)(2,1)S(1)}, bf16[128,2048]{1,0:T(8,128)(2,1)S(1)}, u32[]{:S(2)}, u32[]{:S(2)}) collective-permute-start(bf16[128,2048]{1,0:T(8,128)(2,1)S(1)} %copy-done.85), channel_id=1, source_target_pairs={{0,16},{4,20},{8,24},{12,28},{16,0},{20,4},{24,8},{28,12},{1,17},{... | collective-permute-start | bytes 1572872 | tf_op jit(solution)/shard_map/ppermute | solution.py:71
  568.3 36.6 %all-to-all-start.3 = ((bf16[8,64,1408]{2,1,0:T(8,128)(2,1)}), bf16[8,64,1408]{2,1,0:T(8,128)(2,1)S(1)}, u32[]{:S(2)}, u32[]{:S(2)}) async-start(bf16[8,64,1408]{2,1,0:T(8,128)(2,1)} %bitcast.69), calls=%async_computation.7 | async-start | bytes 2883584 | tf_op jit(solution)/shard_map/all_to_all | solution.py:274
  606.3 22.6 %all-to-all-start.2 = ((bf16[8,64,768]{2,1,0:T(8,128)(2,1)}), bf16[8,64,768]{2,1,0:T(8,128)(2,1)}, u32[]{:S(2)}, u32[]{:S(2)}) async-start(bf16[8,64,768]{2,1,0:T(8,128)(2,1)} %bitcast.75), calls=%async_computation.6 | async-start | bytes 1572864 | tf_op jit(solution)/shard_map/all_to_all | solution.py:274
  (150 other events, 1015.8 us)
Sparse Core Ops, SparseCore 0:
  10.2 31.2 all-gather.6
  43.6 63.7 all-gather.10
  109.0 105.3 all-gather.12
  216.4 57.4 all-gather.8
  316.4 56.1 reduce-scatter.4
  374.7 102.0 reduce-scatter.6
  494.5 28.1 reduce-scatter.8
  525.0 58.8 reduce-scatter.10

commit v4 on v3

--- a/solution.py
+++ b/solution.py
@@ -934,7 +934,6 @@
     out_sums = scatter_sums(hidden, w_down, 0, scatter_away(hidden, w_down, 0))
     begun, out_sums = window(begun, out_sums)
     grad_mixed, grad_out = branch_grads(mixed, w_attn, begun)
-    share_out = owners(grad_out)
     grad_mixed, out_sums, share_down = tie(grad_mixed, out_sums, share_down)
     out_begun = scatter_start(out_sums, False)
     grad_project = attend_back(
@@ -947,9 +946,14 @@
     away, grad_qkv = tie(away, grad_qkv)
     share_qkv = owners_of_rows(grad_qkv)
     sums = scatter_sums(grad_project, w_qkv, 1, away)
-    sums, grad_project, out_parts, share_in, share_out, share_down = tie(
-        sums, grad_project, out_parts, share_in, share_out, share_down
-    )
+    sums, grad_project, out_parts, share_in, grad_out, share_down = tie(
+        sums, grad_project, out_parts, share_in, grad_out, share_down
+    )
+    place = lax.axis_index("fsdp")
+    share_out = F32(0.0)
+    for m in range(groups):
+        block = lax.dynamic_slice_in_dim(grad_out, (place ^ m) * rows, rows, 0)
+        share_out = share_out + (swap(block, m, "fsdp") if m else block).astype(F32)
     layer_out = (resid + total_of(out_parts)).astype(BF16)[None]
     bias_grads = jnp.sum(grad_project.astype(F32), axis=0).reshape(3, wide)
     bias_grads = lax.dynamic_update_slice(jnp.zeros((3, D), F32), bias_grads, (0, here * wide))

time: 650 us -> 675 us (1.038)
  waiting for transfers between devices: 156 us -> 180 us
    ppermute x91 -> x94, waiting for transfers between devices: 140 us -> 165 us  [swap(): return lax.ppermute(value, axis, [(i, i ^ bit) for i in range(size)])]
    ppermute x91 -> x94, starting transfers between devices: 64.3 us -> 66.8 us  [swap(): return lax.ppermute(value, axis, [(i, i ^ bit) for i in range(size)])]
    unnamed x241 -> x227, local copies, waits for them, and re-layouts: 82.2 us -> 79.7 us
  transfers between devices with their start and end apart: 102 -> 104, of which waited for: 45 -> 42; matrix products, arithmetic and copies ran while one was open for 20% -> 19% of each run, Pallas kernels for 20% -> 20%
where the time goes in v4:
time: 675 us; the launch traced here: 668 us
  waiting for transfers between devices  180 us (27%)
  Pallas kernels  145 us (21%)
  local copies, waits for them, and re-layouts  104 us (15%)
  starting transfers between devices  80.3 us (12%)
  matrix products  67.4 us (10%)
  other arithmetic  50.7 us (8%)
  between operations  20.9 us (3%)
  blocking collectives  19.8 us (3%)
    ppermute x94, waiting for transfers between devices, swap(): return lax.ppermute(value, axis, [(i, i ^ bit) for i in range(size)])  165 us
    unnamed x227, local copies, waits for them, and re-layouts  79.7 us
    ppermute x94, starting transfers between devices, swap(): return lax.ppermute(value, axis, [(i, i ^ bit) for i in range(size)])  66.8 us
    dot_general x8, matrix products, dot(): lax.dot_general(left, right, (((left_dim,), (right_dim,)), ((), ())), pre...  66.3 us
    pallas_call x1, Pallas kernels, attend_back(): pl.pallas_call(functools.partial(attend_back_kernel, pairs, blocks), out_...  36.6 us
    pallas_call x4, Pallas kernels, chip_sums(): pl.pallas_call(functools.partial(chip_kernel, right_dim), grid=(2,), out_...  24.9 us
    pallas_call x1, Pallas kernels, attend(): pl.pallas_call(functools.partial(attend_kernel, pairs, blocks), out_shape...  22.9 us
    all_to_all x1, blocking collectives, exchange(): return lax.all_to_all(split, 'ctx', 0, 0)  19.8 us
  transfers between devices with their start and end apart: 104, of which 42 were waited for; matrix products, arithmetic and copies ran while one was open for 19% of the time, Pallas kernels for 20%

profile of v4, /device:TPU:0, one launch (start us, length us, event | category | flops | bytes accessed | tf_op | source)
XLA Modules:
  0.0 668.0 jit_solution(6169929082351862045)
XLA Ops:
  11.4 19.8 %all_to_all.20 = bf16[8,80,768]{2,1,0:T(8,128)(2,1)S(1)} all-to-all(bf16[8,80,768]{2,1,0:T(8,128)(2,1)S(1)} %split_columns.2), channel_id=1, replica_groups=mesh['ctx'=8,'fsdp'=4] {'ctx'}, dimensions={0} | all-to-all | bytes 1966080 | tf_op jit(solution)/shard_map/all_to_all | solution.py:274
  36.2 5.2 collective-permute-done.14
  50.5 9.6 %collective-permute-done.3.refs_3_ = bf16[128,2048]{1,0:T(8,128)(2,1)} collective-permute-done((bf16[128,2048]{1,0:T(8,128)(2,1)S(1)}, bf16[128,2048]{1,0:T(8,128)(2,1)}, u32[]{:S(2)}, u32[]{:S(2)}) %collective-permute-start.3) | collective-permute-done | bytes 524320 | tf_op jit(solution)/shard_map/ppermute | solution.py:71
  61.7 8.9 %collective-permute-done.6.refs_6_ = bf16[128,2048]{1,0:T(8,128)(2,1)} collective-permute-done((bf16[128,2048]{1,0:T(8,128)(2,1)}, bf16[128,2048]{1,0:T(8,128)(2,1)}, u32[]{:S(2)}, u32[]{:S(2)}) %collective-permute-start.6) | collective-permute-done | bytes 524320 | tf_op jit(solution)/shard_map/ppermute | solution.py:71
  81.4 4.4 all-to-all-start.1
  85.8 2.3 convert_element_type.182
  88.2 9.7 %norm_pieces.1 = bf16[2048,2048]{1,0:T(8,128)(2,1)S(1)} custom-call(f32[1,2048]{1,0:T(1,128)S(1)} %get-tuple-element.447.gain_ref.refs_2_, f32[1,2048]{1,0:T(1,128)S(1)} %get-tuple-element.446.shift_ref, bf16[128,2048]{1,0:T(8,128)(2,1)} %get-tuple-element.227.refs_0_, bf16[128,2048]{1,0:T(8,128)(2,1)S(1)} %get-tuple-element.228.refs_1_, ...), custom_call_target="tpu_custom_call" | custom-call | flops 1000000 | bytes 1000000 | tf_op jit(solution)/shard_map/norm_pieces/pallas_call | solution.py:621
  98.0 3.3 copy-done.26
  101.2 4.2 all-to-all-done.1
  111.3 2.2 copy.65
  113.5 12.3 %fusion.40.proj_ref = f32[2048,768]{1,0:T(8,128)} fusion(bf16[2048,2048]{1,0:T(8,128)(2,1)} %copy-done.26, bf16[2048,768]{1,0:T(8,128)(2,1)S(1)} %bitcast.56), kind=kOutput, calls=%fused_computation.124 | convolution fusion | flops 6442450944 | bytes 17825792 | tf_op jit(solution)/shard_map/dot_general | solution.py:64
  125.9 5.8 collective-permute-done.20
  136.9 2.8 copy-done.32
  139.7 22.9 %attend.1 = (bf16[2048,256]{1,0:T(8,128)(2,1)S(1)}, bf16[2048,256]{1,0:T(8,128)(2,1)S(1)}, bf16[2048,256]{1,0:T(8,128)(2,1)S(1)}, bf16[2048,256]{1,0:T(8,128)(2,1)S(1)}, f32[4,2048]{1,0:T(4,128)S(1)}) custom-call(s32[8]{0:T(128)S(1)} %get-tuple-element.224.inv_ref, f32[2048,768]{1,0:T(8,128)S(1)} %copy-done.32, f32[1,768]{1,0:T(1,128)S(1)} %bitcast.63, ...), custom_call_target="tpu_custom_call" | custom-call | flops 1000000 | bytes 1000000 | tf_op jit(solution)/shard_map/attend/pallas_call | solution.py:446
  162.8 3.3 convolution_convert_fusion.3
  176.0 4.4 chip_sums.4
  183.2 11.2 %collective-permute-done.25 = bf16[128,2048]{1,0:T(8,128)(2,1)S(1)} collective-permute-done((bf16[128,2048]{1,0:T(8,128)(2,1)S(1)}, bf16[128,2048]{1,0:T(8,128)(2,1)S(1)}, u32[]{:S(2)}, u32[]{:S(2)}) %collective-permute-start.25) | collective-permute-done | bytes 524320 | tf_op jit(solution)/shard_map/ppermute | solution.py:71
  200.7 3.3 copy-done.17
  204.1 10.3 %all-gather.13.cloned.1.call-done = bf16[32,64,1408]{2,1,0:T(8,128)(2,1)} async-done(((bf16[8,64,1408]{2,1,0:T(8,128)(2,1)}), bf16[32,64,1408]{2,1,0:T(8,128)(2,1)}) %all-gather.13.cloned.1.call-update) | async-done | bytes 5767184 | tf_op jit(solution)/shard_map/all_gather | solution.py:862
  214.4 3.3 copy.68
  217.7 2.6 collective-permute-done.35.refs_5_
  220.3 3.0 enter_feed.1
  229.4 10.6 %collective-permute-done.37.refs_2_ = bf16[128,2048]{1,0:T(8,128)(2,1)S(1)} collective-permute-done((bf16[128,2048]{1,0:T(8,128)(2,1)S(1)}, bf16[128,2048]{1,0:T(8,128)(2,1)S(1)}, u32[]{:S(2)}, u32[]{:S(2)}) %collective-permute-start.37) | collective-permute-done | bytes 524320 | tf_op jit(solution)/shard_map/ppermute | solution.py:71
  240.6 9.7 %collective-permute-done.43.refs_3_ = bf16[128,2048]{1,0:T(8,128)(2,1)S(1)} collective-permute-done((bf16[128,2048]{1,0:T(8,128)(2,1)S(1)}, bf16[128,2048]{1,0:T(8,128)(2,1)S(1)}, u32[]{:S(2)}, u32[]{:S(2)}) %collective-permute-start.43) | collective-permute-done | bytes 524320 | tf_op jit(solution)/shard_map/ppermute | solution.py:71
  253.5 13.4 %ffn_up.2 = (bf16[2048,2048]{1,0:T(8,128)(2,1)}, f32[2048,1408]{1,0:T(8,128)}, bf16[2048,704]{1,0:T(8,128)(2,1)S(1)}) custom-call(bf16[2048,1408]{1,0:T(8,128)(2,1)S(1)} %bitcast.52, bf16[128,2048]{1,0:T(8,128)(2,1)S(1)} %get-tuple-element.286.refs_0_, bf16[128,2048]{1,0:T(8,128)(2,1)S(1)} %get-tuple-element.287.refs_1_, ...), custom_call_target="tpu_custom_call" | custom-call | flops 1000000 | bytes 1000000 | tf_op jit(solution)/shard_map/ffn_up/pallas_call | solution.py:695
  269.7 3.4 copy-done.30
  273.0 5.1 ffn_up.3
  279.7 3.3 copy-done.31
  284.8 3.4 copy-done.18
  288.2 11.4 %ffn_back.1.left_ref = bf16[2048,1408]{1,0:T(8,128)(2,1)S(1)} custom-call(f32[2048,1408]{1,0:T(8,128)} %get-tuple-element.298.both_ref, bf16[2048,2048]{1,0:T(8,128)(2,1)S(1)} %copy-done.18, bf16[704,2048]{1,0:T(8,128)(2,1)S(1)} %copy-done.13), custom_call_target="tpu_custom_call" | custom-call | flops 1000000 | bytes 1000000 | tf_op jit(solution)/shard_map/ffn_back/pallas_call | solution.py:748
  299.7 8.7 %convolution_convert_fusion.2 = bf16[1024,2048]{1,0:T(8,128)(2,1)} fusion(bf16[2048,1408]{1,0:T(8,128)(2,1)S(1)} %bitcast.54, bf16[2048,1408]{1,0:T(8,128)(2,1)S(1)} %ffn_back.1.left_ref), kind=kOutput, calls=%fused_computation.5 | convolution fusion | flops 5907677184 | bytes 12845056 | tf_op jit(solution)/shard_map/dot_general | solution.py:64
  308.5 7.7 %convolution_convert_fusion.6 = bf16[704,2048]{1,0:T(8,128)(2,1)} fusion(bf16[2048,704]{1,0:T(8,128)(2,1)S(1)} %copy-done.9, bf16[2048,2048]{1,0:T(8,128)(2,1)S(1)} %copy-done.18), kind=kOutput, calls=%fused_computation.9 | convolution fusion | flops 5907021824 | bytes 14155776 | tf_op jit(solution)/shard_map/dot_general | solution.py:64
  316.2 2.6 copy-done.4
  318.9 2.6 copy-done.6
  321.5 9.4 %chip_sums.5 = (bf16[256,2048]{1,0:T(8,128)(2,1)S(1)}, bf16[128,2048]{1,0:T(8,128)(2,1)S(1)}, bf16[128,2048]{1,0:T(8,128)(2,1)S(1)}, bf16[128,2048]{1,0:T(8,128)...) custom-call(bf16[2048,1408]{1,0:T(8,128)(2,1)S(1)} %copy-done.6, ...), custom_call_target="tpu_custom_call" | custom-call | flops 1000000 | bytes 1000000 | tf_op jit(solution)/shard_map/chip_sums/pallas_call | solution.py:157
  332.4 12.8 %collective-permute-done.52 = bf16[128,2048]{1,0:T(8,128)(2,1)S(1)} collective-permute-done((bf16[128,2048]{1,0:T(8,128)(2,1)S(1)}, bf16[128,2048]{1,0:T(8,128)(2,1)S(1)}, u32[]{:S(2)}, u32[]{:S(2)}) %collective-permute-start.52) | collective-permute-done | bytes 524320 | tf_op jit(solution)/shard_map/ppermute | solution.py:71
  349.8 15.7 %convolution_convert_fusion = bf16[2048,1408]{1,0:T(8,128)(2,1)S(1)} fusion(bf16[2048,2048]{1,0:T(8,128)(2,1)} %copy-done.31, bf16[2048,1408]{1,0:T(8,128)(2,1)S(1)} %copy-done.6), kind=kOutput, calls=%fused_computation.1 | convolution fusion | flops 11814043648 | bytes 19922944 | tf_op jit(solution)/shard_map/dot_general | solution.py:64
  365.4 3.0 copy.69
  384.8 3.6 convolution_convert_fusion.1
  390.3 12.5 %collective-permute-done.58.refs_2_ = bf16[128,2048]{1,0:T(8,128)(2,1)S(1)} collective-permute-done((bf16[128,2048]{1,0:T(8,128)(2,1)S(1)}, bf16[128,2048]{1,0:T(8,128)(2,1)S(1)}, u32[]{:S(2)}, u32[]{:S(2)}) %collective-permute-start.58) | collective-permute-done | bytes 524320 | tf_op jit(solution)/shard_map/ppermute | solution.py:71
  405.7 5.3 chip_sums.6
  412.0 5.0 collective-permute-done.62.refs_3_
  420.2 7.0 %branch_step.2 = (bf16[2048,256]{1,0:T(8,128)(2,1)S(1)}, f32[256,2048]{1,0:T(8,128)S(1)}) custom-call(bf16[2048,256]{1,0:T(8,128)(2,1)S(1)} %get-tuple-element.258.left_ref.mixed_ref, bf16[256,2048]{1,0:T(8,128)(2,1)S(1)} %copy-done.7, bf16[128,2048]{1,0:T(8,128)(2,1)S(1)} %get-tuple-element.324.refs_0_, bf16[128,2048]{1,0:T(8,128)(2,1)S(1)} %get-tuple-element.325.refs_1_, ...), custom_call_target="tpu_custom_call" | custom-call | flops 1000000 | bytes 1000000 | tf_op jit(solution)/shard_map/branch_step/pallas_call | solution.py:781
  427.2 4.7 collective-permute-done.60.refs_0_
  434.8 2.4 branch_step.3
  450.6 36.6 %attend_back.1.left_ref = bf16[2048,768]{1,0:T(8,128)(2,1)S(1)} custom-call(s32[8]{0:T(128)S(1)} %get-tuple-element.224.inv_ref, bf16[2048,256]{1,0:T(8,128)(2,1)S(1)} %copy-done.45, bf16[2048,256]{1,0:T(8,128)(2,1)S(1)} %copy-done.47, bf16[2048,256]{1,0:T(8,128)(2,1)S(1)} %copy-done.49, bf16[2048,256]{1,0:T(8,128)(2,1)S(1)} %copy-done.51, ...), custom_call_target="tpu_custom_call" | custom-call | flops 1000000 | bytes 1000000 | tf_op jit(solution)/shard_map/attend_back/pallas_call | solution.py:575
  487.3 5.7 convolution_convert_fusion.4
  493.1 9.4 %convolution_convert_fusion.5 = bf16[2048,768]{1,0:T(8,128)(2,1)S(1)} fusion(bf16[2048,2048]{1,0:T(8,128)(2,1)} %copy-done.26, bf16[2048,768]{1,0:T(8,128)(2,1)S(1)} %attend_back.1.left_ref), kind=kOutput, calls=%fused_computation.8 | convolution fusion | flops 6444023808 | bytes 14680064 | tf_op jit(solution)/shard_map/dot_general | solution.py:64
  515.6 2.2 copy-done.39
  517.8 5.8 chip_sums.7
  530.1 3.6 collective-permute-start.88
  548.7 36.1 %collective-permute-done.87 = bf16[64,2048]{1,0:T(8,128)(2,1)S(1)} collective-permute-done((bf16[64,2048]{1,0:T(8,128)(2,1)S(1)}, bf16[64,2048]{1,0:T(8,128)(2,1)S(1)}, u32[]{:S(2)}, u32[]{:S(2)}) %collective-permute-start.87) | collective-permute-done | bytes 262176 | tf_op jit(solution)/shard_map/ppermute | solution.py:71
  587.5 2.5 multiply_reduce_fusion.2
  593.5 3.9 collective-permute-done.85.refs_7_
  597.5 3.6 all-to-all-start.3
  604.8 4.9 leave_layer.1
  617.9 3.2 collective-permute-done.90
  622.7 2.8 collective-permute-done.91
  625.5 4.2 collective-permute-done.92
  631.3 4.6 all-to-all-start.2
  639.3 2.9 multiply_subtract_fusion.3
  642.3 7.9 %multiply_subtract_fusion = (f32[64,11264]{1,0:T(8,128)}, f32[64,11264]{1,0:T(8,128)}, f32[64,11264]{1,0:T(8,128)}) fusion(f32[64,11264]{1,0:T(8,128)S(1)} %copy-done.16, bf16[64,11264]{1,0:T(8,128)(2,1)S(1)} %copy-done.37, f32[]{:T(128)S(6)} %min.3, f32[64,11264]{1,0:T(8,128)} %param.29, f32[64,11264]{1,0:T(8,128)} %param.34), kind=kLoop, calls=%fused_computation.12 | loop fusion | flops 12255232 | bytes 18743300 | tf_op jit(solution)/shard_map/sub | solution.py:59
  651.3 2.8 multiply_subtract_fusion.2
  655.4 4.4 multiply_subtract_fusion.1
  (481 shorter events, 181.8 us)
Async XLA Ops:
  7.2 68.5 %all-gather.7.cloned.1.call-start = ((), (), s32[]{:S(2)}) async-start(), calls=%async_computation.7 | async-start | bytes 1310720 | tf_op jit(solution)/shard_map/all_gather | solution.py:865
  9.1 102.2 %all-gather.11.cloned.1.call-start = ((), (), s32[]{:S(2)}) async-start(), calls=%async_computation.12 | async-start | bytes 3932160 | tf_op jit(solution)/shard_map/all_gather | solution.py:862
  33.0 15.0 %collective-permute-start.2 = (bf16[128,2048]{1,0:T(8,128)(2,1)}, bf16[128,2048]{1,0:T(8,128)(2,1)}, u32[]{:S(2)}, u32[]{:S(2)}) collective-permute-start(bf16[128,2048]{1,0:T(8,128)(2,1)} %get-tuple-element.227.refs_0_), channel_id=1, source_target_pairs={{0,8},{4,12},{8,0},{12,4},{16,24},{20,28},{24,16},{28,20},{1,9},{5... | collective-permute-start | bytes 1572872 | tf_op jit(solution)/shard_map/ppermute | solution.py:71
  33.8 14.8 %collective-permute-start.5 = (bf16[128,2048]{1,0:T(8,128)(2,1)S(1)}, bf16[128,2048]{1,0:T(8,128)(2,1)}, u32[]{:S(2)}, u32[]{:S(2)}) collective-permute-start(bf16[128,2048]{1,0:T(8,128)(2,1)S(1)} %get-tuple-element.228.refs_1_), channel_id=1, source_target_pairs={{0,16},{4,20},{8,24},{12,28},{16,0},{20,4},{24,8},{28,12},{1,17},{... | collective-permute-start | bytes 1572872 | tf_op jit(solution)/shard_map/ppermute | solution.py:71
  45.1 15.0 %collective-permute-start.3 = (bf16[128,2048]{1,0:T(8,128)(2,1)S(1)}, bf16[128,2048]{1,0:T(8,128)(2,1)}, u32[]{:S(2)}, u32[]{:S(2)}) collective-permute-start(bf16[128,2048]{1,0:T(8,128)(2,1)S(1)} %get-tuple-element.228.refs_1_), channel_id=1, source_target_pairs={{0,8},{4,12},{8,0},{12,4},{16,24},{20,28},{24,16},{28,20},{1,9},{5... | collective-permute-start | bytes 1572872 | tf_op jit(solution)/shard_map/ppermute | solution.py:71
  46.6 15.2 %collective-permute-start.4 = (bf16[128,2048]{1,0:T(8,128)(2,1)}, bf16[128,2048]{1,0:T(8,128)(2,1)}, u32[]{:S(2)}, u32[]{:S(2)}) collective-permute-start(bf16[128,2048]{1,0:T(8,128)(2,1)} %get-tuple-element.227.refs_0_), channel_id=1, source_target_pairs={{0,16},{4,20},{8,24},{12,28},{16,0},{20,4},{24,8},{28,12},{1,17},{... | collective-permute-start | bytes 1572872 | tf_op jit(solution)/shard_map/ppermute | solution.py:71
  48.1 22.6 %collective-permute-start.6 = (bf16[128,2048]{1,0:T(8,128)(2,1)}, bf16[128,2048]{1,0:T(8,128)(2,1)}, u32[]{:S(2)}, u32[]{:S(2)}) collective-permute-start(bf16[128,2048]{1,0:T(8,128)(2,1)} %collective-permute-done.2.refs_2_), channel_id=1, source_target_pairs={{0,16},{4,20},{8,24},{12,28},{16,0},{20,4},{24,8},{28,12},{1,17},{... | collective-permute-start | bytes 1572872 | tf_op jit(solution)/shard_map/ppermute | solution.py:71
  48.6 22.6 %collective-permute-start.8 = (bf16[128,2048]{1,0:T(8,128)(2,1)}, bf16[128,2048]{1,0:T(8,128)(2,1)S(1)}, u32[]{:S(2)}, u32[]{:S(2)}) collective-permute-start(bf16[128,2048]{1,0:T(8,128)(2,1)} %collective-permute-done.2.refs_2_), channel_id=1, source_target_pairs={{0,4},{4,0},{8,12},{12,8},{16,20},{20,16},{24,28},{28,24},{1,5},{5... | collective-permute-start | bytes 1572872 | tf_op jit(solution)/shard_map/ppermute | solution.py:71
  48.6 22.0 %collective-permute-start.7 = (bf16[128,2048]{1,0:T(8,128)(2,1)}, bf16[128,2048]{1,0:T(8,128)(2,1)}, u32[]{:S(2)}, u32[]{:S(2)}) collective-permute-start(bf16[128,2048]{1,0:T(8,128)(2,1)} %collective-permute-done.5.refs_5_), channel_id=1, source_target_pairs={{0,8},{4,12},{8,0},{12,4},{16,24},{20,28},{24,16},{28,20},{1,9},{5... | collective-permute-start | bytes 1572872 | tf_op jit(solution)/shard_map/ppermute | solution.py:71
  60.1 15.6 %collective-permute-start.11 = (bf16[128,2048]{1,0:T(8,128)(2,1)}, bf16[128,2048]{1,0:T(8,128)(2,1)}, u32[]{:S(2)}, u32[]{:S(2)}) collective-permute-start(bf16[128,2048]{1,0:T(8,128)(2,1)} %collective-permute-done.5.refs_5_), channel_id=1, source_target_pairs={{0,4},{4,0},{8,12},{12,8},{16,20},{20,16},{24,28},{28,24},{1,5},{5... | collective-permute-start | bytes 1572872 | tf_op jit(solution)/shard_map/ppermute | solution.py:71
  61.7 13.9 %collective-permute-start.9 = (bf16[128,2048]{1,0:T(8,128)(2,1)}, bf16[128,2048]{1,0:T(8,128)(2,1)}, u32[]{:S(2)}, u32[]{:S(2)}) collective-permute-start(bf16[128,2048]{1,0:T(8,128)(2,1)} %collective-permute-done.3.refs_3_), channel_id=1, source_target_pairs={{0,4},{4,0},{8,12},{12,8},{16,20},{20,16},{24,28},{28,24},{1,5},{5... | collective-permute-start | bytes 1572872 | tf_op jit(solution)/shard_map/ppermute | solution.py:71
  81.4 24.1 %all-to-all-start.1 = ((bf16[8,64,1408]{2,1,0:T(8,128)(2,1)}), bf16[8,64,1408]{2,1,0:T(8,128)(2,1)}, u32[]{:S(2)}, u32[]{:S(2)}) async-start(bf16[8,64,1408]{2,1,0:T(8,128)(2,1)} %copy-done.35), calls=%async_computation.1 | async-start | bytes 2883584 | tf_op jit(solution)/shard_map/all_to_all | solution.py:274
  85.8 128.6 %all-gather.13.cloned.1.call-start = ((), (), s32[]{:S(2)}) async-start(), calls=%async_computation.13 | async-start | bytes 7208960 | tf_op jit(solution)/shard_map/all_gather | solution.py:862
  105.5 177.5 %all-gather.9.cloned.1.call-start = ((), (), s32[]{:S(2)}) async-start(), calls=%async_computation.8 | async-start | bytes 3604480 | tf_op jit(solution)/shard_map/all_gather | solution.py:892
  106.4 19.4 %collective-permute-start.18 = (bf16[128,2048]{1,0:T(8,128)(2,1)S(1)}, bf16[128,2048]{1,0:T(8,128)(2,1)}, u32[]{:S(2)}, u32[]{:S(2)}) collective-permute-start(bf16[128,2048]{1,0:T(8,128)(2,1)S(1)} %get-tuple-element.267), channel_id=1, source_target_pairs={{0,8},{4,12},{8,0},{12,4},{16,24},{20,28},{24,16},{28,20},{1,9},{5... | collective-permute-start | bytes 1572872 | tf_op jit(solution)/shard_map/ppermute | solution.py:71
  106.9 18.9 %collective-permute-start.19 = (bf16[128,2048]{1,0:T(8,128)(2,1)S(1)}, bf16[128,2048]{1,0:T(8,128)(2,1)}, u32[]{:S(2)}, u32[]{:S(2)}) collective-permute-start(bf16[128,2048]{1,0:T(8,128)(2,1)S(1)} %get-tuple-element.268), channel_id=1, source_target_pairs={{0,16},{4,20},{8,24},{12,28},{16,0},{20,4},{24,8},{28,12},{1,17},{... | collective-permute-start | bytes 1572872 | tf_op jit(solution)/shard_map/ppermute | solution.py:71
  108.6 23.1 %collective-permute-start.20 = (bf16[128,2048]{1,0:T(8,128)(2,1)S(1)}, bf16[128,2048]{1,0:T(8,128)(2,1)}, u32[]{:S(2)}, u32[]{:S(2)}) collective-permute-start(bf16[128,2048]{1,0:T(8,128)(2,1)S(1)} %get-tuple-element.268), channel_id=1, source_target_pairs={{0,8},{4,12},{8,0},{12,4},{16,24},{20,28},{24,16},{28,20},{1,9},{5... | collective-permute-start | bytes 1572872 | tf_op jit(solution)/shard_map/ppermute | solution.py:71
  109.8 22.1 %collective-permute-start.21 = (bf16[128,2048]{1,0:T(8,128)(2,1)S(1)}, bf16[128,2048]{1,0:T(8,128)(2,1)}, u32[]{:S(2)}, u32[]{:S(2)}) collective-permute-start(bf16[128,2048]{1,0:T(8,128)(2,1)S(1)} %get-tuple-element.267), channel_id=1, source_target_pairs={{0,16},{4,20},{8,24},{12,28},{16,0},{20,4},{24,8},{28,12},{1,17},{... | collective-permute-start | bytes 1572872 | tf_op jit(solution)/shard_map/ppermute | solution.py:71
  131.9 30.9 %collective-permute-start.22 = (bf16[128,2048]{1,0:T(8,128)(2,1)}, bf16[128,2048]{1,0:T(8,128)(2,1)}, u32[]{:S(2)}, u32[]{:S(2)}) collective-permute-start(bf16[128,2048]{1,0:T(8,128)(2,1)} %collective-permute-done.18), channel_id=1, source_target_pairs={{0,16},{4,20},{8,24},{12,28},{16,0},{20,4},{24,8},{28,12},{1,17},{... | collective-permute-start | bytes 1572872 | tf_op jit(solution)/shard_map/ppermute | solution.py:71
  132.5 30.2 %collective-permute-start.23 = (bf16[128,2048]{1,0:T(8,128)(2,1)}, bf16[128,2048]{1,0:T(8,128)(2,1)}, u32[]{:S(2)}, u32[]{:S(2)}) collective-permute-start(bf16[128,2048]{1,0:T(8,128)(2,1)} %collective-permute-done.19), channel_id=1, source_target_pairs={{0,8},{4,12},{8,0},{12,4},{16,24},{20,28},{24,16},{28,20},{1,9},{5... | collective-permute-start | bytes 1572872 | tf_op jit(solution)/shard_map/ppermute | solution.py:71
  166.2 273.0 %reduce-scatter.4.cloned.1.call-start = ((), (), s32[]{:S(2)}) async-start(), calls=%async_computation.9 | async-start | bytes 3604480 | tf_op jit(solution)/shard_map/reduce_scatter | solution.py:908
  166.4 14.5 %collective-permute-start.29 = (bf16[128,2048]{1,0:T(8,128)(2,1)}, bf16[128,2048]{1,0:T(8,128)(2,1)S(1)}, u32[]{:S(2)}, u32[]{:S(2)}) collective-permute-start(bf16[128,2048]{1,0:T(8,128)(2,1)} %collective-permute-done.18), channel_id=1, source_target_pairs={{0,4},{4,0},{8,12},{12,8},{16,20},{20,16},{24,28},{28,24},{1,5},{5... | collective-permute-start | bytes 1572872 | tf_op jit(solution)/shard_map/ppermute | solution.py:71
  167.0 32.4 %collective-permute-start.32 = (bf16[128,2048]{1,0:T(8,128)(2,1)}, bf16[128,2048]{1,0:T(8,128)(2,1)S(1)}, u32[]{:S(2)}, u32[]{:S(2)}) collective-permute-start(bf16[128,2048]{1,0:T(8,128)(2,1)} %collective-permute-done.19), channel_id=1, source_target_pairs={{0,4},{4,0},{8,12},{12,8},{16,20},{20,16},{24,28},{28,24},{1,5},{5... | collective-permute-start | bytes 1572872 | tf_op jit(solution)/shard_map/ppermute | solution.py:71
  167.1 15.3 %collective-permute-start.30 = (bf16[128,2048]{1,0:T(8,128)(2,1)}, bf16[128,2048]{1,0:T(8,128)(2,1)S(1)}, u32[]{:S(2)}, u32[]{:S(2)}) collective-permute-start(bf16[128,2048]{1,0:T(8,128)(2,1)} %collective-permute-done.20), channel_id=1, source_target_pairs={{0,4},{4,0},{8,12},{12,8},{16,20},{20,16},{24,28},{28,24},{1,5},{5... | collective-permute-start | bytes 1572872 | tf_op jit(solution)/shard_map/ppermute | solution.py:71
  167.5 15.0 %collective-permute-start.31 = (bf16[128,2048]{1,0:T(8,128)(2,1)}, bf16[128,2048]{1,0:T(8,128)(2,1)S(1)}, u32[]{:S(2)}, u32[]{:S(2)}) collective-permute-start(bf16[128,2048]{1,0:T(8,128)(2,1)} %collective-permute-done.21), channel_id=1, source_target_pairs={{0,4},{4,0},{8,12},{12,8},{16,20},{20,16},{24,28},{28,24},{1,5},{5... | collective-permute-start | bytes 1572872 | tf_op jit(solution)/shard_map/ppermute | solution.py:71
  180.4 14.0 %collective-permute-start.25 = (bf16[128,2048]{1,0:T(8,128)(2,1)S(1)}, bf16[128,2048]{1,0:T(8,128)(2,1)S(1)}, u32[]{:S(2)}, u32[]{:S(2)}) collective-permute-start(bf16[128,2048]{1,0:T(8,128)(2,1)S(1)} %get-tuple-element.261), channel_id=1, source_target_pairs={{0,8},{4,12},{8,0},{12,4},{16,24},{20,28},{24,16},{28,20},{1,9},{5... | collective-permute-start | bytes 1572872 | tf_op jit(solution)/shard_map/ppermute | solution.py:71
  182.4 17.6 %collective-permute-start.33 = (bf16[128,2048]{1,0:T(8,128)(2,1)}, bf16[128,2048]{1,0:T(8,128)(2,1)S(1)}, u32[]{:S(2)}, u32[]{:S(2)}) collective-permute-start(bf16[128,2048]{1,0:T(8,128)(2,1)} %collective-permute-done.22), channel_id=1, source_target_pairs={{0,4},{4,0},{8,12},{12,8},{16,20},{20,16},{24,28},{28,24},{1,5},{5... | collective-permute-start | bytes 1572872 | tf_op jit(solution)/shard_map/ppermute | solution.py:71
  182.6 18.1 %collective-permute-start.34 = (bf16[128,2048]{1,0:T(8,128)(2,1)}, bf16[128,2048]{1,0:T(8,128)(2,1)S(1)}, u32[]{:S(2)}, u32[]{:S(2)}) collective-permute-start(bf16[128,2048]{1,0:T(8,128)(2,1)} %collective-permute-done.23), channel_id=1, source_target_pairs={{0,4},{4,0},{8,12},{12,8},{16,20},{20,16},{24,28},{28,24},{1,5},{5... | collective-permute-start | bytes 1572872 | tf_op jit(solution)/shard_map/ppermute | solution.py:71
  194.7 23.0 %collective-permute-start.27 = (bf16[128,2048]{1,0:T(8,128)(2,1)}, bf16[128,2048]{1,0:T(8,128)(2,1)}, u32[]{:S(2)}, u32[]{:S(2)}) collective-permute-start(bf16[128,2048]{1,0:T(8,128)(2,1)} %get-tuple-element.265), channel_id=1, source_target_pairs={{0,8},{4,12},{8,0},{12,4},{16,24},{20,28},{24,16},{28,20},{1,9},{5... | collective-permute-start | bytes 1572872 | tf_op jit(solution)/shard_map/ppermute | solution.py:71
  196.1 21.6 %collective-permute-start.28 = (bf16[128,2048]{1,0:T(8,128)(2,1)}, bf16[128,2048]{1,0:T(8,128)(2,1)}, u32[]{:S(2)}, u32[]{:S(2)}) collective-permute-start(bf16[128,2048]{1,0:T(8,128)(2,1)} %get-tuple-element.266), channel_id=1, source_target_pairs={{0,16},{4,20},{8,24},{12,28},{16,0},{20,4},{24,8},{28,12},{1,17},{... | collective-permute-start | bytes 1572872 | tf_op jit(solution)/shard_map/ppermute | solution.py:71
  199.5 20.9 %collective-permute-start.35 = (bf16[128,2048]{1,0:T(8,128)(2,1)}, bf16[128,2048]{1,0:T(8,128)(2,1)}, u32[]{:S(2)}, u32[]{:S(2)}) collective-permute-start(bf16[128,2048]{1,0:T(8,128)(2,1)} %add_convert_fusion.7), channel_id=1, source_target_pairs={{0,16},{4,20},{8,24},{12,28},{16,0},{20,4},{24,8},{28,12},{1,17},{... | collective-permute-start | bytes 1572872 | tf_op jit(solution)/shard_map/ppermute | solution.py:71
  200.0 20.3 %collective-permute-start.36 = (bf16[128,2048]{1,0:T(8,128)(2,1)}, bf16[128,2048]{1,0:T(8,128)(2,1)}, u32[]{:S(2)}, u32[]{:S(2)}) collective-permute-start(bf16[128,2048]{1,0:T(8,128)(2,1)} %add_convert_fusion.6), channel_id=1, source_target_pairs={{0,8},{4,12},{8,0},{12,4},{16,24},{20,28},{24,16},{28,20},{1,9},{5... | collective-permute-start | bytes 1572872 | tf_op jit(solution)/shard_map/ppermute | solution.py:71
  225.2 14.8 %collective-permute-start.37 = (bf16[128,2048]{1,0:T(8,128)(2,1)S(1)}, bf16[128,2048]{1,0:T(8,128)(2,1)S(1)}, u32[]{:S(2)}, u32[]{:S(2)}) collective-permute-start(bf16[128,2048]{1,0:T(8,128)(2,1)S(1)} %get-tuple-element.286.refs_0_), channel_id=1, source_target_pairs={{0,8},{4,12},{8,0},{12,4},{16,24},{20,28},{24,16},{28,20},{1,9},{5... | collective-permute-start | bytes 1572872 | tf_op jit(solution)/shard_map/ppermute | solution.py:71
  225.8 14.8 %collective-permute-start.39 = (bf16[128,2048]{1,0:T(8,128)(2,1)S(1)}, bf16[128,2048]{1,0:T(8,128)(2,1)S(1)}, u32[]{:S(2)}, u32[]{:S(2)}) collective-permute-start(bf16[128,2048]{1,0:T(8,128)(2,1)S(1)} %get-tuple-element.287.refs_1_), channel_id=1, source_target_pairs={{0,16},{4,20},{8,24},{12,28},{16,0},{20,4},{24,8},{28,12},{1,17},{... | collective-permute-start | bytes 1572872 | tf_op jit(solution)/shard_map/ppermute | solution.py:71
  227.4 22.9 %collective-permute-start.43 = (bf16[128,2048]{1,0:T(8,128)(2,1)S(1)}, bf16[128,2048]{1,0:T(8,128)(2,1)S(1)}, u32[]{:S(2)}, u32[]{:S(2)}) collective-permute-start(bf16[128,2048]{1,0:T(8,128)(2,1)S(1)} %get-tuple-element.287.refs_1_), channel_id=1, source_target_pairs={{0,8},{4,12},{8,0},{12,4},{16,24},{20,28},{24,16},{28,20},{1,9},{5... | collective-permute-start | bytes 1572872 | tf_op jit(solution)/shard_map/ppermute | solution.py:71
  228.7 21.9 %collective-permute-start.44 = (bf16[128,2048]{1,0:T(8,128)(2,1)S(1)}, bf16[128,2048]{1,0:T(8,128)(2,1)S(1)}, u32[]{:S(2)}, u32[]{:S(2)}) collective-permute-start(bf16[128,2048]{1,0:T(8,128)(2,1)S(1)} %get-tuple-element.286.refs_0_), channel_id=1, source_target_pairs={{0,16},{4,20},{8,24},{12,28},{16,0},{20,4},{24,8},{28,12},{1,17},{... | collective-permute-start | bytes 1572872 | tf_op jit(solution)/shard_map/ppermute | solution.py:71
  250.8 16.1 %collective-permute-start.38 = (bf16[128,2048]{1,0:T(8,128)(2,1)S(1)}, bf16[128,2048]{1,0:T(8,128)(2,1)S(1)}, u32[]{:S(2)}, u32[]{:S(2)}) collective-permute-start(bf16[128,2048]{1,0:T(8,128)(2,1)S(1)} %collective-permute-done.37.refs_2_), channel_id=1, source_target_pairs={{0,16},{4,20},{8,24},{12,28},{16,0},{20,4},{24,8},{28,12},{1,17},{... | collective-permute-start | bytes 1572872 | tf_op jit(solution)/shard_map/ppermute | solution.py:71
  252.2 14.7 %collective-permute-start.40 = (bf16[128,2048]{1,0:T(8,128)(2,1)S(1)}, bf16[128,2048]{1,0:T(8,128)(2,1)S(1)}, u32[]{:S(2)}, u32[]{:S(2)}) collective-permute-start(bf16[128,2048]{1,0:T(8,128)(2,1)S(1)} %collective-permute-done.39.refs_5_), channel_id=1, source_target_pairs={{0,8},{4,12},{8,0},{12,4},{16,24},{20,28},{24,16},{28,20},{1,9},{5... | collective-permute-start | bytes 1572872 | tf_op jit(solution)/shard_map/ppermute | solution.py:71
  316.2 171.1 %reduce-scatter.6.cloned.1.call-start = ((), (), s32[]{:S(2)}) async-start(), calls=%async_computation.10 | async-start | bytes 7208960 | tf_op jit(solution)/shard_map/reduce_scatter | solution.py:908
  330.9 14.2 %collective-permute-start.52 = (bf16[128,2048]{1,0:T(8,128)(2,1)S(1)}, bf16[128,2048]{1,0:T(8,128)(2,1)S(1)}, u32[]{:S(2)}, u32[]{:S(2)}) collective-permute-start(bf16[128,2048]{1,0:T(8,128)(2,1)S(1)} %get-tuple-element.304), channel_id=1, source_target_pairs={{0,8},{4,12},{8,0},{12,4},{16,24},{20,28},{24,16},{28,20},{1,9},{5... | collective-permute-start | bytes 1572872 | tf_op jit(solution)/shard_map/ppermute | solution.py:71
  331.3 14.0 %collective-permute-start.53 = (bf16[128,2048]{1,0:T(8,128)(2,1)S(1)}, bf16[128,2048]{1,0:T(8,128)(2,1)S(1)}, u32[]{:S(2)}, u32[]{:S(2)}) collective-permute-start(bf16[128,2048]{1,0:T(8,128)(2,1)S(1)} %get-tuple-element.305), channel_id=1, source_target_pairs={{0,16},{4,20},{8,24},{12,28},{16,0},{20,4},{24,8},{28,12},{1,17},{... | collective-permute-start | bytes 1572872 | tf_op jit(solution)/shard_map/ppermute | solution.py:71
  345.3 23.1 %collective-permute-start.54 = (bf16[128,2048]{1,0:T(8,128)(2,1)S(1)}, bf16[128,2048]{1,0:T(8,128)(2,1)S(1)}, u32[]{:S(2)}, u32[]{:S(2)}) collective-permute-start(bf16[128,2048]{1,0:T(8,128)(2,1)S(1)} %get-tuple-element.308), channel_id=1, source_target_pairs={{0,8},{4,12},{8,0},{12,4},{16,24},{20,28},{24,16},{28,20},{1,9},{5... | collective-permute-start | bytes 1572872 | tf_op jit(solution)/shard_map/ppermute | solution.py:71
  347.1 22.2 %collective-permute-start.55 = (bf16[128,2048]{1,0:T(8,128)(2,1)S(1)}, bf16[128,2048]{1,0:T(8,128)(2,1)S(1)}, u32[]{:S(2)}, u32[]{:S(2)}) collective-permute-start(bf16[128,2048]{1,0:T(8,128)(2,1)S(1)} %add_convert_fusion.5), channel_id=1, source_target_pairs={{0,16},{4,20},{8,24},{12,28},{16,0},{20,4},{24,8},{28,12},{1,17},{... | collective-permute-start | bytes 1572872 | tf_op jit(solution)/shard_map/ppermute | solution.py:71
  347.7 22.3 %collective-permute-start.56 = (bf16[128,2048]{1,0:T(8,128)(2,1)S(1)}, bf16[128,2048]{1,0:T(8,128)(2,1)S(1)}, u32[]{:S(2)}, u32[]{:S(2)}) collective-permute-start(bf16[128,2048]{1,0:T(8,128)(2,1)S(1)} %add_convert_fusion.4), channel_id=1, source_target_pairs={{0,8},{4,12},{8,0},{12,4},{16,24},{20,28},{24,16},{28,20},{1,9},{5... | collective-permute-start | bytes 1572872 | tf_op jit(solution)/shard_map/ppermute | solution.py:71
  348.7 22.5 %collective-permute-start.57 = (bf16[128,2048]{1,0:T(8,128)(2,1)S(1)}, bf16[128,2048]{1,0:T(8,128)(2,1)S(1)}, u32[]{:S(2)}, u32[]{:S(2)}) collective-permute-start(bf16[128,2048]{1,0:T(8,128)(2,1)S(1)} %get-tuple-element.313), channel_id=1, source_target_pairs={{0,16},{4,20},{8,24},{12,28},{16,0},{20,4},{24,8},{28,12},{1,17},{... | collective-permute-start | bytes 1572872 | tf_op jit(solution)/shard_map/ppermute | solution.py:71
  372.1 238.8 %reduce-scatter.8.cloned.1.call-start = ((), (), s32[]{:S(2)}) async-start(), calls=%async_computation.11 | async-start | bytes 3932160 | tf_op jit(solution)/shard_map/reduce_scatter | solution.py:908
  388.5 17.2 %collective-permute-start.65 = (bf16[1024,2048]{1,0:T(8,128)(2,1)S(1)}, bf16[1024,2048]{1,0:T(8,128)(2,1)S(1)}, u32[]{:S(2)}, u32[]{:S(2)}) collective-permute-start(bf16[1024,2048]{1,0:T(8,128)(2,1)S(1)} %convolution_convert_fusion.1), channel_id=1, source_target_pairs={{0,4},{4,0},{8,12},{12,8},{16,20},{20,16},{24,28},{28,24},{1,5},{5... | collective-permute-start | bytes 12582920 | tf_op jit(solution)/shard_map/ppermute | solution.py:71
  388.7 14.2 %collective-permute-start.58 = (bf16[128,2048]{1,0:T(8,128)(2,1)S(1)}, bf16[128,2048]{1,0:T(8,128)(2,1)S(1)}, u32[]{:S(2)}, u32[]{:S(2)}) collective-permute-start(bf16[128,2048]{1,0:T(8,128)(2,1)S(1)} %get-tuple-element.324.refs_0_), channel_id=1, source_target_pairs={{0,8},{4,12},{8,0},{12,4},{16,24},{20,28},{24,16},{28,20},{1,9},{5... | collective-permute-start | bytes 1572872 | tf_op jit(solution)/shard_map/ppermute | solution.py:71
  405.7 14.0 %collective-permute-start.70 = (bf16[128,2048]{1,0:T(8,128)(2,1)S(1)}, bf16[128,2048]{1,0:T(8,128)(2,1)S(1)}, u32[]{:S(2)}, u32[]{:S(2)}) collective-permute-start(bf16[128,2048]{1,0:T(8,128)(2,1)S(1)} %collective-permute-done.59.refs_5_), channel_id=1, source_target_pairs={{0,4},{4,0},{8,12},{12,8},{16,20},{20,16},{24,28},{28,24},{1,5},{5... | collective-permute-start | bytes 1572872 | tf_op jit(solution)/shard_map/ppermute | solution.py:71
  439.2 48.0 %collective-permute-start.73 = (bf16[128,2048]{1,0:T(8,128)(2,1)}, bf16[128,2048]{1,0:T(8,128)(2,1)}, u32[]{:S(2)}, u32[]{:S(2)}) collective-permute-start(bf16[128,2048]{1,0:T(8,128)(2,1)} %get-tuple-element.357), channel_id=1, source_target_pairs={{0,8},{4,12},{8,0},{12,4},{16,24},{20,28},{24,16},{28,20},{1,9},{5... | collective-permute-start | bytes 1572872 | tf_op jit(solution)/shard_map/ppermute | solution.py:71
  440.3 46.9 %collective-permute-start.74 = (bf16[128,2048]{1,0:T(8,128)(2,1)}, bf16[128,2048]{1,0:T(8,128)(2,1)}, u32[]{:S(2)}, u32[]{:S(2)}) collective-permute-start(bf16[128,2048]{1,0:T(8,128)(2,1)} %get-tuple-element.358), channel_id=1, source_target_pairs={{0,16},{4,20},{8,24},{12,28},{16,0},{20,4},{24,8},{28,12},{1,17},{... | collective-permute-start | bytes 1572872 | tf_op jit(solution)/shard_map/ppermute | solution.py:71
  441.9 45.3 %collective-permute-start.75 = (bf16[128,2048]{1,0:T(8,128)(2,1)}, bf16[128,2048]{1,0:T(8,128)(2,1)}, u32[]{:S(2)}, u32[]{:S(2)}) collective-permute-start(bf16[128,2048]{1,0:T(8,128)(2,1)} %get-tuple-element.359), channel_id=1, source_target_pairs={{0,8},{4,12},{8,0},{12,4},{16,24},{20,28},{24,16},{28,20},{1,9},{5... | collective-permute-start | bytes 1572872 | tf_op jit(solution)/shard_map/ppermute | solution.py:71
  442.7 44.5 %collective-permute-start.76 = (bf16[128,2048]{1,0:T(8,128)(2,1)}, bf16[128,2048]{1,0:T(8,128)(2,1)}, u32[]{:S(2)}, u32[]{:S(2)}) collective-permute-start(bf16[128,2048]{1,0:T(8,128)(2,1)} %get-tuple-element.360), channel_id=1, source_target_pairs={{0,16},{4,20},{8,24},{12,28},{16,0},{20,4},{24,8},{28,12},{1,17},{... | collective-permute-start | bytes 1572872 | tf_op jit(solution)/shard_map/ppermute | solution.py:71
  508.7 17.5 %collective-permute-start.78 = (bf16[128,2048]{1,0:T(8,128)(2,1)}, bf16[128,2048]{1,0:T(8,128)(2,1)}, u32[]{:S(2)}, u32[]{:S(2)}) collective-permute-start(bf16[128,2048]{1,0:T(8,128)(2,1)} %add_convert_fusion.3), channel_id=1, source_target_pairs={{0,16},{4,20},{8,24},{12,28},{16,0},{20,4},{24,8},{28,12},{1,17},{... | collective-permute-start | bytes 1572872 | tf_op jit(solution)/shard_map/ppermute | solution.py:71
  512.3 14.4 %collective-permute-start.79 = (bf16[128,2048]{1,0:T(8,128)(2,1)}, bf16[128,2048]{1,0:T(8,128)(2,1)}, u32[]{:S(2)}, u32[]{:S(2)}) collective-permute-start(bf16[128,2048]{1,0:T(8,128)(2,1)} %add_convert_fusion.2), channel_id=1, source_target_pairs={{0,8},{4,12},{8,0},{12,4},{16,24},{20,28},{24,16},{28,20},{1,9},{5... | collective-permute-start | bytes 1572872 | tf_op jit(solution)/shard_map/ppermute | solution.py:71
  526.6 14.3 %collective-permute-start.80 = (bf16[128,2048]{1,0:T(8,128)(2,1)}, bf16[128,2048]{1,0:T(8,128)(2,1)}, u32[]{:S(2)}, u32[]{:S(2)}) collective-permute-start(bf16[128,2048]{1,0:T(8,128)(2,1)} %get-tuple-element.382), channel_id=1, source_target_pairs={{0,8},{4,12},{8,0},{12,4},{16,24},{20,28},{24,16},{28,20},{1,9},{5... | collective-permute-start | bytes 1572872 | tf_op jit(solution)/shard_map/ppermute | solution.py:71
  530.1 17.3 %collective-permute-start.88 = (bf16[64,2048]{1,0:T(8,128)(2,1)S(1)}, bf16[64,2048]{1,0:T(8,128)(2,1)S(1)}, u32[]{:S(2)}, u32[]{:S(2)}) collective-permute-start(bf16[64,2048]{1,0:T(8,128)(2,1)S(1)} %get-tuple-element.438), channel_id=1, source_target_pairs={{0,3},{1,2},{2,1},{3,0},{4,7},{5,6},{6,5},{7,4},{8,11},{9,10},{10,... | collective-permute-start | bytes 786440 | tf_op jit(solution)/shard_map/ppermute | solution.py:71
  533.8 51.0 %collective-permute-start.87 = (bf16[64,2048]{1,0:T(8,128)(2,1)S(1)}, bf16[64,2048]{1,0:T(8,128)(2,1)S(1)}, u32[]{:S(2)}, u32[]{:S(2)}) collective-permute-start(bf16[64,2048]{1,0:T(8,128)(2,1)S(1)} %get-tuple-element.439), channel_id=1, source_target_pairs={{0,2},{1,3},{2,0},{3,1},{4,6},{5,7},{6,4},{7,5},{8,10},{9,11},{10,... | collective-permute-start | bytes 786440 | tf_op jit(solution)/shard_map/ppermute | solution.py:71
  533.8 53.7 %collective-permute-start.86 = (bf16[64,2048]{1,0:T(8,128)(2,1)S(1)}, bf16[64,2048]{1,0:T(8,128)(2,1)S(1)}, u32[]{:S(2)}, u32[]{:S(2)}) collective-permute-start(bf16[64,2048]{1,0:T(8,128)(2,1)S(1)} %get-tuple-element.437), channel_id=1, source_target_pairs={{0,1},{1,0},{2,3},{3,2},{4,5},{5,4},{6,7},{7,6},{8,9},{9,8},{10,11... | collective-permute-start | bytes 786440 | tf_op jit(solution)/shard_map/ppermute | solution.py:71
  541.1 50.8 %collective-permute-start.82 = (bf16[128,2048]{1,0:T(8,128)(2,1)}, bf16[128,2048]{1,0:T(8,128)(2,1)S(1)}, u32[]{:S(2)}, u32[]{:S(2)}) collective-permute-start(bf16[128,2048]{1,0:T(8,128)(2,1)} %get-tuple-element.386), channel_id=1, source_target_pairs={{0,8},{4,12},{8,0},{12,4},{16,24},{20,28},{24,16},{28,20},{1,9},{5... | collective-permute-start | bytes 1572872 | tf_op jit(solution)/shard_map/ppermute | solution.py:71
  544.1 48.6 %collective-permute-start.83 = (bf16[128,2048]{1,0:T(8,128)(2,1)}, bf16[128,2048]{1,0:T(8,128)(2,1)S(1)}, u32[]{:S(2)}, u32[]{:S(2)}) collective-permute-start(bf16[128,2048]{1,0:T(8,128)(2,1)} %add_convert_fusion.1), channel_id=1, source_target_pairs={{0,16},{4,20},{8,24},{12,28},{16,0},{20,4},{24,8},{28,12},{1,17},{... | collective-permute-start | bytes 1572872 | tf_op jit(solution)/shard_map/ppermute | solution.py:71
  547.4 46.1 %collective-permute-start.84 = (bf16[128,2048]{1,0:T(8,128)(2,1)}, bf16[128,2048]{1,0:T(8,128)(2,1)}, u32[]{:S(2)}, u32[]{:S(2)}) collective-permute-start(bf16[128,2048]{1,0:T(8,128)(2,1)} %add_convert_fusion), channel_id=1, source_target_pairs={{0,8},{4,12},{8,0},{12,4},{16,24},{20,28},{24,16},{28,20},{1,9},{5... | collective-permute-start | bytes 1572872 | tf_op jit(solution)/shard_map/ppermute | solution.py:71
  597.5 32.4 %all-to-all-start.3 = ((bf16[8,64,1408]{2,1,0:T(8,128)(2,1)}), bf16[8,64,1408]{2,1,0:T(8,128)(2,1)S(1)}, u32[]{:S(2)}, u32[]{:S(2)}) async-start(bf16[8,64,1408]{2,1,0:T(8,128)(2,1)} %bitcast.68), calls=%async_computation.6 | async-start | bytes 2883584 | tf_op jit(solution)/shard_map/all_to_all | solution.py:274
  631.3 22.9 %all-to-all-start.2 = ((bf16[8,64,768]{2,1,0:T(8,128)(2,1)}), bf16[8,64,768]{2,1,0:T(8,128)(2,1)}, u32[]{:S(2)}, u32[]{:S(2)}) async-start(bf16[8,64,768]{2,1,0:T(8,128)(2,1)} %bitcast.75), calls=%async_computation.5 | async-start | bytes 1572864 | tf_op jit(solution)/shard_map/all_to_all | solution.py:274
  (145 other events, 1048.1 us)
Sparse Core Ops, SparseCore 0:
  10.2 31.2 all-gather.6
  43.6 63.7 all-gather.10
  109.0 105.3 all-gather.12
  216.4 57.4 all-gather.8
  316.3 56.1 reduce-scatter.3
  374.7 102.1 reduce-scatter.5
  506.6 78.1 reduce-scatter.7
